TPU v7x, 256 devices: a whole 4x4x8 slice. The times are simulated.
256 devices in a mesh: dp: 16 (over x_hi, y, core), proto: 16 (over x_lo, z).
Axes of the slice: x: 4 (x_hi: 2, x_lo: 2; x = x_hi * 2 + x_lo), y: 4, z: 8, core: 2. Of those that a mesh axis runs over, the one named last changes fastest.
Arguments:
- student_cls: bfloat16 [8192, 1536], P('dp', 'proto'), may hold values from -56 to 56
- teacher_cls: bfloat16 [8192, 1536], P('dp', 'proto'), may hold values from -56 to 56
- student_gain: float32 [1536], replicated, may hold values from 0.1 to 1.9
- teacher_gain: float32 [1536], replicated, may hold values from 0.1 to 1.9
- student_proj: bfloat16 [1536, 384], P('proto'), may hold values from -1 to 1
- teacher_proj: float32 [1536, 384], P('proto'), may hold values from -1 to 1
- prototypes: bfloat16 [65536, 384], P('proto'), may hold values from -1 to 1
- partner: int32 [8192], P('dp'), may hold values from 0 to 8191, as said below
Outputs:
- crop_loss: float32 [8192], P('dp')
- grad_proj: float32 [1536, 384], P('proto')
- grad_protos: float32 [65536, 384], P(('proto', 'dp'))
- teacher_next: float32 [1536, 384], P('proto')
Inputs may be any that keep to these rules, and one draw needn't show every extreme that they name: partner pairs the crops: partner[partner[i]] = i and partner[i] != i; crop i's partner lies among the 512 crops of the dp index half the dp axis away from i's.
All inputs are finite; a program needn't handle non-finite values.
Results may differ from a plain program's by a relative error of at most 0.02.
Values may be sent and summed in bfloat16 or wider, within the bound.
No kernel may reach another device: no remote copies, remote signals or barrier semaphores. Data moves between devices by JAX's collectives and lax.ppermute only.
A program may use at most 128 MiB of HBM per device.

v0:
```python
import jax
import jax.numpy as jnp
from jax import lax
from jax.sharding import PartitionSpec as P

D = 1536
ITERS = 3


EPSILON = 1e-06
TEACHER_TEMP = 0.07
STUDENT_TEMP = 0.1
MOMENTUM = 0.994


def passed_along(value, axis, steps):
    count = lax.axis_size(axis)
    pairs = [(source, (source + steps) % count) for source in range(count)]
    return lax.ppermute(value, axis, pairs)


def finish_norm(values, center, spread, gain):
    normed = (values - center[:, None]) * lax.rsqrt(spread[:, None] + EPSILON) * gain[None, :]
    return normed.astype(jnp.bfloat16)


def unit_rows(values):
    factor = lax.rsqrt(jnp.sum(values * values, axis=1, keepdims=True) + EPSILON)
    return (values * factor, factor)


def contract_last(left, right):
    return lax.dot_general(
        left, right, (((1,), (1,)), ((), ())), preferred_element_type=jnp.float32
    )


def contract_first(left, right):
    return lax.dot_general(
        left, right, (((0,), (0,)), ((), ())), preferred_element_type=jnp.float32
    )


def prototype_inverse(local_sums):
    return 1.0 / lax.psum(local_sums, "dp")


def crop_inverse(local_sums):
    return 1.0 / lax.psum(local_sums, "proto")


def body(
    student_cls,
    teacher_cls,
    student_gain,
    teacher_gain,
    student_proj,
    teacher_proj,
    prototypes,
    partner,
):
    local_width = student_cls.shape[1]
    offset = lax.axis_index("proto") * local_width
    student_full, teacher_full = (
        lax.all_gather(student_cls, "proto", axis=1, tiled=True),
        lax.all_gather(teacher_cls, "proto", axis=1, tiled=True),
    )
    student_weight, teacher_weight = (
        lax.all_gather(student_proj, "proto", axis=0, tiled=True),
        lax.all_gather(teacher_proj.astype(jnp.bfloat16), "proto", axis=0, tiled=True),
    )
    student_values = student_full.astype(jnp.float32)
    teacher_values = teacher_full.astype(jnp.float32)
    student_center = jnp.sum(student_values, axis=1) / D
    student_spread = (
        jnp.sum(student_values * student_values, axis=1) / D - student_center * student_center
    )
    teacher_center = jnp.sum(teacher_values, axis=1) / D
    teacher_spread = (
        jnp.sum(teacher_values * teacher_values, axis=1) / D - teacher_center * teacher_center
    )
    student_normed = finish_norm(student_values, student_center, student_spread, student_gain)
    teacher_normed = finish_norm(teacher_values, teacher_center, teacher_spread, teacher_gain)
    student_hidden = jnp.dot(student_normed, student_weight, preferred_element_type=jnp.float32)
    teacher_hidden = jnp.dot(teacher_normed, teacher_weight, preferred_element_type=jnp.float32)
    student_own = lax.dynamic_slice_in_dim(student_normed, offset, local_width, 1)
    student_unit32, student_factor = unit_rows(student_hidden)
    student_unit = student_unit32.astype(jnp.bfloat16)
    teacher_unit32, teacher_factor = unit_rows(teacher_hidden)
    teacher_unit = teacher_unit32.astype(jnp.bfloat16)
    opposite = passed_along(teacher_unit, "dp", lax.axis_size("dp") // 2)
    paired = jnp.take(opposite, partner % opposite.shape[0], axis=0)
    proto_unit32, proto_factor = unit_rows(prototypes.astype(jnp.float32))
    proto_unit = proto_unit32.astype(jnp.bfloat16)
    energy = jnp.exp(contract_last(paired, proto_unit) / TEACHER_TEMP)
    codes = energy
    for step in range(ITERS):
        codes = codes * prototype_inverse(jnp.sum(codes, axis=0))[None, :]
        codes = codes * crop_inverse(jnp.sum(codes, axis=1))[:, None]
    logits = contract_last(student_unit, proto_unit) / STUDENT_TEMP
    exponent = jnp.exp(logits)
    partition, expected = lax.psum(
        (jnp.sum(exponent, axis=1), jnp.sum(codes * logits, axis=1)), "proto"
    )
    crop_loss = jnp.log(partition) - expected
    score_grad = ((exponent / partition[:, None] - codes) / STUDENT_TEMP).astype(jnp.bfloat16)
    unit_grad = lax.psum(
        jnp.dot(score_grad, proto_unit, preferred_element_type=jnp.float32).astype(jnp.bfloat16),
        "proto",
    ).astype(jnp.float32)
    share = prototypes.shape[0] // lax.axis_size("dp")
    proto_unit_grad = lax.psum_scatter(
        contract_first(score_grad, student_unit).astype(jnp.bfloat16),
        "dp",
        scatter_dimension=0,
        tiled=True,
    ).astype(jnp.float32)
    own_start = lax.axis_index("dp") * share
    own_unit = lax.dynamic_slice_in_dim(proto_unit32, own_start, share, 0)
    own_factor = lax.dynamic_slice_in_dim(proto_factor, own_start, share, 0)
    grad_protos = own_factor * (
        proto_unit_grad - own_unit * jnp.sum(own_unit * proto_unit_grad, axis=1, keepdims=True)
    )
    hidden_grad = (
        student_factor
        * (unit_grad - student_unit32 * jnp.sum(student_unit32 * unit_grad, axis=1, keepdims=True))
    ).astype(jnp.bfloat16)
    grad_proj = lax.psum(
        contract_first(student_own, hidden_grad).astype(jnp.bfloat16), "dp"
    ).astype(jnp.float32)
    teacher_next = MOMENTUM * teacher_proj + (1.0 - MOMENTUM) * student_proj.astype(jnp.float32)
    return (crop_loss, grad_proj, grad_protos, teacher_next)


def solution(mesh):
    placed = (
        P("dp", "proto"),
        P("dp", "proto"),
        P(),
        P(),
        P("proto", None),
        P("proto", None),
        P("proto", None),
        P("dp"),
    )
    return jax.shard_map(
        body,
        mesh=mesh,
        in_specs=placed,
        out_specs=(P("dp"), P("proto", None), P(("proto", "dp"), None), P("proto", None)),
        check_vma=False,
    )
```

profile of v0, /device:TPU:1, one launch (start us, length us, event | category | flops | bytes accessed | tf_op | source)
XLA Modules:
  0.0 1035.3 jit_solution(12929146348667235754)
XLA Ops:
  7.2 0.0 all-gather.9.cloned.1.call-start
  7.2 0.7 all-gather.9.cloned.1.call-update
  7.9 0.0 all-gather.11.cloned.1.call-start
  7.9 1.7 multiply_add_fusion
  9.7 0.0 all-gather.11.cloned.1.call-update
  9.7 0.0 all-gather.5.cloned.1.call-start
  9.8 0.7 all-gather.5.cloned.1.call-update
  10.4 0.0 all-gather.7.cloned.1.call-start
  10.5 0.5 all-gather.7.cloned.1.call-update
  11.0 0.0 all-reduce.4.cloned.1.call-start
  11.1 2.6 fusion.3
  13.7 1.2 compare_and_fusion
  14.8 0.6 pad_clamp_fusion
  15.4 59.0 %all-gather.9.cloned.1.call-done = bf16[512,1536]{0,1:T(8,128)(2,1)} async-done(((bf16[512,96]{0,1:T(8,128)(2,1)}), bf16[512,1536]{0,1:T(8,128)(2,1)}) %all-gather.9.cloned.1.call-update) | async-done | bytes 1572880 | tf_op jit(solution)/shard_map/all_gather | solution.py:66
  74.4 1.9 convert_reduce_fusion
  76.3 66.6 %all-gather.11.cloned.1.call-done = bf16[1536,384]{1,0:T(8,128)(2,1)} async-done(((bf16[96,384]{1,0:T(8,128)(2,1)}), bf16[1536,384]{1,0:T(8,128)(2,1)}) %all-gather.11.cloned.1.call-update) | async-done | bytes 1179664 | tf_op jit(solution)/shard_map/all_gather | solution.py:70
  142.9 2.8 multiply_reduce_fusion.3
  145.7 0.0 copy-start
  145.7 0.1 multiply_convert_fusion.1
  145.8 2.5 collective-permute-start
  148.3 65.2 %all-gather.5.cloned.1.call-done = bf16[512,1536]{0,1:T(8,128)(2,1)} async-done(((bf16[512,96]{0,1:T(8,128)(2,1)}), bf16[512,1536]{0,1:T(8,128)(2,1)}) %all-gather.5.cloned.1.call-update) | async-done | bytes 1572880 | tf_op jit(solution)/shard_map/all_gather | solution.py:65
  213.5 1.9 convert_reduce_fusion.1
  215.4 3.0 fusion.7
  218.5 62.8 %all-gather.7.cloned.1.call-done = bf16[1536,384]{1,0:T(8,128)(2,1)} async-done(((bf16[96,384]{1,0:T(8,128)(2,1)}), bf16[1536,384]{1,0:T(8,128)(2,1)}) %all-gather.7.cloned.1.call-update) | async-done | bytes 1179664 | tf_op jit(solution)/shard_map/all_gather | solution.py:69
  281.3 3.4 multiply_reduce_fusion.4
  284.7 0.6 add_rsqrt_fusion.3
  285.3 0.0 collective-permute-done
  285.3 1.2 copy.12
  286.5 2.7 gather_fusion
  289.2 0.0 copy-done
  289.2 5.9 fusion.1
  295.1 70.1 %psum.71 = f32[4096]{0:T(1024)S(1)} all-reduce(f32[4096]{0:T(1024)S(1)} %get-tuple-element.24), channel_id=1, replica_groups=mesh['dp'=16,'proto'=16] {'dp'}, use_global_device_ids=true, to_apply=%region_10.11 | all-reduce | flops 4096 | bytes 32768 | tf_op jit(solution)/shard_map/psum | solution.py:45
  365.2 4.8 fusion.38
  370.0 26.0 %psum.72 = f32[512]{0:T(512)S(1)} all-reduce(f32[512]{0:T(512)S(1)} %fusion.38), channel_id=1, replica_groups=mesh['dp'=16,'proto'=16] {'proto'}, use_global_device_ids=true, to_apply=%region_12.13 | all-reduce | flops 512 | bytes 4096 | tf_op jit(solution)/shard_map/psum | solution.py:49
  396.1 4.4 multiply_reduce_fusion.2
  400.5 72.2 %psum.73 = f32[4096]{0:T(1024)S(1)} all-reduce(f32[4096]{0:T(1024)S(1)} %multiply_reduce_fusion.2), channel_id=1, replica_groups=mesh['dp'=16,'proto'=16] {'dp'}, use_global_device_ids=true, to_apply=%region_14.15 | all-reduce | flops 4096 | bytes 32768 | tf_op jit(solution)/shard_map/psum | solution.py:45
  472.6 4.6 fusion.2
  477.3 24.0 %psum.74 = f32[512]{0:T(512)S(1)} all-reduce(f32[512]{0:T(512)S(1)} %fusion.2), channel_id=1, replica_groups=mesh['dp'=16,'proto'=16] {'proto'}, use_global_device_ids=true, to_apply=%region_16.17 | all-reduce | flops 512 | bytes 4096 | tf_op jit(solution)/shard_map/psum | solution.py:49
  501.3 4.7 multiply_reduce_fusion.1
  506.0 71.7 %psum.75 = f32[4096]{0:T(1024)S(1)} all-reduce(f32[4096]{0:T(1024)S(1)} %multiply_reduce_fusion.1), channel_id=1, replica_groups=mesh['dp'=16,'proto'=16] {'dp'}, use_global_device_ids=true, to_apply=%region_18.19 | all-reduce | flops 4096 | bytes 32768 | tf_op jit(solution)/shard_map/psum | solution.py:45
  577.7 5.1 fusion.4
  582.8 25.5 %psum.76 = f32[512]{0:T(512)S(1)} all-reduce(f32[512]{0:T(512)S(1)} %fusion.4), channel_id=1, replica_groups=mesh['dp'=16,'proto'=16] {'proto'}, use_global_device_ids=true, to_apply=%region_20.21 | all-reduce | flops 512 | bytes 4096 | tf_op jit(solution)/shard_map/psum | solution.py:49
  608.3 10.2 exponential_reduce_fusion
  618.6 23.6 %all-reduce = (f32[512]{0:T(512)S(1)}, f32[512]{0:T(512)S(1)}) all-reduce(f32[512]{0:T(512)S(1)} %get-tuple-element.5, f32[512]{0:T(512)S(1)} %get-tuple-element.4), channel_id=1, replica_groups=mesh['dp'=16,'proto'=16] {'proto'}, use_global_device_ids=true, to_apply=%region_22.23 | all-reduce | flops 1024 | bytes 8192 | tf_op jit(solution)/shard_map/psum | solution.py:102
  642.2 8.4 multiply_convert_fusion
  650.7 1.9 copy-done.1
  652.6 3.2 convolution_convert_fusion.1
  655.8 0.0 all-reduce.4.cloned.1.call-update
  655.8 0.0 all-reduce.6.cloned.1.call-start
  655.9 139.4 %all-reduce.4.cloned.1.call-done = bf16[512,384]{0,1:T(8,128)(2,1)} async-done(((bf16[512,384]{0,1:T(8,128)(2,1)}), bf16[512,384]{0,1:T(8,128)(2,1)}) %all-reduce.4.cloned.1.call-update) | async-done | bytes 393232 | tf_op jit(solution)/shard_map/psum | solution.py:107
  795.2 1.4 fusion.18
  796.6 2.2 convolution_convert_fusion.2
  798.9 0.0 all-reduce.6.cloned.1.call-update
  798.9 0.3 reduce-scatter.2.cloned.1.call-start
  799.2 6.5 convolution_convert_fusion
  805.7 0.0 reduce-scatter.2.cloned.1.call-update
  805.7 0.1 dynamic-slice.3
  805.8 3.0 convert_multiply_fusion
  808.8 0.6 log_subtract_fusion
  809.4 129.7 %all-reduce.6.cloned.1.call-done = bf16[96,384]{1,0:T(8,128)(2,1)} async-done(((bf16[96,384]{1,0:T(8,128)(2,1)}), bf16[96,384]{1,0:T(8,128)(2,1)}) %all-reduce.6.cloned.1.call-update) | async-done | bytes 73744 | tf_op jit(solution)/shard_map/psum | solution.py:128
  939.1 1.6 convert_element_type.68
  940.6 84.6 %reduce-scatter.2.cloned.1.call-done = bf16[256,384]{1,0:T(8,128)(2,1)} async-done(((bf16[4096,384]{1,0:T(8,128)(2,1)}), bf16[256,384]{1,0:T(8,128)(2,1)}) %reduce-scatter.2.cloned.1.call-update) | async-done | bytes 196624 | tf_op jit(solution)/shard_map/reduce_scatter | solution.py:112
  1025.3 1.2 fusion.21
  1026.5 2.0 fusion.22
  (13 shorter events, 0.1 us)
Async XLA Ops:
  7.2 67.3 %all-gather.9.cloned.1.call-start = ((), (), s32[]{:S(2)}) async-start(), calls=%async_computation.3 | async-start | bytes 1671168 | tf_op jit(solution)/shard_map/all_gather | solution.py:66
  7.9 135.0 %all-gather.11.cloned.1.call-start = ((), (), s32[]{:S(2)}) async-start(), calls=%async_computation.4 | async-start | bytes 1253376 | tf_op jit(solution)/shard_map/all_gather | solution.py:70
  9.7 203.8 %all-gather.5.cloned.1.call-start = ((), (), s32[]{:S(2)}) async-start(), calls=%async_computation.1 | async-start | bytes 1671168 | tf_op jit(solution)/shard_map/all_gather | solution.py:65
  10.4 270.8 %all-gather.7.cloned.1.call-start = ((), (), s32[]{:S(2)}) async-start(), calls=%async_computation.2 | async-start | bytes 1253376 | tf_op jit(solution)/shard_map/all_gather | solution.py:69
  11.0 784.2 %all-reduce.4.cloned.1.call-start = ((), (), s32[]{:S(2)}) async-start(), calls=%async_computation.5 | async-start | bytes 786432 | tf_op jit(solution)/shard_map/psum | solution.py:107
  145.7 143.5 %copy-start = (bf16[4096,384]{1,0:T(8,128)(2,1)S(1)}, bf16[4096,384]{1,0:T(8,128)(2,1)}, u32[]{:S(2)}) copy-start(bf16[4096,384]{1,0:T(8,128)(2,1)} %param.14) | copy-start | bytes 9437188
  145.8 139.5 %collective-permute-start = (bf16[512,384]{0,1:T(8,128)(2,1)S(1)}, bf16[512,384]{0,1:T(8,128)(2,1)}, u32[]{:S(2)}, u32[]{:S(2)}) collective-permute-start(bf16[512,384]{0,1:T(8,128)(2,1)S(1)} %multiply_convert_fusion.1), channel_id=1, source_target_pairs={{0,128},{16,144},{32,160},{48,176},{64,192},{80,208},{96,224},{112... | collective-permute-start | bytes 1179656 | tf_op jit(solution)/shard_map/ppermute | solution.py:19
  501.3 107.1 %copy-start.2 = (f32[512]{0:T(512)S(1)}, f32[512]{0:T(512)}, u32[]{:S(2)}) copy-start(f32[512]{0:T(512)} %add_rsqrt_fusion.3) | copy-start | bytes 6148
  650.7 1.9 copy-start.1
  655.8 283.3 %all-reduce.6.cloned.1.call-start = ((), (), s32[]{:S(2)}) async-start(), calls=%async_computation.6 | async-start | bytes 147456 | tf_op jit(solution)/shard_map/psum | solution.py:128
  798.9 226.4 %reduce-scatter.2.cloned.1.call-start = ((), (), s32[]{:S(2)}) async-start(), calls=%async_computation.7 | async-start | bytes 3342336 | tf_op jit(solution)/shard_map/reduce_scatter | solution.py:112
Sparse Core Ops, SparseCore 0:
  9.8 64.6 all-gather.8
  76.8 66.0 all-gather.10
  144.7 68.7 all-gather.4
  215.2 66.0 all-gather.6
  655.9 139.2 all-reduce.3
  799.0 139.9 all-reduce.5
  943.4 81.8 reduce-scatter.1
where the time goes:
time: 1040 us
  waiting for transfers between devices  609 us (59%)
  blocking collectives  313 us (30%)
  other arithmetic  55.4 us (5%)
  matrix products  34.3 us (3%)
  between operations  14.2 us (1%)
    psum x3, blocking collectives, prototype_inverse(): return 1.0 / lax.psum(local_sums, 'dp')  214 us
    psum x1, waiting for transfers between devices, body(): lax.psum(jnp.dot(score_grad, proto_unit, preferred_element_type=jnp.float...  139 us
    psum x1, waiting for transfers between devices, body(): lax.psum(contract_first(student_own, hidden_grad).astype(jnp.bfloat16), '...  130 us
    reduce_scatter x1, waiting for transfers between devices, body(): lax.psum_scatter(contract_first(score_grad, student_unit).astype(jnp.bflo...  84.6 us
    psum x3, blocking collectives, crop_inverse(): return 1.0 / lax.psum(local_sums, 'proto')  75.5 us
    all_gather x1, waiting for transfers between devices, body(): lax.all_gather(teacher_proj.astype(jnp.bfloat16), 'proto', axis=0, tiled=...  66.6 us
    all_gather x1, waiting for transfers between devices, body(): lax.all_gather(student_cls, 'proto', axis=1, tiled=True)  65.2 us
    all_gather x1, waiting for transfers between devices, body(): lax.all_gather(student_proj, 'proto', axis=0, tiled=True)  62.8 us
  transfers between devices with their start and end apart: 8, of which 7 were waited for; matrix products, arithmetic and copies ran while one was open for 3% of the time, Pallas kernels for 0%

commit v1 on v0

v1 whole, which is shorter than its diff:
```python
import jax
import jax.numpy as jnp
from jax import lax
from jax.sharding import PartitionSpec as P

D = 1536
ITERS = 3


EPSILON = 1e-06
TEACHER_TEMP = 0.07
STUDENT_TEMP = 0.1
MOMENTUM = 0.994
BF16 = jnp.bfloat16
F32 = jnp.float32


def contract_last(left, right):
    return lax.dot_general(left, right, (((1,), (1,)), ((), ())), preferred_element_type=F32)


def contract_first(left, right):
    return lax.dot_general(left, right, (((0,), (0,)), ((), ())), preferred_element_type=F32)


def unit_rows(values):
    factor = lax.rsqrt(jnp.sum(values * values, axis=1, keepdims=True) + EPSILON)
    return (values * factor, factor)


def exchanged(blocks, axis):
    return lax.all_to_all(blocks, axis, 0, 0)


def from_all(value, axis):
    count = lax.axis_size(axis)
    return exchanged(jnp.broadcast_to(value[None], (count,) + value.shape), axis)


def three_terms(value):
    high = value.astype(BF16)
    rest = value - high.astype(F32)
    middle = rest.astype(BF16)
    low = (rest - middle.astype(F32)).astype(BF16)
    return high, middle, low


def swapped(value, axis, bit):
    count = lax.axis_size(axis)
    return lax.ppermute(value, axis, [(one, one ^ bit) for one in range(count)])


def partial_hidden(features, gain, weight):
    scaled = (gain[:, None] * weight.astype(BF16).astype(F32)).astype(BF16)
    share = jnp.dot(features, scaled, preferred_element_type=F32)
    column = jnp.sum(scaled.astype(F32), axis=0)
    values = features.astype(F32)
    return share, column, jnp.sum(values, axis=1), jnp.sum(values * values, axis=1)


def center_and_scale(first, second):
    center = first / D
    return center, lax.rsqrt(second / D - center * center + EPSILON)


def summed_protos(part):
    me = lax.axis_index("dp")
    core, along_y, along_x = me % 2, (me // 2) % 4, me // 8
    rows = part.shape[0] // 16
    blocks = part.reshape(2, 4, 2, rows, part.shape[1])
    keep = lax.dynamic_index_in_dim(blocks, core, 2, False)
    give = lax.dynamic_index_in_dim(blocks, 1 - core, 2, False)
    blocks = (keep.astype(F32) + swapped(give, "dp", 1).astype(F32)).astype(BF16)
    yield None
    total = lax.dynamic_index_in_dim(blocks, along_y, 1, False).astype(F32)
    for step in range(1, 4):
        give = lax.dynamic_index_in_dim(blocks, (along_y + step) % 4, 1, False)
        pairs = [(one, (one & 9) | ((one + 2 * step) & 6)) for one in range(16)]
        total = total + lax.ppermute(give, "dp", pairs).astype(F32)
    blocks = total.astype(BF16)
    yield None
    keep = lax.dynamic_index_in_dim(blocks, along_x, 0, False)
    give = lax.dynamic_index_in_dim(blocks, 1 - along_x, 0, False)
    yield keep.astype(F32) + swapped(give, "dp", 8).astype(F32)


def body(
    student_cls,
    teacher_cls,
    student_gain,
    teacher_gain,
    student_proj,
    teacher_proj,
    prototypes,
    partner,
):
    crops, width = student_cls.shape
    parts = lax.axis_size("proto")
    own = crops // parts
    size = student_proj.shape[1]
    start = lax.axis_index("proto") * width
    opposite = swapped(teacher_cls, "dp", 8)
    gain_s = lax.dynamic_slice_in_dim(student_gain, start, width)
    gain_t = lax.dynamic_slice_in_dim(teacher_gain, start, width)

    share, column, first, second = partial_hidden(student_cls, gain_s, student_proj)
    extra = jnp.concatenate(
        [
            jnp.broadcast_to(column, (parts, 1, size)),
            jnp.pad(
                jnp.stack([first.reshape(parts, own), second.reshape(parts, own)], 1),
                ((0, 0), (0, 5), (0, size - own)),
            ),
        ],
        1,
    )
    packed = jnp.concatenate([share.reshape(parts, own, size), extra], 1)
    packed = packed.reshape(parts * (own + 8), size)
    packed = lax.psum_scatter(packed, "proto", scatter_dimension=0, tiled=True)
    student_center, student_scale = center_and_scale(
        packed[own + 1, :own, None], packed[own + 2, :own, None]
    )
    student_hidden = student_scale * (packed[:own] - student_center * packed[own][None])
    student_unit32, student_factor = unit_rows(student_hidden)
    student_unit = lax.all_gather(student_unit32.astype(BF16), "proto", axis=0, tiled=True)

    share, column, first, second = partial_hidden(opposite, gain_t, teacher_proj)
    small = jnp.pad(
        jnp.stack(three_terms(jnp.stack([first, second])), 0).reshape(6, parts, own).transpose(1, 0, 2).reshape(parts, 1, 6 * own),
        ((0, 0), (0, 0), (0, size - 6 * own)),
    )
    columns = jnp.broadcast_to(jnp.stack(three_terms(column))[None], (parts, 3, size))
    packed = jnp.concatenate([share.astype(BF16).reshape(parts, own, size), columns, small], 1)
    packed = jnp.sum(exchanged(packed, "proto").astype(F32), axis=0)
    sums = jnp.sum(packed[own + 3, : 6 * own].reshape(3, 2, own), axis=0)
    teacher_center, teacher_scale = center_and_scale(sums[0][:, None], sums[1][:, None])
    teacher_hidden = teacher_scale * (
        packed[:own] - teacher_center * jnp.sum(packed[own : own + 3], axis=0)[None]
    )
    teacher_unit = unit_rows(teacher_hidden)[0].astype(BF16)
    teacher_all = from_all(teacher_unit, "proto").reshape(crops, size)
    pick = (partner[:, None] % crops == jnp.arange(crops, dtype=jnp.int32)[None]).astype(BF16)
    paired = jnp.dot(pick, teacher_all, preferred_element_type=F32).astype(BF16)

    proto_unit32, proto_factor = unit_rows(prototypes.astype(F32))
    proto_unit = proto_unit32.astype(BF16)
    protos = proto_unit.shape[0]
    energy = jnp.exp(contract_last(paired, proto_unit) / TEACHER_TEMP)
    row = jnp.ones((crops,), F32)
    for step in range(ITERS):
        sums = jnp.sum(energy * row[:, None], axis=0)
        col = 1.0 / jnp.sum(from_all(sums.reshape(protos // 128, 128), "dp"), axis=0).reshape(protos)
        scaled = energy * col[None, :]
        if step < ITERS - 1:
            sums = jnp.sum(scaled, axis=1)
            row = 1.0 / jnp.sum(from_all(sums.reshape(crops // 128, 128), "proto"), axis=0).reshape(crops)
    logits = contract_last(student_unit, proto_unit) / STUDENT_TEMP
    exponent = jnp.exp(logits)
    sums = jnp.stack([jnp.sum(scaled, axis=1), jnp.sum(exponent, axis=1), jnp.sum(scaled * logits, axis=1)])
    sums = jnp.sum(from_all(sums.reshape(3 * crops // 128, 128), "proto"), axis=0).reshape(3, crops)
    row = 1.0 / sums[0]
    partition = sums[1]
    crop_loss = jnp.log(partition) - sums[2] * row
    score_grad = (
        exponent * (1.0 / (partition * STUDENT_TEMP))[:, None] - scaled * (row / STUDENT_TEMP)[:, None]
    ).astype(BF16)

    stages = summed_protos(contract_first(score_grad, student_unit).astype(BF16))
    next(stages)
    unit_grad = jnp.dot(score_grad, proto_unit, preferred_element_type=F32).astype(BF16)
    unit_grad = jnp.sum(exchanged(unit_grad.reshape(parts, own, size), "proto").astype(F32), axis=0)
    hidden_grad = student_factor * (
        unit_grad - student_unit32 * jnp.sum(student_unit32 * unit_grad, axis=1, keepdims=True)
    )
    sent = (hidden_grad * student_scale).astype(BF16)
    moved = jnp.stack(three_terms(jnp.sum(student_center * sent.astype(F32), axis=0)))
    next(stages)
    packed = from_all(jnp.concatenate([sent, moved], 0), "proto")
    moved = jnp.sum(packed[:, own:].astype(F32), axis=(0, 1))
    sent = packed[:, :own].reshape(crops, size)
    share = gain_s[:, None] * (contract_first(student_cls, sent) - moved[None])
    proto_unit_grad = next(stages)
    grad_proj = jnp.sum(from_all(share.astype(BF16), "dp").astype(F32), axis=0)

    count = protos // lax.axis_size("dp")
    own_start = lax.axis_index("dp") * count
    own_unit, own_factor = unit_rows(
        lax.dynamic_slice_in_dim(prototypes, own_start, count, 0).astype(F32)
    )
    grad_protos = own_factor * (
        proto_unit_grad - own_unit * jnp.sum(own_unit * proto_unit_grad, axis=1, keepdims=True)
    )
    teacher_next = MOMENTUM * teacher_proj + (1.0 - MOMENTUM) * student_proj.astype(F32)
    return (crop_loss, grad_proj, grad_protos, teacher_next)


def solution(mesh):
    placed = (
        P("dp", "proto"),
        P("dp", "proto"),
        P(),
        P(),
        P("proto", None),
        P("proto", None),
        P("proto", None),
        P("dp"),
    )
    return jax.shard_map(
        body,
        mesh=mesh,
        in_specs=placed,
        out_specs=(P("dp"), P("proto", None), P(("proto", "dp"), None), P("proto", None)),
        check_vma=False,
    )
```

time: 1040 us -> 409 us (0.39)
  waiting for transfers between devices: 609 us -> 158 us
  blocking collectives: 313 us -> 40.1 us
  starting transfers between devices: 2.99 us -> 95.5 us
  local copies, waits for them, and re-layouts: 5.92 us -> 18.8 us
    psum x7 -> x0, blocking collectives: 313 us -> none  [the longest x3 214 us: prototype_inverse(): return 1.0 / lax.psum(local_sums, 'dp')]
    psum x2 -> x0, waiting for transfers between devices: 269 us -> none  [the longest x1 139 us: body(): lax.psum(jnp.dot(score_grad, proto_unit, preferred_element_type=jnp.float...]
    all_gather x4 -> x0, waiting for transfers between devices: 254 us -> none  [the longest x1 66.6 us: body(): lax.all_gather(teacher_proj.astype(jnp.bfloat16), 'proto', axis=0, tiled=...]
    unnamed x7 -> x2, waiting for transfers between devices: 1.95 us -> 92.1 us
    reduce_scatter x1 -> x0, waiting for transfers between devices: 84.6 us -> none  [body(): lax.psum_scatter(contract_first(score_grad, student_unit).astype(jnp.bflo...]
    all_to_all x0 -> x10, starting transfers between devices: none -> 76.6 us  [exchanged(): return lax.all_to_all(blocks, axis, 0, 0)]
    all_to_all x0 -> x10, waiting for transfers between devices: none -> 47.9 us  [exchanged(): return lax.all_to_all(blocks, axis, 0, 0)]
    all_gather x0 -> x1, blocking collectives: none -> 28.5 us  [body(): lax.all_gather(student_unit32.astype(BF16), 'proto', axis=0, tiled=True)]
  transfers between devices with their start and end apart: 8 -> 17, of which waited for: 7 -> 9; matrix products, arithmetic and copies ran while one was open for 3% -> 11% of each run, Pallas kernels for 0% -> 0%
where the time goes in v1:
time: 409 us; the launch traced here: 404 us
  waiting for transfers between devices  158 us (39%)
  starting transfers between devices  95.5 us (23%)
  other arithmetic  50.2 us (12%)
  blocking collectives  40.1 us (10%)
  matrix products  26.5 us (6%)
  local copies, waits for them, and re-layouts  18.8 us (5%)
  between operations  15.2 us (4%)
    unnamed x2, waiting for transfers between devices  92.1 us
    all_to_all x10, starting transfers between devices, exchanged(): return lax.all_to_all(blocks, axis, 0, 0)  76.6 us
    all_to_all x10, waiting for transfers between devices, exchanged(): return lax.all_to_all(blocks, axis, 0, 0)  47.9 us
    all_gather x1, blocking collectives, body(): lax.all_gather(student_unit32.astype(BF16), 'proto', axis=0, tiled=True)  28.5 us
    ppermute x3, starting transfers between devices, swapped(): return lax.ppermute(value, axis, [(one, one ^ bit) for one in range(count)])  15.2 us
    dot_general x2, matrix products, contract_last(): lax.dot_general(left, right, (((1,), (1,)), ((), ())), preferred_element_...  15 us
    ppermute x3, waiting for transfers between devices, summed_protos(): total = total + lax.ppermute(give, 'dp', pairs).astype(F32)  13.5 us
    all_to_all x1, blocking collectives, exchanged(): return lax.all_to_all(blocks, axis, 0, 0)  11.7 us
  transfers between devices with their start and end apart: 17, of which 9 were waited for; matrix products, arithmetic and copies ran while one was open for 11% of the time, Pallas kernels for 0%

profile of v1, /device:TPU:1, one launch (start us, length us, event | category | flops | bytes accessed | tf_op | source)
XLA Modules:
  0.0 404.2 jit_solution(5475875510772701185)
XLA Ops:
  7.2 3.7 collective-permute-start
  10.8 0.8 dynamic_slice.36
  11.6 0.8 dynamic_slice.37
  12.4 2.3 fusion.23
  16.0 1.3 fusion.3
  17.4 0.9 copy.72
  19.0 1.9 fusion.13
  20.9 8.3 %all-to-all-start = ((bf16[16,36,384]{2,1,0:T(8,128)(2,1)}), bf16[16,36,384]{2,1,0:T(8,128)(2,1)}, u32[]{:S(2)}, u32[]{:S(2)}) async-start(bf16[16,36,384]{2,1,0:T(8,128)(2,1)} %fusion.13), calls=%async_computation | async-start | bytes 983040 | tf_op jit(solution)/shard_map/all_to_all | solution.py:32
  29.2 0.9 convert_reduce_fusion.3
  30.3 2.2 convolution_bitcast_fusion
  32.5 2.3 copy.77
  34.8 6.9 %all-to-all-done = bf16[16,36,384]{2,1,0:T(8,128)(2,1)} async-done(((bf16[16,36,384]{2,1,0:T(8,128)(2,1)}), bf16[16,36,384]{2,1,0:T(8,128)(2,1)}, u32[]{:S(2)}, u32[]{:S(2)}) %all-to-all-start) | async-done | bytes 442400 | tf_op jit(solution)/shard_map/all_to_all | solution.py:32
  41.7 1.1 convert_reduce_fusion.1
  43.3 0.8 broadcast_in_dim.35
  44.1 6.1 %all-to-all-start.1 = ((bf16[16,32,384]{2,1,0:T(8,128)(2,1)}), bf16[16,32,384]{2,1,0:T(8,128)(2,1)S(1)}, u32[]{:S(2)}, u32[]{:S(2)}) async-start(bf16[16,32,384]{2,1,0:T(8,128)(2,1)} %broadcast_in_dim.35), calls=%async_computation.1 | async-start | bytes 786432 | tf_op jit(solution)/shard_map/all_to_all | solution.py:32
  50.2 1.3 add_select_fusion
  52.8 8.0 %all-to-all-done.1 = bf16[16,32,384]{2,1,0:T(8,128)(2,1)S(1)} async-done(((bf16[16,32,384]{2,1,0:T(8,128)(2,1)}), bf16[16,32,384]{2,1,0:T(8,128)(2,1)S(1)}, u32[]{:S(2)}, u32[]{:S(2)}) %all-to-all-start.1) | async-done | bytes 393248 | tf_op jit(solution)/shard_map/all_to_all | solution.py:32
  60.7 7.3 %fusion.46 = (f32[4096]{0:T(1024)}, f32[512,4096]{1,0:T(8,128)}) fusion(bf16[4096,384]{1,0:T(8,128)(2,1)S(1)} %copy-done, f32[4096]{0:T(1024)} %add_rsqrt_fusion, bf16[512,384]{1,0:T(8,128)(2,1)S(1)} %bitcast.100, s32[512]{0:T(512)} %add_select_fusion), kind=kOutput, calls=%fused_computation.135 | convolution fusion | flops 1821306880 | bytes 11962368 | tf_op jit(solution)/shard_map/dot_general | solution.py:19
  68.1 1.4 broadcast_in_dim.37
  69.5 8.7 %all-to-all-start.2 = ((f32[16,32,128]{2,1,0:T(8,128)}), f32[16,32,128]{2,1,0:T(8,128)S(1)}, u32[]{:S(2)}, u32[]{:S(2)}) async-start(f32[16,32,128]{2,1,0:T(8,128)} %broadcast_in_dim.37), calls=%async_computation.2 | async-start | bytes 524288 | tf_op jit(solution)/shard_map/all_to_all | solution.py:32
  79.0 2.2 pad_maximum_fusion
  81.3 5.6 %all-to-all-done.2 = f32[16,32,128]{2,1,0:T(8,128)S(1)} async-done(((f32[16,32,128]{2,1,0:T(8,128)}), f32[16,32,128]{2,1,0:T(8,128)S(1)}, u32[]{:S(2)}, u32[]{:S(2)}) %all-to-all-start.2) | async-done | bytes 262176 | tf_op jit(solution)/shard_map/all_to_all | solution.py:32
  87.0 4.1 %multiply_reduce_fusion.4 = f32[512]{0:T(512)S(1)} fusion(f32[512,4096]{1,0:T(8,128)} %get-tuple-element.33, f32[4096]{0:T(1024)S(1)} %divide_bitcast_fusion.2), kind=kLoop, calls=%fused_computation.5 | loop fusion | flops 4193792 | bytes 8407040 | tf_op jit(solution)/shard_map/reduce_sum | solution.py:155
  91.1 11.7 %all_to_all.55 = f32[16,4,128]{2,1,0:T(4,128)S(1)} all-to-all(f32[16,4,128]{2,1,0:T(4,128)S(1)} %broadcast_in_dim.39), channel_id=1, replica_groups=mesh['dp'=16,'proto'=16] {'proto'}, dimensions={0} | all-to-all | bytes 65536 | tf_op jit(solution)/shard_map/all_to_all | solution.py:32
  102.8 4.6 %multiply_reduce_fusion.3 = f32[4096]{0:T(1024)S(1)} fusion(f32[512,4096]{1,0:T(8,128)} %get-tuple-element.33, f32[512]{0:T(512)S(1)} %divide_bitcast_fusion.5), kind=kLoop, calls=%fused_computation.4 | loop fusion | flops 4190208 | bytes 8407040 | tf_op jit(solution)/shard_map/reduce_sum | solution.py:151
  108.1 5.6 %all-to-all-start.4 = ((f32[16,32,128]{2,1,0:T(8,128)}), f32[16,32,128]{2,1,0:T(8,128)S(1)}, u32[]{:S(2)}, u32[]{:S(2)}) async-start(f32[16,32,128]{2,1,0:T(8,128)} %broadcast_in_dim.41), calls=%async_computation.4 | async-start | bytes 524288 | tf_op jit(solution)/shard_map/all_to_all | solution.py:32
  114.9 92.1 %all-reduce.5.cloned.1.call-done = f32[640,384]{1,0:T(8,128)} async-done(((f32[640,384]{1,0:T(8,128)}), f32[640,384]{1,0:T(8,128)}) %all-reduce.5.cloned.1.call-update) | async-done | bytes 983056
  207.8 0.8 add_rsqrt_fusion.3
  208.5 1.0 multiply_reduce_fusion.8
  209.6 4.1 %multiply_reduce_fusion.2 = f32[512]{0:T(512)S(1)} fusion(f32[512,4096]{1,0:T(8,128)} %get-tuple-element.33, f32[4096]{0:T(1024)S(1)} %divide_bitcast_fusion.1), kind=kLoop, calls=%fused_computation.3 | loop fusion | flops 4193792 | bytes 8407040 | tf_op jit(solution)/shard_map/reduce_sum | solution.py:155
  214.3 3.5 all-to-all-start.5
  217.8 7.3 %all-to-all-done.5 = f32[16,4,128]{2,1,0:T(4,128)S(1)} async-done(((f32[16,4,128]{2,1,0:T(4,128)}), f32[16,4,128]{2,1,0:T(4,128)S(1)}, u32[]{:S(2)}, u32[]{:S(2)}) %all-to-all-start.5) | async-done | bytes 32800 | tf_op jit(solution)/shard_map/all_to_all | solution.py:32
  225.1 4.6 %multiply_reduce_fusion.1 = f32[4096]{0:T(1024)S(1)} fusion(f32[512,4096]{1,0:T(8,128)} %get-tuple-element.33, f32[512]{0:T(512)S(1)} %divide_bitcast_fusion.4), kind=kLoop, calls=%fused_computation.2 | loop fusion | flops 4190208 | bytes 8407040 | tf_op jit(solution)/shard_map/reduce_sum | solution.py:151
  230.4 19.3 %all-to-all-start.6 = ((f32[16,32,128]{2,1,0:T(8,128)}), f32[16,32,128]{2,1,0:T(8,128)S(1)}, u32[]{:S(2)}, u32[]{:S(2)}) async-start(f32[16,32,128]{2,1,0:T(8,128)} %broadcast_in_dim.45), calls=%async_computation.6 | async-start | bytes 524288 | tf_op jit(solution)/shard_map/all_to_all | solution.py:32
  249.7 0.9 multiply_convert_fusion.3
  250.6 28.5 %all_gather.3 = bf16[512,384]{1,0:T(8,128)(2,1)} all-gather(bf16[32,384]{1,0:T(8,128)(2,1)S(1)} %multiply_convert_fusion.3), channel_id=1, replica_groups=mesh['dp'=16,'proto'=16] {'proto'}, dimensions={0}, use_global_device_ids=true | all-gather | bytes 417792 | tf_op jit(solution)/shard_map/all_gather | solution.py:125
  279.1 7.7 %multiply_reduce_fusion.5 = (f32[512]{0:T(512)S(1)}, f32[512]{0:T(512)S(1)}, f32[512]{0:T(512)S(1)}, f32[512,4096]{1,0:T(8,128)}) fusion(f32[512,4096]{1,0:T(8,128)} %get-tuple-element.33, f32[4096]{0:T(1024)S(1)} %divide_bitcast_fusion, bf16[512,384]{1,0:T(8,128)(2,1)} %all_gather.3, bf16[4096,384]{1,0:T(8,128)(2,1)S(1)} %copy-done, f32[4096]{0:T(1024)S(1)} %copy-done.6), kind=kOutput, calls=%fused_computation.10 | convolution fusion | flops 1627912704 | bytes 20355072 | tf_op jit(solution)/shard_map/dot_general | solution.py:19
  287.5 3.5 all-to-all-start.7
  291.0 7.4 %all-to-all-done.7 = f32[16,12,128]{2,1,0:T(8,128)S(1)} async-done(((f32[16,12,128]{2,1,0:T(8,128)}), f32[16,12,128]{2,1,0:T(8,128)S(1)}, u32[]{:S(2)}, u32[]{:S(2)}) %all-to-all-start.7) | async-done | bytes 98336 | tf_op jit(solution)/shard_map/all_to_all | solution.py:32
  299.0 7.2 %subtract_convert_fusion = bf16[512,4096]{1,0:T(8,128)(2,1)S(1)} fusion(f32[512,4096]{1,0:T(8,128)} %get-tuple-element.34, f32[512,4096]{1,0:T(8,128)} %get-tuple-element.33, f32[512]{0:T(512)S(1)} %get-tuple-element.25, f32[512]{0:T(512)S(1)} %get-tuple-element.23, f32[4096]{0:T(1024)S(1)} %divide_bitcast_fusion), kind=kLoop, calls=%fused_computation | loop fusion | flops 12582912 | bytes 20992000 | tf_op jit(solution)/shard_map/convert_element_type | solution.py:166
  306.3 3.2 convolution_convert_fusion.3
  309.5 3.6 all-to-all-start.8
  313.1 4.6 %convolution_convert_fusion = bf16[4096,384]{1,0:T(8,128)(2,1)S(1)} fusion(bf16[512,4096]{1,0:T(8,128)(2,1)} %copy-done.1, bf16[512,384]{1,0:T(8,128)(2,1)S(1)} %copy-done.4), kind=kOutput, calls=%fused_computation.13 | convolution fusion | flops 1612185600 | bytes 7733248 | tf_op jit(solution)/shard_map/dot_general | solution.py:23
  318.0 1.3 copy.97
  319.3 7.8 %collective-permute-start.1 = (bf16[2,4,256,384]{3,2,0,1:T(8,128)(2,1)}, bf16[2,4,256,384]{3,2,0,1:T(8,128)(2,1)}, u32[]{:S(2)}, u32[]{:S(2)}) collective-permute-start(bf16[2,4,256,384]{3,2,0,1:T(8,128)(2,1)} %bitcast.93), channel_id=1, source_target_pairs={{0,16},{16,0},{32,48},{48,32},{64,80},{80,64},{96,112},{112,96},{1... | collective-permute-start | bytes 4718600 | tf_op jit(solution)/shard_map/ppermute | solution.py:50
  327.2 1.0 multiply_reduce_fusion.7
  328.2 0.9 multiply_reduce_fusion.6
  329.2 0.8 broadcast_in_dim.49
  330.0 7.8 %all-to-all-start.9 = ((bf16[16,35,384]{2,1,0:T(8,128)(2,1)}), bf16[16,35,384]{2,1,0:T(8,128)(2,1)S(1)}, u32[]{:S(2)}, u32[]{:S(2)}) async-start(bf16[16,35,384]{2,1,0:T(8,128)(2,1)} %broadcast_in_dim.49), calls=%async_computation.9 | async-start | bytes 983040 | tf_op jit(solution)/shard_map/all_to_all | solution.py:32
  337.9 12.7 %all-to-all-done.9 = bf16[16,35,384]{2,1,0:T(8,128)(2,1)S(1)} async-done(((bf16[16,35,384]{2,1,0:T(8,128)(2,1)}), bf16[16,35,384]{2,1,0:T(8,128)(2,1)S(1)}, u32[]{:S(2)}, u32[]{:S(2)}) %all-to-all-start.9) | async-done | bytes 430112 | tf_op jit(solution)/shard_map/all_to_all | solution.py:32
  350.6 0.7 copy-done.2
  351.3 1.8 fusion.2
  353.2 1.0 dynamic-slice_bitcast_fusion.2
  354.2 2.6 collective-permute-start.4
  358.3 1.1 broadcast_in_dim.50
  359.4 10.1 %all-to-all-start.10 = ((bf16[16,96,384]{2,1,0:T(8,128)(2,1)}), bf16[16,96,384]{2,1,0:T(8,128)(2,1)S(1)}, u32[]{:S(2)}, u32[]{:S(2)}) async-start(bf16[16,96,384]{2,1,0:T(8,128)(2,1)} %broadcast_in_dim.50), calls=%async_computation.10 | async-start | bytes 2359296 | tf_op jit(solution)/shard_map/all_to_all | solution.py:32
  369.5 1.0 fusion.19
  370.6 13.5 %collective-permute-done.2 = bf16[2,256,384]{2,1,0:T(8,128)(2,1)} collective-permute-done((bf16[2,256,384]{2,1,0:T(8,128)(2,1)S(1)}, bf16[2,256,384]{2,1,0:T(8,128)(2,1)}, u32[]{:S(2)}, u32[]{:S(2)}) %collective-permute-start.2) | collective-permute-done | bytes 393248 | tf_op jit(solution)/shard_map/ppermute | solution.py:79
  384.0 1.4 fusion.10
  385.5 3.7 collective-permute-start.5
  389.2 4.4 %collective-permute-done.5 = bf16[256,384]{1,0:T(8,128)(2,1)S(1)} collective-permute-done((bf16[256,384]{1,0:T(8,128)(2,1)S(1)}, bf16[256,384]{1,0:T(8,128)(2,1)S(1)}, u32[]{:S(2)}, u32[]{:S(2)}) %collective-permute-start.5) | collective-permute-done | bytes 196640 | tf_op jit(solution)/shard_map/ppermute | solution.py:50
  393.6 1.1 fusion.16
  394.7 1.9 fusion.18
  396.6 0.8 convert_reduce_fusion
  (95 shorter events, 11.5 us)
Async XLA Ops:
  7.2 44.3 %copy-start = (bf16[4096,384]{1,0:T(8,128)(2,1)S(1)}, bf16[4096,384]{1,0:T(8,128)(2,1)}, u32[]{:S(2)}) copy-start(bf16[4096,384]{1,0:T(8,128)(2,1)} %param.14) | copy-start | bytes 9437188
  7.2 8.1 %collective-permute-start = (bf16[512,96]{0,1:T(8,128)(2,1)}, bf16[512,96]{0,1:T(8,128)(2,1)S(1)}, u32[]{:S(2)}, u32[]{:S(2)}) collective-permute-start(bf16[512,96]{0,1:T(8,128)(2,1)} %param.9), channel_id=1, source_target_pairs={{0,128},{16,144},{32,160},{48,176},{64,192},{80,208},{96,224},{112... | collective-permute-start | bytes 294920 | tf_op jit(solution)/shard_map/ppermute | solution.py:50
  11.6 3.1 copy-start.10
  12.4 2.3 copy-start.8
  15.3 0.6 copy-start.5
  20.9 20.8 %all-to-all-start = ((bf16[16,36,384]{2,1,0:T(8,128)(2,1)}), bf16[16,36,384]{2,1,0:T(8,128)(2,1)}, u32[]{:S(2)}, u32[]{:S(2)}) async-start(bf16[16,36,384]{2,1,0:T(8,128)(2,1)} %fusion.13), calls=%async_computation | async-start | bytes 983040 | tf_op jit(solution)/shard_map/all_to_all | solution.py:32
  44.1 16.7 %all-to-all-start.1 = ((bf16[16,32,384]{2,1,0:T(8,128)(2,1)}), bf16[16,32,384]{2,1,0:T(8,128)(2,1)S(1)}, u32[]{:S(2)}, u32[]{:S(2)}) async-start(bf16[16,32,384]{2,1,0:T(8,128)(2,1)} %broadcast_in_dim.35), calls=%async_computation.1 | async-start | bytes 786432 | tf_op jit(solution)/shard_map/all_to_all | solution.py:32
  69.5 17.4 %all-to-all-start.2 = ((f32[16,32,128]{2,1,0:T(8,128)}), f32[16,32,128]{2,1,0:T(8,128)S(1)}, u32[]{:S(2)}, u32[]{:S(2)}) async-start(f32[16,32,128]{2,1,0:T(8,128)} %broadcast_in_dim.37), calls=%async_computation.2 | async-start | bytes 524288 | tf_op jit(solution)/shard_map/all_to_all | solution.py:32
  78.2 128.8 %all-reduce.5.cloned.1.call-start = ((), (), s32[]{:S(2)}) async-start(), calls=%async_computation.11 | async-start | bytes 1966080
  91.0 22.7 %copy-start.11 = (u32[256]{0:T(256)S(1)}, u32[256]{0:T(256)}, u32[]{:S(2)}) copy-start(u32[256]{0:T(256)} %constant.149) | copy-start | bytes 3076
  108.1 101.4 %all-to-all-start.4 = ((f32[16,32,128]{2,1,0:T(8,128)}), f32[16,32,128]{2,1,0:T(8,128)S(1)}, u32[]{:S(2)}, u32[]{:S(2)}) async-start(f32[16,32,128]{2,1,0:T(8,128)} %broadcast_in_dim.41), calls=%async_computation.4 | async-start | bytes 524288 | tf_op jit(solution)/shard_map/all_to_all | solution.py:32
  213.6 65.5 %copy-start.6 = (f32[4096]{0:T(1024)S(1)}, f32[4096]{0:T(1024)}, u32[]{:S(2)}) copy-start(f32[4096]{0:T(1024)} %add_rsqrt_fusion) | copy-start | bytes 49156
  214.3 10.9 %all-to-all-start.5 = ((f32[16,4,128]{2,1,0:T(4,128)}), f32[16,4,128]{2,1,0:T(4,128)S(1)}, u32[]{:S(2)}, u32[]{:S(2)}) async-start(f32[16,4,128]{2,1,0:T(4,128)} %broadcast_in_dim.43), calls=%async_computation.5 | async-start | bytes 65536 | tf_op jit(solution)/shard_map/all_to_all | solution.py:32
  230.4 48.6 %all-to-all-start.6 = ((f32[16,32,128]{2,1,0:T(8,128)}), f32[16,32,128]{2,1,0:T(8,128)S(1)}, u32[]{:S(2)}, u32[]{:S(2)}) async-start(f32[16,32,128]{2,1,0:T(8,128)} %broadcast_in_dim.45), calls=%async_computation.6 | async-start | bytes 524288 | tf_op jit(solution)/shard_map/all_to_all | solution.py:32
  287.5 10.9 %all-to-all-start.7 = ((f32[16,12,128]{2,1,0:T(8,128)}), f32[16,12,128]{2,1,0:T(8,128)S(1)}, u32[]{:S(2)}, u32[]{:S(2)}) async-start(f32[16,12,128]{2,1,0:T(8,128)} %broadcast_in_dim.48), calls=%async_computation.7 | async-start | bytes 262144 | tf_op jit(solution)/shard_map/all_to_all | solution.py:32
  299.0 7.3 %copy-start.7 = (f32[4096]{0:T(1024)S(1)}, f32[4096]{0:T(1024)}, u32[]{:S(2)}) copy-start(f32[4096]{0:T(1024)} %add_rsqrt_fusion) | copy-start | bytes 49156
  306.3 3.2 copy-start.1
  306.3 6.8 %copy-start.4 = (bf16[512,384]{1,0:T(8,128)(2,1)S(1)}, bf16[512,384]{1,0:T(8,128)(2,1)}, u32[]{:S(2)}) copy-start(bf16[512,384]{1,0:T(8,128)(2,1)} %all_gather.3) | copy-start | bytes 1179652
  309.5 17.7 %all-to-all-start.8 = ((bf16[16,32,384]{2,1,0:T(8,128)(2,1)}), bf16[16,32,384]{2,1,0:T(8,128)(2,1)S(1)}, u32[]{:S(2)}, u32[]{:S(2)}) async-start(bf16[16,32,384]{2,1,0:T(8,128)(2,1)} %bitcast.99), calls=%async_computation.8 | async-start | bytes 786432 | tf_op jit(solution)/shard_map/all_to_all | solution.py:32
  318.0 40.0 %copy-start.3 = (bf16[512,96]{0,1:T(8,128)(2,1)S(1)}, bf16[512,96]{0,1:T(8,128)(2,1)}, u32[]{:S(2)}) copy-start(bf16[512,96]{0,1:T(8,128)(2,1)} %param.8) | copy-start | bytes 294916
  318.0 40.0 %copy-start.9 = (f32[96]{0:T(128)S(1)}, f32[96]{0:T(128)}, u32[]{:S(2)}) copy-start(f32[96]{0:T(128)} %copy-done.8) | copy-start | bytes 1156
  319.3 31.2 %collective-permute-start.1 = (bf16[2,4,256,384]{3,2,0,1:T(8,128)(2,1)}, bf16[2,4,256,384]{3,2,0,1:T(8,128)(2,1)}, u32[]{:S(2)}, u32[]{:S(2)}) collective-permute-start(bf16[2,4,256,384]{3,2,0,1:T(8,128)(2,1)} %bitcast.93), channel_id=1, source_target_pairs={{0,16},{16,0},{32,48},{48,32},{64,80},{80,64},{96,112},{112,96},{1... | collective-permute-start | bytes 4718600 | tf_op jit(solution)/shard_map/ppermute | solution.py:50
  330.0 20.6 %all-to-all-start.9 = ((bf16[16,35,384]{2,1,0:T(8,128)(2,1)}), bf16[16,35,384]{2,1,0:T(8,128)(2,1)S(1)}, u32[]{:S(2)}, u32[]{:S(2)}) async-start(bf16[16,35,384]{2,1,0:T(8,128)(2,1)} %broadcast_in_dim.49), calls=%async_computation.9 | async-start | bytes 983040 | tf_op jit(solution)/shard_map/all_to_all | solution.py:32
  350.6 0.8 copy-start.2
  351.3 6.7 %slice-start = ((bf16[16,35,384]{2,1,0:T(8,128)(2,1)}), bf16[16,32,384]{2,1,0:T(8,128)(2,1)S(1)}, s32[]{:S(2)}) async-start(bf16[16,35,384]{2,1,0:T(8,128)(2,1)} %copy-done.2), calls=%async_computation.12 | async-start | bytes 786432 | tf_op jit(solution)/shard_map/slice | solution.py:180
  354.2 16.3 %collective-permute-start.4 = (bf16[2,256,384]{2,1,0:T(8,128)(2,1)}, bf16[2,256,384]{2,1,0:T(8,128)(2,1)}, u32[]{:S(2)}, u32[]{:S(2)}) collective-permute-start(bf16[2,256,384]{2,1,0:T(8,128)(2,1)} %get-tuple-element.18), channel_id=1, source_target_pairs={{0,96},{16,112},{32,0},{48,16},{64,32},{80,48},{96,64},{112,80},{1... | collective-permute-start | bytes 1179656 | tf_op jit(solution)/shard_map/ppermute | solution.py:79
  356.8 13.7 %collective-permute-start.3 = (bf16[2,256,384]{2,1,0:T(8,128)(2,1)}, bf16[2,256,384]{2,1,0:T(8,128)(2,1)}, u32[]{:S(2)}, u32[]{:S(2)}) collective-permute-start(bf16[2,256,384]{2,1,0:T(8,128)(2,1)} %get-tuple-element.19), channel_id=1, source_target_pairs={{0,64},{16,80},{32,96},{48,112},{64,0},{80,16},{96,32},{112,48},{1... | collective-permute-start | bytes 1179656 | tf_op jit(solution)/shard_map/ppermute | solution.py:79
  357.4 26.6 %collective-permute-start.2 = (bf16[2,256,384]{2,1,0:T(8,128)(2,1)S(1)}, bf16[2,256,384]{2,1,0:T(8,128)(2,1)}, u32[]{:S(2)}, u32[]{:S(2)}) collective-permute-start(bf16[2,256,384]{2,1,0:T(8,128)(2,1)S(1)} %get-tuple-element.17), channel_id=1, source_target_pairs={{0,32},{16,48},{32,64},{48,80},{64,96},{80,112},{96,0},{112,16},{1... | collective-permute-start | bytes 1179656 | tf_op jit(solution)/shard_map/ppermute | solution.py:79
  359.4 37.2 %all-to-all-start.10 = ((bf16[16,96,384]{2,1,0:T(8,128)(2,1)}), bf16[16,96,384]{2,1,0:T(8,128)(2,1)S(1)}, u32[]{:S(2)}, u32[]{:S(2)}) async-start(bf16[16,96,384]{2,1,0:T(8,128)(2,1)} %broadcast_in_dim.50), calls=%async_computation.10 | async-start | bytes 2359296 | tf_op jit(solution)/shard_map/all_to_all | solution.py:32
  385.5 8.0 %collective-permute-start.5 = (bf16[256,384]{1,0:T(8,128)(2,1)S(1)}, bf16[256,384]{1,0:T(8,128)(2,1)S(1)}, u32[]{:S(2)}, u32[]{:S(2)}) collective-permute-start(bf16[256,384]{1,0:T(8,128)(2,1)S(1)} %dynamic-slice_bitcast_fusion.3), channel_id=1, source_target_pairs={{0,128},{16,144},{32,160},{48,176},{64,192},{80,208},{96,224},{112... | collective-permute-start | bytes 589832 | tf_op jit(solution)/shard_map/ppermute | solution.py:50
Sparse Core Ops, SparseCore 0:
  81.7 125.2 all-reduce.4

commit v2 on v1

--- a/solution.py
+++ b/solution.py
@@ -61,6 +61,26 @@
 def center_and_scale(first, second):
     center = first / D
     return center, lax.rsqrt(second / D - center * center + EPSILON)
+
+
+def packed_shares(features, gain, weight, parts):
+    crops, size = features.shape[0], weight.shape[1]
+    own = crops // parts
+    share, column, first, second = partial_hidden(features, gain, weight)
+    sums = jnp.stack(three_terms(jnp.stack([first, second])))
+    sums = sums.reshape(6, parts, own).transpose(1, 0, 2).reshape(parts, 1, 6 * own)
+    sums = jnp.pad(sums, ((0, 0), (0, 0), (0, size - 6 * own)))
+    columns = jnp.broadcast_to(jnp.stack(three_terms(column))[None], (parts, 3, size))
+    return jnp.concatenate([share.astype(BF16).reshape(parts, own, size), columns, sums], 1)
+
+
+def summed_hidden(packed):
+    own = packed.shape[1] - 4
+    packed = jnp.sum(packed.astype(F32), axis=0)
+    sums = jnp.sum(packed[own + 3, : 6 * own].reshape(3, 2, own), axis=0)
+    center, scale = center_and_scale(sums[0][:, None], sums[1][:, None])
+    column = jnp.sum(packed[own : own + 3], axis=0)[None]
+    return scale * (packed[:own] - center * column), center, scale
 
 
 def summed_protos(part):
@@ -103,40 +123,9 @@
     gain_s = lax.dynamic_slice_in_dim(student_gain, start, width)
     gain_t = lax.dynamic_slice_in_dim(teacher_gain, start, width)
 
-    share, column, first, second = partial_hidden(student_cls, gain_s, student_proj)
-    extra = jnp.concatenate(
-        [
-            jnp.broadcast_to(column, (parts, 1, size)),
-            jnp.pad(
-                jnp.stack([first.reshape(parts, own), second.reshape(parts, own)], 1),
-                ((0, 0), (0, 5), (0, size - own)),
-            ),
-        ],
-        1,
-    )
-    packed = jnp.concatenate([share.reshape(parts, own, size), extra], 1)
-    packed = packed.reshape(parts * (own + 8), size)
-    packed = lax.psum_scatter(packed, "proto", scatter_dimension=0, tiled=True)
-    student_center, student_scale = center_and_scale(
-        packed[own + 1, :own, None], packed[own + 2, :own, None]
-    )
-    student_hidden = student_scale * (packed[:own] - student_center * packed[own][None])
-    student_unit32, student_factor = unit_rows(student_hidden)
-    student_unit = lax.all_gather(student_unit32.astype(BF16), "proto", axis=0, tiled=True)
-
-    share, column, first, second = partial_hidden(opposite, gain_t, teacher_proj)
-    small = jnp.pad(
-        jnp.stack(three_terms(jnp.stack([first, second])), 0).reshape(6, parts, own).transpose(1, 0, 2).reshape(parts, 1, 6 * own),
-        ((0, 0), (0, 0), (0, size - 6 * own)),
-    )
-    columns = jnp.broadcast_to(jnp.stack(three_terms(column))[None], (parts, 3, size))
-    packed = jnp.concatenate([share.astype(BF16).reshape(parts, own, size), columns, small], 1)
-    packed = jnp.sum(exchanged(packed, "proto").astype(F32), axis=0)
-    sums = jnp.sum(packed[own + 3, : 6 * own].reshape(3, 2, own), axis=0)
-    teacher_center, teacher_scale = center_and_scale(sums[0][:, None], sums[1][:, None])
-    teacher_hidden = teacher_scale * (
-        packed[:own] - teacher_center * jnp.sum(packed[own : own + 3], axis=0)[None]
-    )
+    student_blocks = packed_shares(student_cls, gain_s, student_proj, parts)
+    teacher_blocks = packed_shares(opposite, gain_t, teacher_proj, parts)
+    teacher_hidden = summed_hidden(exchanged(teacher_blocks, "proto"))[0]
     teacher_unit = unit_rows(teacher_hidden)[0].astype(BF16)
     teacher_all = from_all(teacher_unit, "proto").reshape(crops, size)
     pick = (partner[:, None] % crops == jnp.arange(crops, dtype=jnp.int32)[None]).astype(BF16)
@@ -148,27 +137,49 @@
     energy = jnp.exp(contract_last(paired, proto_unit) / TEACHER_TEMP)
     row = jnp.ones((crops,), F32)
     for step in range(ITERS):
-        sums = jnp.sum(energy * row[:, None], axis=0)
-        col = 1.0 / jnp.sum(from_all(sums.reshape(protos // 128, 128), "dp"), axis=0).reshape(protos)
+        sums = jnp.sum(energy * row[:, None], axis=0).reshape(protos // 128, 128)
+        if step == 0:
+            sums, student_blocks = lax.optimization_barrier((sums, student_blocks))
+            student_blocks = exchanged(student_blocks, "proto")
+        if step == 1:
+            sums, student_own = lax.optimization_barrier((sums, student_own))
+            student_unit = from_all(student_own, "proto").reshape(crops, size)
+        if step == 2:
+            sums, student_unit = lax.optimization_barrier((sums, student_unit))
+            exponent = jnp.exp(contract_last(student_unit, proto_unit) / STUDENT_TEMP)
+            partition = jnp.sum(exponent, axis=1)
+            exponent = exponent.astype(BF16)
+            pulled = jnp.dot(exponent, proto_unit, preferred_element_type=F32)
+        sums = from_all(sums, "dp")
+        if step == 2:
+            sums, exponent, partition, pulled = lax.optimization_barrier(
+                (sums, exponent, partition, pulled)
+            )
+        col = 1.0 / jnp.sum(sums, axis=0).reshape(protos)
         scaled = energy * col[None, :]
         if step < ITERS - 1:
             sums = jnp.sum(scaled, axis=1)
             row = 1.0 / jnp.sum(from_all(sums.reshape(crops // 128, 128), "proto"), axis=0).reshape(crops)
-    logits = contract_last(student_unit, proto_unit) / STUDENT_TEMP
-    exponent = jnp.exp(logits)
-    sums = jnp.stack([jnp.sum(scaled, axis=1), jnp.sum(exponent, axis=1), jnp.sum(scaled * logits, axis=1)])
+        if step == 0:
+            student_hidden, student_center, student_scale = summed_hidden(student_blocks)
+            student_unit32, student_factor = unit_rows(student_hidden)
+            student_own = student_unit32.astype(BF16)
+    coded = jnp.dot(scaled.astype(BF16), proto_unit, preferred_element_type=F32)
+    expected = jnp.sum(student_unit.astype(F32) * coded, axis=1) / STUDENT_TEMP
+    sums = jnp.stack([jnp.sum(scaled, axis=1), partition, expected])
     sums = jnp.sum(from_all(sums.reshape(3 * crops // 128, 128), "proto"), axis=0).reshape(3, crops)
     row = 1.0 / sums[0]
     partition = sums[1]
     crop_loss = jnp.log(partition) - sums[2] * row
-    score_grad = (
-        exponent * (1.0 / (partition * STUDENT_TEMP))[:, None] - scaled * (row / STUDENT_TEMP)[:, None]
-    ).astype(BF16)
+    wanted = (1.0 / (partition * STUDENT_TEMP))[:, None]
+    given = (row / STUDENT_TEMP)[:, None]
+    unit_grad = (pulled * wanted - coded * given).astype(BF16).reshape(parts, own, size)
+    unit_grad = exchanged(unit_grad, "proto")
+    score_grad = (exponent.astype(F32) * wanted - scaled * given).astype(BF16)
 
     stages = summed_protos(contract_first(score_grad, student_unit).astype(BF16))
     next(stages)
-    unit_grad = jnp.dot(score_grad, proto_unit, preferred_element_type=F32).astype(BF16)
-    unit_grad = jnp.sum(exchanged(unit_grad.reshape(parts, own, size), "proto").astype(F32), axis=0)
+    unit_grad = jnp.sum(unit_grad.astype(F32), axis=0)
     hidden_grad = student_factor * (
         unit_grad - student_unit32 * jnp.sum(student_unit32 * unit_grad, axis=1, keepdims=True)
     )

time: 409 us -> 298 us (0.73)
  waiting for transfers between devices: 158 us -> 61.4 us
  starting transfers between devices: 95.5 us -> 72 us
  blocking collectives: 40.1 us -> 56 us
  between operations: 15.2 us -> 1.28 us
  matrix products: 26.5 us -> 32.2 us
    unnamed x2 -> x0, waiting for transfers between devices: 92.1 us -> none
    all_to_all x1 -> x4, blocking collectives: 11.7 us -> 56 us  [exchanged(): return lax.all_to_all(blocks, axis, 0, 0)]
    all_gather x1 -> x0, blocking collectives: 28.5 us -> none  [body(): lax.all_gather(student_unit32.astype(BF16), 'proto', axis=0, tiled=True)]
    all_to_all x10 -> x9, starting transfers between devices: 76.6 us -> 56.5 us  [exchanged(): return lax.all_to_all(blocks, axis, 0, 0)]
    dot_general x1 -> x2, matrix products: 3.2 us -> 10.1 us  [the longest x1 6.67 us: body(): coded = jnp.dot(scaled.astype(BF16), proto_unit, preferred_element_type=F32)]
    reduce_sum x9 -> x13, other arithmetic: 10.4 us -> 17.1 us  [the longest x2 9.11 us: body(): sums = jnp.sum(energy * row[:, None], axis=0).reshape(protos // 128, 128)]
    convert_element_type x2, other arithmetic: 8.12 us -> 2.4 us  [the longest x1 2.32 us: body(): (pulled * wanted - coded * given).astype(BF16).reshape(parts, own, size)]
    all_to_all x10 -> x9, waiting for transfers between devices: 47.9 us -> 46.2 us  [exchanged(): return lax.all_to_all(blocks, axis, 0, 0)]
  transfers between devices with their start and end apart: 17 -> 15, of which waited for: 9 -> 8; matrix products, arithmetic and copies ran while one was open for 11% -> 17% of each run, Pallas kernels for 0% -> 0%
where the time goes in v2:
time: 298 us; the launch traced here: 295 us
  starting transfers between devices  72 us (24%)
  waiting for transfers between devices  61.4 us (21%)
  blocking collectives  56 us (19%)
  other arithmetic  49.9 us (17%)
  matrix products  32.2 us (11%)
  local copies, waits for them, and re-layouts  22.1 us (7%)
    all_to_all x9, starting transfers between devices, exchanged(): return lax.all_to_all(blocks, axis, 0, 0)  56.5 us
    all_to_all x4, blocking collectives, exchanged(): return lax.all_to_all(blocks, axis, 0, 0)  56 us
    all_to_all x9, waiting for transfers between devices, exchanged(): return lax.all_to_all(blocks, axis, 0, 0)  46.2 us
    dot_general x2, matrix products, contract_last(): lax.dot_general(left, right, (((1,), (1,)), ((), ())), preferred_element_...  11.7 us
    ppermute x3, starting transfers between devices, swapped(): return lax.ppermute(value, axis, [(one, one ^ bit) for one in range(count)])  11.6 us
    ppermute x3, waiting for transfers between devices, summed_protos(): total = total + lax.ppermute(give, 'dp', pairs).astype(F32)  10.6 us
    reduce_sum x2, other arithmetic, body(): sums = jnp.sum(energy * row[:, None], axis=0).reshape(protos // 128, 128)  9.11 us
    reduce_sum x2, other arithmetic, body(): sums = jnp.sum(scaled, axis=1)  8.16 us
  transfers between devices with their start and end apart: 15, of which 8 were waited for; matrix products, arithmetic and copies ran while one was open for 17% of the time, Pallas kernels for 0%

profile of v2, /device:TPU:1, one launch (start us, length us, event | category | flops | bytes accessed | tf_op | source)
XLA Modules:
  0.0 294.8 jit_solution(13778088131221238024)
XLA Ops:
  0.6 3.7 %collective-permute-start = (bf16[512,96]{0,1:T(8,128)(2,1)}, bf16[512,96]{0,1:T(8,128)(2,1)S(1)}, u32[]{:S(2)}, u32[]{:S(2)}) collective-permute-start(bf16[512,96]{0,1:T(8,128)(2,1)} %param.9), channel_id=1, source_target_pairs={{0,128},{16,144},{32,160},{48,176},{64,192},{80,208},{96,224},{112... | collective-permute-start | bytes 294920 | tf_op jit(solution)/shard_map/ppermute | solution.py:50
  6.3 1.7 fusion.33
  10.0 1.3 fusion.10
  11.3 0.9 copy.63
  13.0 1.9 fusion.22
  14.8 8.3 %all-to-all-start = ((bf16[16,36,384]{2,1,0:T(8,128)(2,1)}), bf16[16,36,384]{2,1,0:T(8,128)(2,1)}, u32[]{:S(2)}, u32[]{:S(2)}) async-start(bf16[16,36,384]{2,1,0:T(8,128)(2,1)} %fusion.22), calls=%async_computation | async-start | bytes 983040 | tf_op jit(solution)/shard_map/all_to_all | solution.py:32
  23.2 0.9 convert_reduce_fusion.4
  24.1 1.2 reduce_sum.427
  25.6 1.3 fusion.11
  26.9 0.9 copy.66
  28.6 1.9 fusion.23
  30.5 5.2 %all-to-all-done = bf16[16,36,384]{2,1,0:T(8,128)(2,1)} async-done(((bf16[16,36,384]{2,1,0:T(8,128)(2,1)}), bf16[16,36,384]{2,1,0:T(8,128)(2,1)}, u32[]{:S(2)}, u32[]{:S(2)}) %all-to-all-start) | async-done | bytes 442400 | tf_op jit(solution)/shard_map/all_to_all | solution.py:32
  35.6 1.1 convert_reduce_fusion.2
  38.0 6.1 %all-to-all-start.1 = ((bf16[16,32,384]{2,1,0:T(8,128)(2,1)}), bf16[16,32,384]{2,1,0:T(8,128)(2,1)S(1)}, u32[]{:S(2)}, u32[]{:S(2)}) async-start(bf16[16,32,384]{2,1,0:T(8,128)(2,1)} %broadcast_in_dim.31), calls=%async_computation.1 | async-start | bytes 786432 | tf_op jit(solution)/shard_map/all_to_all | solution.py:32
  44.2 1.3 add_select_fusion
  46.1 8.5 %all-to-all-done.1 = bf16[16,32,384]{2,1,0:T(8,128)(2,1)S(1)} async-done(((bf16[16,32,384]{2,1,0:T(8,128)(2,1)}), bf16[16,32,384]{2,1,0:T(8,128)(2,1)S(1)}, u32[]{:S(2)}, u32[]{:S(2)}) %all-to-all-start.1) | async-done | bytes 393248 | tf_op jit(solution)/shard_map/all_to_all | solution.py:32
  54.7 7.3 %fusion.57 = (f32[4096]{0:T(1024)}, f32[512,4096]{1,0:T(8,128)}) fusion(bf16[4096,384]{1,0:T(8,128)(2,1)S(1)} %copy-done, f32[4096]{0:T(1024)S(1)} %add_rsqrt_fusion, bf16[512,384]{1,0:T(8,128)(2,1)S(1)} %bitcast.102, s32[512]{0:T(512)} %add_select_fusion), kind=kOutput, calls=%fused_computation.153 | convolution fusion | flops 1821306880 | bytes 11962368 | tf_op jit(solution)/shard_map/dot_general | solution.py:19
  62.7 17.5 %all_to_all.65 = f32[16,32,128]{2,1,0:T(8,128)S(1)} all-to-all(f32[16,32,128]{2,1,0:T(8,128)S(1)} %broadcast_in_dim.33), channel_id=1, replica_groups=mesh['dp'=16,'proto'=16] {'dp'}, dimensions={0} | all-to-all | bytes 524288 | tf_op jit(solution)/shard_map/all_to_all | solution.py:32
  80.2 4.1 %multiply_reduce_fusion.3 = f32[512]{0:T(512)S(1)} fusion(f32[512,4096]{1,0:T(8,128)} %get-tuple-element.54, f32[4096]{0:T(1024)S(1)} %divide_bitcast_fusion.2), kind=kLoop, calls=%fused_computation.5 | loop fusion | flops 4193792 | bytes 8407040 | tf_op jit(solution)/shard_map/reduce_sum | solution.py:161
  84.3 11.5 %all_to_all.66 = f32[16,4,128]{2,1,0:T(4,128)S(1)} all-to-all(f32[16,4,128]{2,1,0:T(4,128)S(1)} %broadcast_in_dim.35), channel_id=1, replica_groups=mesh['dp'=16,'proto'=16] {'proto'}, dimensions={0} | all-to-all | bytes 65536 | tf_op jit(solution)/shard_map/all_to_all | solution.py:32
  95.8 4.2 %all-to-all-start.4 = ((bf16[16,36,384]{2,1,0:T(8,128)(2,1)}), bf16[16,36,384]{2,1,0:T(8,128)(2,1)}, u32[]{:S(2)}, u32[]{:S(2)}) async-start(bf16[16,36,384]{2,1,0:T(8,128)(2,1)} %fusion.23), calls=%async_computation.4 | async-start | bytes 983040 | tf_op jit(solution)/shard_map/all_to_all | solution.py:32
  100.1 4.6 %multiply_reduce_fusion.2 = f32[4096]{0:T(1024)S(1)} fusion(f32[512,4096]{1,0:T(8,128)} %get-tuple-element.54, f32[512]{0:T(512)S(1)} %divide_bitcast_fusion.5), kind=kLoop, calls=%fused_computation.4 | loop fusion | flops 4190208 | bytes 8407040 | tf_op jit(solution)/shard_map/reduce_sum | solution.py:140
  104.6 7.4 %all-to-all-done.4 = bf16[16,36,384]{2,1,0:T(8,128)(2,1)} async-done(((bf16[16,36,384]{2,1,0:T(8,128)(2,1)}), bf16[16,36,384]{2,1,0:T(8,128)(2,1)}, u32[]{:S(2)}, u32[]{:S(2)}) %all-to-all-start.4) | async-done | bytes 442400 | tf_op jit(solution)/shard_map/all_to_all | solution.py:32
  112.0 1.1 convert_reduce_fusion.1
  114.1 15.2 %all_to_all.67 = f32[16,32,128]{2,1,0:T(8,128)S(1)} all-to-all(f32[16,32,128]{2,1,0:T(8,128)S(1)} %broadcast_in_dim.36), channel_id=1, replica_groups=mesh['dp'=16,'proto'=16] {'dp'}, dimensions={0} | all-to-all | bytes 524288 | tf_op jit(solution)/shard_map/all_to_all | solution.py:32
  129.4 4.1 %multiply_reduce_fusion.1 = f32[512]{0:T(512)S(1)} fusion(f32[512,4096]{1,0:T(8,128)} %get-tuple-element.54, f32[4096]{0:T(1024)S(1)} %divide_bitcast_fusion.1), kind=kLoop, calls=%fused_computation.3 | loop fusion | flops 4193792 | bytes 8407040 | tf_op jit(solution)/shard_map/reduce_sum | solution.py:161
  133.5 11.8 %all_to_all.68 = f32[16,4,128]{2,1,0:T(4,128)} all-to-all(f32[16,4,128]{2,1,0:T(4,128)S(1)} %broadcast_in_dim.38), channel_id=1, replica_groups=mesh['dp'=16,'proto'=16] {'proto'}, dimensions={0} | all-to-all | bytes 65536 | tf_op jit(solution)/shard_map/all_to_all | solution.py:32
  146.1 3.6 %all-to-all-start.7 = ((bf16[16,32,384]{2,1,0:T(8,128)(2,1)}), bf16[16,32,384]{2,1,0:T(8,128)(2,1)S(1)}, u32[]{:S(2)}, u32[]{:S(2)}) async-start(bf16[16,32,384]{2,1,0:T(8,128)(2,1)} %broadcast_in_dim.39), calls=%async_computation.7 | async-start | bytes 786432 | tf_op jit(solution)/shard_map/all_to_all | solution.py:32
  150.5 4.6 %multiply_reduce_fusion = f32[4096]{0:T(1024)S(1)} fusion(f32[512,4096]{1,0:T(8,128)} %get-tuple-element.54, f32[512]{0:T(512)S(1)} %divide_bitcast_fusion.4), kind=kLoop, calls=%fused_computation.2 | loop fusion | flops 4190208 | bytes 8407040 | tf_op jit(solution)/shard_map/reduce_sum | solution.py:140
  155.0 3.9 %all-to-all-done.7 = bf16[16,32,384]{2,1,0:T(8,128)(2,1)S(1)} async-done(((bf16[16,32,384]{2,1,0:T(8,128)(2,1)}), bf16[16,32,384]{2,1,0:T(8,128)(2,1)S(1)}, u32[]{:S(2)}, u32[]{:S(2)}) %all-to-all-start.7) | async-done | bytes 393248 | tf_op jit(solution)/shard_map/all_to_all | solution.py:32
  159.7 8.3 %all-to-all-start.8 = ((f32[16,32,128]{2,1,0:T(8,128)}), f32[16,32,128]{2,1,0:T(8,128)}, u32[]{:S(2)}, u32[]{:S(2)}) async-start(f32[16,32,128]{2,1,0:T(8,128)} %broadcast_in_dim.40), calls=%async_computation.8 | async-start | bytes 524288 | tf_op jit(solution)/shard_map/all_to_all | solution.py:32
  167.9 4.4 %fusion = (f32[512]{0:T(512)}, bf16[512,4096]{1,0:T(8,128)(2,1)S(1)}) fusion(bf16[512,384]{1,0:T(8,128)(2,1)S(1)} %bitcast.99, bf16[4096,384]{1,0:T(8,128)(2,1)S(1)} %copy-done, f32[4096]{0:T(1024)} %copy-done.6), kind=kOutput, calls=%fused_computation.9 | convolution fusion | flops 1621622272 | bytes 7751680 | tf_op jit(solution)/shard_map/dot_general | solution.py:19
  172.3 2.0 copy-done.23
  174.3 3.4 %fusion.52 = f32[512,384]{1,0:T(8,128)} fusion(bf16[512,4096]{1,0:T(8,128)(2,1)S(1)} %get-tuple-element.23, bf16[4096,384]{1,0:T(8,128)(2,1)S(1)} %copy-done, f32[4096]{0:T(1024)S(1)} %copy-done.7), kind=kOutput, calls=%fused_computation.151 | convolution fusion | flops 1615331328 | bytes 8142848 | tf_op jit(solution)/shard_map/dot_general | solution.py:152
  177.7 1.6 reduce_sum.357
  180.0 6.7 %multiply_reduce_fusion.5 = (f32[512]{0:T(512)S(1)}, f32[512,384]{1,0:T(8,128)}) fusion(bf16[512,384]{1,0:T(8,128)(2,1)S(1)} %bitcast.100, bf16[4096,384]{1,0:T(8,128)(2,1)S(1)} %copy-done, f32[4096]{0:T(1024)} %copy-done.6, f32[512,4096]{1,0:T(8,128)} %get-tuple-element.54, f32[4096]{0:T(1024)S(1)} %divide_bitcast_fusion), kind=kOutput, calls=%fused_computation.47 | convolution fusion | flops 1620114944 | bytes 12748800 | tf_op jit(solution)/shard_map/dot_general | solution.py:167
  186.6 4.0 %multiply_reduce_fusion.4 = f32[512]{0:T(512)S(1)} fusion(f32[512,4096]{1,0:T(8,128)} %get-tuple-element.54, f32[4096]{0:T(1024)S(1)} %divide_bitcast_fusion), kind=kLoop, calls=%fused_computation.12 | loop fusion | flops 4193792 | bytes 8407040 | tf_op jit(solution)/shard_map/reduce_sum | solution.py:169
  191.4 4.7 %all-to-all-start.9 = ((f32[16,12,128]{2,1,0:T(8,128)}), f32[16,12,128]{2,1,0:T(8,128)S(1)}, u32[]{:S(2)}, u32[]{:S(2)}) async-start(f32[16,12,128]{2,1,0:T(8,128)} %broadcast_in_dim.42), calls=%async_computation.9 | async-start | bytes 262144 | tf_op jit(solution)/shard_map/all_to_all | solution.py:32
  196.1 7.4 %all-to-all-done.9 = f32[16,12,128]{2,1,0:T(8,128)S(1)} async-done(((f32[16,12,128]{2,1,0:T(8,128)}), f32[16,12,128]{2,1,0:T(8,128)S(1)}, u32[]{:S(2)}, u32[]{:S(2)}) %all-to-all-start.9) | async-done | bytes 98336 | tf_op jit(solution)/shard_map/all_to_all | solution.py:32
  204.1 2.3 subtract_convert_fusion.2
  206.5 4.0 %all-to-all-start.10 = ((bf16[16,32,384]{2,1,0:T(8,128)(2,1)}), bf16[16,32,384]{2,1,0:T(8,128)(2,1)S(1)}, u32[]{:S(2)}, u32[]{:S(2)}) async-start(bf16[16,32,384]{2,1,0:T(8,128)(2,1)} %bitcast.98), calls=%async_computation.10 | async-start | bytes 786432 | tf_op jit(solution)/shard_map/all_to_all | solution.py:32
  210.5 7.6 %convolution_convert_fusion = bf16[4096,384]{1,0:T(8,128)(2,1)S(1)} fusion(bf16[512,384]{1,0:T(8,128)(2,1)} %bitcast.101, bf16[512,4096]{1,0:T(8,128)(2,1)} %copy-done.23, f32[512,4096]{1,0:T(8,128)} %get-tuple-element.54, f32[512]{0:T(512)} %copy-done.16, f32[512]{0:T(512)} %copy-done.15, f32[4096]{0:T(1024)S(1)} %divide_bitcast_fusion), kind=kOutput, calls=%fused_computation.15 | convolution fusion | flops 1624768512 | bytes 16142336 | tf_op jit(solution)/shard_map/dot_general | solution.py:23
  218.1 1.5 constant_dynamic-slice_fusion.1
  219.7 1.3 copy.88
  221.0 1.4 collective-permute-start.1
  222.5 1.0 multiply_reduce_fusion.7
  223.4 0.9 multiply_reduce_fusion.6
  224.4 0.8 broadcast_in_dim.43
  225.2 7.8 %all-to-all-start.11 = ((bf16[16,35,384]{2,1,0:T(8,128)(2,1)}), bf16[16,35,384]{2,1,0:T(8,128)(2,1)}, u32[]{:S(2)}, u32[]{:S(2)}) async-start(bf16[16,35,384]{2,1,0:T(8,128)(2,1)} %broadcast_in_dim.43), calls=%async_computation.11 | async-start | bytes 983040 | tf_op jit(solution)/shard_map/all_to_all | solution.py:32
  233.2 13.8 %all-to-all-done.11 = bf16[16,35,384]{2,1,0:T(8,128)(2,1)} async-done(((bf16[16,35,384]{2,1,0:T(8,128)(2,1)}), bf16[16,35,384]{2,1,0:T(8,128)(2,1)}, u32[]{:S(2)}, u32[]{:S(2)}) %all-to-all-start.11) | async-done | bytes 430112 | tf_op jit(solution)/shard_map/all_to_all | solution.py:32
  247.0 0.9 slice.73
  247.9 2.3 fusion.9
  250.2 1.1 copy-done.1
  251.4 1.0 dynamic-slice_bitcast_fusion.2
  252.4 2.7 collective-permute-start.4
  256.3 1.0 slice.72
  257.6 1.1 broadcast_in_dim.44
  258.7 9.5 %all-to-all-start.12 = ((bf16[16,96,384]{2,1,0:T(8,128)(2,1)}), bf16[16,96,384]{2,1,0:T(8,128)(2,1)}, u32[]{:S(2)}, u32[]{:S(2)}) async-start(bf16[16,96,384]{2,1,0:T(8,128)(2,1)} %broadcast_in_dim.44), calls=%async_computation.12 | async-start | bytes 2359296 | tf_op jit(solution)/shard_map/all_to_all | solution.py:32
  268.3 10.6 %collective-permute-done.2 = bf16[2,256,384]{2,1,0:T(8,128)(2,1)} collective-permute-done((bf16[2,256,384]{2,1,0:T(8,128)(2,1)}, bf16[2,256,384]{2,1,0:T(8,128)(2,1)}, u32[]{:S(2)}, u32[]{:S(2)}) %collective-permute-start.2) | collective-permute-done | bytes 393248 | tf_op jit(solution)/shard_map/ppermute | solution.py:99
  278.9 1.6 fusion.19
  280.5 6.6 %collective-permute-start.5 = (bf16[256,384]{1,0:T(8,128)(2,1)S(1)}, bf16[256,384]{1,0:T(8,128)(2,1)S(1)}, u32[]{:S(2)}, u32[]{:S(2)}) collective-permute-start(bf16[256,384]{1,0:T(8,128)(2,1)S(1)} %dynamic-slice_bitcast_fusion.3), channel_id=1, source_target_pairs={{0,128},{16,144},{32,160},{48,176},{64,192},{80,208},{96,224},{112... | collective-permute-start | bytes 589832 | tf_op jit(solution)/shard_map/ppermute | solution.py:50
  287.1 4.5 %collective-permute-done.5 = bf16[256,384]{1,0:T(8,128)(2,1)S(1)} collective-permute-done((bf16[256,384]{1,0:T(8,128)(2,1)S(1)}, bf16[256,384]{1,0:T(8,128)(2,1)S(1)}, u32[]{:S(2)}, u32[]{:S(2)}) %collective-permute-start.5) | collective-permute-done | bytes 196640 | tf_op jit(solution)/shard_map/ppermute | solution.py:50
  291.8 0.9 fusion.28
  292.7 2.1 convert_reduce_fusion
  (128 shorter events, 15.6 us)
Async XLA Ops:
  0.6 8.6 %collective-permute-start = (bf16[512,96]{0,1:T(8,128)(2,1)}, bf16[512,96]{0,1:T(8,128)(2,1)S(1)}, u32[]{:S(2)}, u32[]{:S(2)}) collective-permute-start(bf16[512,96]{0,1:T(8,128)(2,1)} %param.9), channel_id=1, source_target_pairs={{0,128},{16,144},{32,160},{48,176},{64,192},{80,208},{96,224},{112... | collective-permute-start | bytes 294920 | tf_op jit(solution)/shard_map/ppermute | solution.py:50
  5.1 0.8 copy-start.22
  5.8 0.5 copy-start.19
  8.0 1.3 copy-start.10
  8.0 37.4 %copy-start = (bf16[4096,384]{1,0:T(8,128)(2,1)S(1)}, bf16[4096,384]{1,0:T(8,128)(2,1)}, u32[]{:S(2)}) copy-start(bf16[4096,384]{1,0:T(8,128)(2,1)} %param.14) | copy-start | bytes 9437188
  9.3 0.6 copy-start.5
  14.8 20.8 %all-to-all-start = ((bf16[16,36,384]{2,1,0:T(8,128)(2,1)}), bf16[16,36,384]{2,1,0:T(8,128)(2,1)}, u32[]{:S(2)}, u32[]{:S(2)}) async-start(bf16[16,36,384]{2,1,0:T(8,128)(2,1)} %fusion.22), calls=%async_computation | async-start | bytes 983040 | tf_op jit(solution)/shard_map/all_to_all | solution.py:32
  38.0 16.7 %all-to-all-start.1 = ((bf16[16,32,384]{2,1,0:T(8,128)(2,1)}), bf16[16,32,384]{2,1,0:T(8,128)(2,1)S(1)}, u32[]{:S(2)}, u32[]{:S(2)}) async-start(bf16[16,32,384]{2,1,0:T(8,128)(2,1)} %broadcast_in_dim.31), calls=%async_computation.1 | async-start | bytes 786432 | tf_op jit(solution)/shard_map/all_to_all | solution.py:32
  46.1 15.9 %copy-start.6 = (f32[4096]{0:T(1024)}, f32[4096]{0:T(1024)S(1)}, u32[]{:S(2)}) copy-start(f32[4096]{0:T(1024)S(1)} %add_rsqrt_fusion) | copy-start | bytes 49156
  95.8 16.2 %all-to-all-start.4 = ((bf16[16,36,384]{2,1,0:T(8,128)(2,1)}), bf16[16,36,384]{2,1,0:T(8,128)(2,1)}, u32[]{:S(2)}, u32[]{:S(2)}) async-start(bf16[16,36,384]{2,1,0:T(8,128)(2,1)} %fusion.23), calls=%async_computation.4 | async-start | bytes 983040 | tf_op jit(solution)/shard_map/all_to_all | solution.py:32
  113.1 20.4 %copy-start.3 = (f32[36,384]{1,0:T(8,128)}, f32[36,384]{1,0:T(8,128)S(1)}, u32[]{:S(2)}) copy-start(f32[36,384]{1,0:T(8,128)S(1)} %convert_reduce_fusion.1) | copy-start | bytes 165892
  113.2 0.6 copy-start.8
  113.3 0.5 copy-start.11
  113.3 0.6 copy-start.13
  113.5 0.6 copy-start.17
  146.1 12.8 %all-to-all-start.7 = ((bf16[16,32,384]{2,1,0:T(8,128)(2,1)}), bf16[16,32,384]{2,1,0:T(8,128)(2,1)S(1)}, u32[]{:S(2)}, u32[]{:S(2)}) async-start(bf16[16,32,384]{2,1,0:T(8,128)(2,1)} %broadcast_in_dim.39), calls=%async_computation.7 | async-start | bytes 786432 | tf_op jit(solution)/shard_map/all_to_all | solution.py:32
  158.9 21.1 %copy-start.2 = (bf16[16,32,384]{2,1,0:T(8,128)(2,1)}, bf16[16,32,384]{2,1,0:T(8,128)(2,1)S(1)}, u32[]{:S(2)}) copy-start(bf16[16,32,384]{2,1,0:T(8,128)(2,1)S(1)} %all-to-all-done.7) | copy-start | bytes 1179652
  159.7 18.0 %all-to-all-start.8 = ((f32[16,32,128]{2,1,0:T(8,128)}), f32[16,32,128]{2,1,0:T(8,128)}, u32[]{:S(2)}, u32[]{:S(2)}) async-start(f32[16,32,128]{2,1,0:T(8,128)} %broadcast_in_dim.40), calls=%async_computation.8 | async-start | bytes 524288 | tf_op jit(solution)/shard_map/all_to_all | solution.py:32
  167.9 6.4 %copy-start.7 = (f32[4096]{0:T(1024)S(1)}, f32[4096]{0:T(1024)}, u32[]{:S(2)}) copy-start(f32[4096]{0:T(1024)} %copy-done.6) | copy-start | bytes 49156
  172.3 2.0 copy-start.23
  186.6 4.0 %copy-start.21 = (f32[512]{0:T(512)S(1)}, f32[512]{0:T(512)}, u32[]{:S(2)}) copy-start(f32[512]{0:T(512)} %get-tuple-element.21) | copy-start | bytes 6148
  191.4 12.1 %all-to-all-start.9 = ((f32[16,12,128]{2,1,0:T(8,128)}), f32[16,12,128]{2,1,0:T(8,128)S(1)}, u32[]{:S(2)}, u32[]{:S(2)}) async-start(f32[16,12,128]{2,1,0:T(8,128)} %broadcast_in_dim.42), calls=%async_computation.9 | async-start | bytes 262144 | tf_op jit(solution)/shard_map/all_to_all | solution.py:32
  204.1 2.3 copy-start.15
  204.1 2.3 copy-start.16
  206.5 15.9 %all-to-all-start.10 = ((bf16[16,32,384]{2,1,0:T(8,128)(2,1)}), bf16[16,32,384]{2,1,0:T(8,128)(2,1)S(1)}, u32[]{:S(2)}, u32[]{:S(2)}) async-start(bf16[16,32,384]{2,1,0:T(8,128)(2,1)} %bitcast.98), calls=%async_computation.10 | async-start | bytes 786432 | tf_op jit(solution)/shard_map/all_to_all | solution.py:32
  218.1 4.3 %copy-start.9 = (f32[384]{0:T(512)S(1)}, f32[384]{0:T(512)}, u32[]{:S(2)}) copy-start(f32[384]{0:T(512)} %copy-done.8) | copy-start | bytes 4612
  218.1 4.3 %copy-start.12 = (f32[32]{0:T(128)S(1)}, f32[32]{0:T(128)}, u32[]{:S(2)}) copy-start(f32[32]{0:T(128)} %copy-done.11) | copy-start | bytes 388
  218.1 4.3 %copy-start.14 = (f32[32]{0:T(128)S(1)}, f32[32]{0:T(128)}, u32[]{:S(2)}) copy-start(f32[32]{0:T(128)} %copy-done.13) | copy-start | bytes 388
  218.1 4.3 %copy-start.18 = (f32[32]{0:T(128)S(1)}, f32[32]{0:T(128)}, u32[]{:S(2)}) copy-start(f32[32]{0:T(128)} %copy-done.17) | copy-start | bytes 388
  221.0 27.0 %collective-permute-start.1 = (bf16[2,4,256,384]{3,2,0,1:T(8,128)(2,1)}, bf16[2,4,256,384]{3,2,0,1:T(8,128)(2,1)}, u32[]{:S(2)}, u32[]{:S(2)}) collective-permute-start(bf16[2,4,256,384]{3,2,0,1:T(8,128)(2,1)} %bitcast.93), channel_id=1, source_target_pairs={{0,16},{16,0},{32,48},{48,32},{64,80},{80,64},{96,112},{112,96},{1... | collective-permute-start | bytes 4718600 | tf_op jit(solution)/shard_map/ppermute | solution.py:50
  225.2 21.8 %all-to-all-start.11 = ((bf16[16,35,384]{2,1,0:T(8,128)(2,1)}), bf16[16,35,384]{2,1,0:T(8,128)(2,1)}, u32[]{:S(2)}, u32[]{:S(2)}) async-start(bf16[16,35,384]{2,1,0:T(8,128)(2,1)} %broadcast_in_dim.43), calls=%async_computation.11 | async-start | bytes 983040 | tf_op jit(solution)/shard_map/all_to_all | solution.py:32
  233.1 24.2 %copy-start.4 = (bf16[512,96]{0,1:T(8,128)(2,1)S(1)}, bf16[512,96]{0,1:T(8,128)(2,1)}, u32[]{:S(2)}) copy-start(bf16[512,96]{0,1:T(8,128)(2,1)} %param.8) | copy-start | bytes 294916
  233.1 24.2 %copy-start.20 = (f32[96]{0:T(128)S(1)}, f32[96]{0:T(128)}, u32[]{:S(2)}) copy-start(f32[96]{0:T(128)} %copy-done.19) | copy-start | bytes 1156
  250.2 1.2 copy-start.1
  252.4 15.9 %collective-permute-start.4 = (bf16[2,256,384]{2,1,0:T(8,128)(2,1)}, bf16[2,256,384]{2,1,0:T(8,128)(2,1)}, u32[]{:S(2)}, u32[]{:S(2)}) collective-permute-start(bf16[2,256,384]{2,1,0:T(8,128)(2,1)} %get-tuple-element.35), channel_id=1, source_target_pairs={{0,96},{16,112},{32,0},{48,16},{64,32},{80,48},{96,64},{112,80},{1... | collective-permute-start | bytes 1179656 | tf_op jit(solution)/shard_map/ppermute | solution.py:99
  255.1 13.2 %collective-permute-start.3 = (bf16[2,256,384]{2,1,0:T(8,128)(2,1)}, bf16[2,256,384]{2,1,0:T(8,128)(2,1)}, u32[]{:S(2)}, u32[]{:S(2)}) collective-permute-start(bf16[2,256,384]{2,1,0:T(8,128)(2,1)} %get-tuple-element.36), channel_id=1, source_target_pairs={{0,64},{16,80},{32,96},{48,112},{64,0},{80,16},{96,32},{112,48},{1... | collective-permute-start | bytes 1179656 | tf_op jit(solution)/shard_map/ppermute | solution.py:99
  255.7 23.2 %collective-permute-start.2 = (bf16[2,256,384]{2,1,0:T(8,128)(2,1)}, bf16[2,256,384]{2,1,0:T(8,128)(2,1)}, u32[]{:S(2)}, u32[]{:S(2)}) collective-permute-start(bf16[2,256,384]{2,1,0:T(8,128)(2,1)} %get-tuple-element.34), channel_id=1, source_target_pairs={{0,32},{16,48},{32,64},{48,80},{64,96},{80,112},{96,0},{112,16},{1... | collective-permute-start | bytes 1179656 | tf_op jit(solution)/shard_map/ppermute | solution.py:99
  258.7 34.0 %all-to-all-start.12 = ((bf16[16,96,384]{2,1,0:T(8,128)(2,1)}), bf16[16,96,384]{2,1,0:T(8,128)(2,1)}, u32[]{:S(2)}, u32[]{:S(2)}) async-start(bf16[16,96,384]{2,1,0:T(8,128)(2,1)} %broadcast_in_dim.44), calls=%async_computation.12 | async-start | bytes 2359296 | tf_op jit(solution)/shard_map/all_to_all | solution.py:32
  280.5 11.1 %collective-permute-start.5 = (bf16[256,384]{1,0:T(8,128)(2,1)S(1)}, bf16[256,384]{1,0:T(8,128)(2,1)S(1)}, u32[]{:S(2)}, u32[]{:S(2)}) collective-permute-start(bf16[256,384]{1,0:T(8,128)(2,1)S(1)} %dynamic-slice_bitcast_fusion.3), channel_id=1, source_target_pairs={{0,128},{16,144},{32,160},{48,176},{64,192},{80,208},{96,224},{112... | collective-permute-start | bytes 589832 | tf_op jit(solution)/shard_map/ppermute | solution.py:50

commit v3 on v2

v3 whole, which is shorter than its diff:
```python
import jax
import jax.numpy as jnp
from jax import lax
from jax.experimental import pallas as pl
from jax.experimental.pallas import tpu as pltpu
from jax.sharding import PartitionSpec as P

D = 1536
ITERS = 3


EPSILON = 1e-06
TEACHER_TEMP = 0.07
STUDENT_TEMP = 0.1
MOMENTUM = 0.994
BF16 = jnp.bfloat16
F32 = jnp.float32
LOG2E = 1.4426950408889634
BLOCK = 1024
LANES = 128


def contract_last(left, right):
    return lax.dot_general(left, right, (((1,), (1,)), ((), ())), preferred_element_type=F32)


def contract_first(left, right):
    return lax.dot_general(left, right, (((0,), (0,)), ((), ())), preferred_element_type=F32)


def unit_rows(values):
    factor = lax.rsqrt(jnp.sum(values * values, axis=1, keepdims=True) + EPSILON)
    return (values * factor, factor)


def exchanged(blocks, axis):
    return lax.all_to_all(blocks, axis, 0, 0)


def from_all(value, axis):
    count = lax.axis_size(axis)
    return exchanged(jnp.broadcast_to(value[None], (count,) + value.shape), axis)


def three_terms(value):
    high = value.astype(BF16)
    rest = value - high.astype(F32)
    middle = rest.astype(BF16)
    low = (rest - middle.astype(F32)).astype(BF16)
    return high, middle, low


def swapped(value, axis, bit):
    count = lax.axis_size(axis)
    return lax.ppermute(value, axis, [(one, one ^ bit) for one in range(count)])


def partial_hidden(features, gain, weight):
    scaled = (gain[:, None] * weight.astype(BF16).astype(F32)).astype(BF16)
    share = jnp.dot(features, scaled, preferred_element_type=F32)
    column = jnp.sum(scaled.astype(F32), axis=0)
    values = features.astype(F32)
    return share, column, jnp.sum(values, axis=1), jnp.sum(values * values, axis=1)


def center_and_scale(first, second):
    center = first / D
    return center, lax.rsqrt(second / D - center * center + EPSILON)


def packed_shares(features, gain, weight, parts):
    crops, size = features.shape[0], weight.shape[1]
    own = crops // parts
    share, column, first, second = partial_hidden(features, gain, weight)
    sums = jnp.stack(three_terms(jnp.stack([first, second])))
    sums = sums.reshape(6, parts, own).transpose(1, 0, 2).reshape(parts, 1, 6 * own)
    sums = jnp.pad(sums, ((0, 0), (0, 0), (0, size - 6 * own)))
    columns = jnp.broadcast_to(jnp.stack(three_terms(column))[None], (parts, 3, size))
    return jnp.concatenate([share.astype(BF16).reshape(parts, own, size), columns, sums], 1)


def summed_hidden(packed):
    own = packed.shape[1] - 4
    packed = jnp.sum(packed.astype(F32), axis=0)
    sums = jnp.sum(packed[own + 3, : 6 * own].reshape(3, 2, own), axis=0)
    center, scale = center_and_scale(sums[0][:, None], sums[1][:, None])
    column = jnp.sum(packed[own : own + 3], axis=0)[None]
    return scale * (packed[:own] - center * column)


def column_form(rows):
    return jnp.concatenate(
        [jnp.transpose(jnp.broadcast_to(rows[q : q + 1], (LANES, LANES))) for q in range(rows.shape[0])], 0
    )


def row_form(partial):
    return jnp.concatenate(
        [
            jnp.sum(jnp.transpose(partial[q * LANES : (q + 1) * LANES]), axis=0, keepdims=True)
            for q in range(partial.shape[0] // LANES)
        ],
        0,
    )


def stack_sum(ref):
    total = ref[0].astype(F32)
    for one in range(1, ref.shape[0]):
        total = total + ref[one].astype(F32)
    return total


def energy_kernel(pick_ref, teacher_ref, protos_ref, energy_ref, sums_ref, paired, held):
    step = pl.program_id(0)

    @pl.when(step == 0)
    def _():
        paired[...] = jnp.dot(pick_ref[...], teacher_ref[...], preferred_element_type=F32).astype(BF16)

    rows = []
    for part in range(BLOCK // 256):
        cut = slice(part * 256, part * 256 + 256)
        value = jnp.exp2(contract_last(paired[...], protos_ref[cut, :]) * (LOG2E / TEACHER_TEMP))
        energy_ref[:, cut] = value.astype(BF16)
        total = jnp.sum(value, axis=0, keepdims=True)
        rows += [total[:, :LANES], total[:, LANES:]]
    held[pl.ds(pl.multiple_of(step * 8, 8), 8), :] = jnp.concatenate(rows, 0)

    @pl.when(step == pl.num_programs(0) - 1)
    def _():
        for one in range(sums_ref.shape[0]):
            sums_ref[one] = held[...].astype(BF16)


def row_kernel(got_ref, energy_ref, sums_ref, scale, held):
    step = pl.program_id(0)

    @pl.when(step == 0)
    def _():
        scale[...] = 1.0 / stack_sum(got_ref)
        held[...] = jnp.zeros_like(held)

    start = step * 8
    for low in range(0, held.shape[0], LANES):
        cut = slice(low, low + LANES)
        total = held[cut, :]
        for tile in range(8):
            total = total + energy_ref[cut, tile * LANES : (tile + 1) * LANES].astype(F32) * scale[pl.ds(start + tile, 1), :]
        held[cut, :] = total

    @pl.when(step == pl.num_programs(0) - 1)
    def _():
        total = row_form(held[...])
        for one in range(sums_ref.shape[0]):
            sums_ref[one] = total


def col_kernel(got_ref, energy_ref, sums_ref, scale, held):
    step = pl.program_id(0)

    @pl.when(step == 0)
    def _():
        scale[...] = column_form(1.0 / stack_sum(got_ref))

    rows = []
    for tile in range(8):
        value = energy_ref[:, tile * LANES : (tile + 1) * LANES].astype(F32) * scale[...]
        rows.append(jnp.sum(value, axis=0, keepdims=True))
    held[pl.ds(pl.multiple_of(step * 8, 8), 8), :] = jnp.concatenate(rows, 0)

    @pl.when(step == pl.num_programs(0) - 1)
    def _():
        for one in range(sums_ref.shape[0]):
            sums_ref[one] = held[...].astype(BF16)


def student_kernel(student_ref, protos_ref, exponent_ref, pulled_ref, partition_ref, held):
    step = pl.program_id(0)

    @pl.when(step == 0)
    def _():
        held[...] = jnp.zeros_like(held)
        pulled_ref[...] = jnp.zeros_like(pulled_ref)

    for part in range(BLOCK // 256):
        cut = slice(part * 256, part * 256 + 256)
        value = jnp.exp2(contract_last(student_ref[...], protos_ref[cut, :]) * (LOG2E / STUDENT_TEMP))
        held[...] += value[:, :LANES] + value[:, LANES:]
        value = value.astype(BF16)
        exponent_ref[:, cut] = value
        pulled_ref[...] += jnp.dot(value, protos_ref[cut, :], preferred_element_type=F32)

    @pl.when(step == pl.num_programs(0) - 1)
    def _():
        partition_ref[...] = row_form(held[...])


def last_kernel(got_ref, partition_ref, energy_ref, student_ref, protos_ref, sums_ref, coded_ref, scale_ref, held):
    step = pl.program_id(0)

    @pl.when(step == 0)
    def _():
        scale_ref[...] = 1.0 / stack_sum(got_ref)
        held[...] = jnp.zeros_like(held)
        coded_ref[...] = jnp.zeros_like(coded_ref)

    start = step * 8
    for part in range(BLOCK // 256):
        left = energy_ref[:, part * 256 : part * 256 + LANES].astype(F32) * scale_ref[pl.ds(start + 2 * part, 1), :]
        right = energy_ref[:, part * 256 + LANES : part * 256 + 256].astype(F32) * scale_ref[pl.ds(start + 2 * part + 1, 1), :]
        held[...] += left + right
        value = jnp.concatenate([left.astype(BF16), right.astype(BF16)], 1)
        coded_ref[...] += jnp.dot(value, protos_ref[part * 256 : part * 256 + 256, :], preferred_element_type=F32)

    @pl.when(step == pl.num_programs(0) - 1)
    def _():
        value = student_ref[...].astype(F32) * coded_ref[...]
        expected = value[:, :LANES]
        for tile in range(1, value.shape[1] // LANES):
            expected = expected + value[:, tile * LANES : (tile + 1) * LANES]
        total = jnp.concatenate(
            [row_form(held[...]), partition_ref[...], row_form(expected) * (1.0 / STUDENT_TEMP)], 0
        )
        for one in range(sums_ref.shape[0]):
            sums_ref[one] = total


def unit_grad_kernel(got_ref, pulled_ref, coded_ref, grad_ref, loss_ref, wanted_ref, given_ref):
    total = stack_sum(got_ref)
    count = total.shape[0] // 3
    row = 1.0 / total[:count]
    partition = total[count : 2 * count]
    loss_ref[...] = jnp.log(partition) - total[2 * count :] * row
    wanted = column_form(1.0 / (partition * STUDENT_TEMP))
    given = column_form(row * (1.0 / STUDENT_TEMP))
    wanted_ref[...] = wanted
    given_ref[...] = given
    for tile in range(pulled_ref.shape[1] // LANES):
        cut = slice(tile * LANES, (tile + 1) * LANES)
        grad_ref[:, cut] = (pulled_ref[:, cut] * wanted - coded_ref[:, cut] * given).astype(BF16)


def proto_grad_kernel(core_ref, turned_ref, wanted_ref, given_ref, scale_ref, exponent_ref, energy_ref, keep_ref, give_ref):
    step = pl.program_id(0)
    core = core_ref[0]
    for out_ref, which in ((give_ref, 1 - core), (keep_ref, core)):
        parts = []
        for half in range(2):
            cut = pl.ds(pl.multiple_of(which * 256 + half * LANES, LANES), LANES)
            scale = scale_ref[pl.ds(step * 4 + which * 2 + half, 1), :]
            score = exponent_ref[:, cut].astype(F32) * wanted_ref[...] - energy_ref[:, cut].astype(F32) * scale * given_ref[...]
            parts.append(score.astype(BF16))
        out_ref[0] = jnp.dot(turned_ref[...], jnp.concatenate(parts, 1), preferred_element_type=F32).astype(BF16)


def whole(shape):
    return pl.BlockSpec(shape, lambda step: (0,) * len(shape))


def called(kernel, steps, ins, outs, scratch, flops=0, moved=0, exps=0):
    return pl.pallas_call(
        kernel,
        grid=(steps,),
        in_specs=ins,
        out_specs=[spec for _, spec in outs],
        out_shape=[shape for shape, _ in outs],
        scratch_shapes=scratch,
        compiler_params=pltpu.CompilerParams(
            dimension_semantics=("arbitrary",), vmem_limit_bytes=24 * 1024 * 1024
        ),
        cost_estimate=pl.CostEstimate(flops=flops, bytes_accessed=moved, transcendentals=exps),
    )


def array(shape, dtype):
    return jax.ShapeDtypeStruct(shape, dtype)


def make_calls(crops, protos, size, dps, parts):
    steps = protos // BLOCK
    lines, tiles = crops // LANES, protos // LANES
    across = pl.BlockSpec((crops, BLOCK), lambda step: (0, step))
    down = pl.BlockSpec((BLOCK, size), lambda step: (step, 0))
    matrix = crops * protos
    product = 2 * matrix * size
    col_sent = (array((dps, tiles, LANES), BF16), whole((dps, tiles, LANES)))
    row_sent = (array((parts, lines, LANES), F32), whole((parts, lines, LANES)))
    tall = pltpu.VMEM((crops, LANES), F32)
    short = pltpu.VMEM((tiles, LANES), F32)
    energy = called(
        energy_kernel, steps, [whole((crops, crops)), whole((crops, size)), down],
        [(array((crops, protos), BF16), across), col_sent],
        [pltpu.VMEM((crops, size), BF16), short], product, 2 * matrix, matrix,
    )
    rows = called(
        row_kernel, steps, [whole((dps, tiles, LANES)), across], [row_sent], [short, tall], 2 * matrix, 2 * matrix
    )
    cols = called(
        col_kernel, steps, [whole((parts, lines, LANES)), across], [col_sent], [tall, short], 2 * matrix, 2 * matrix
    )
    student = called(
        student_kernel, steps, [whole((crops, size)), down],
        [
            (array((crops, protos), BF16), across),
            (array((crops, size), F32), whole((crops, size))),
            (array((lines, LANES), F32), whole((lines, LANES))),
        ],
        [tall], 2 * product, 2 * matrix, matrix,
    )
    last = called(
        last_kernel, steps,
        [whole((dps, tiles, LANES)), whole((lines, LANES)), across, whole((crops, size)), down],
        [
            (array((parts, 3 * lines, LANES), F32), whole((parts, 3 * lines, LANES))),
            (array((crops, size), F32), whole((crops, size))),
            (array((tiles, LANES), F32), whole((tiles, LANES))),
        ],
        [tall], product, 2 * matrix,
    )
    unit_grad = called(
        unit_grad_kernel, 1,
        [whole((parts, 3 * lines, LANES)), whole((crops, size)), whole((crops, size))],
        [
            (array((crops, size), BF16), whole((crops, size))),
            (array((lines, LANES), F32), whole((lines, LANES))),
            (array((crops, LANES), F32), whole((crops, LANES))),
            (array((crops, LANES), F32), whole((crops, LANES))),
        ],
        [], 4 * crops * size, 10 * crops * size,
    )
    wide = protos // dps
    pair = pl.BlockSpec((crops, 2 * wide), lambda step: (0, step))
    block = (array((dps // 2, size, wide), BF16), pl.BlockSpec((1, size, wide), lambda step: (step, 0, 0)))
    proto_grad = called(
        proto_grad_kernel, dps // 2,
        [
            pl.BlockSpec(memory_space=pltpu.SMEM), whole((size, crops)), whole((crops, LANES)),
            whole((crops, LANES)), whole((tiles, LANES)), pair, pair,
        ],
        [block, block], [], product, 4 * matrix + 2 * protos * size,
    )
    return energy, rows, cols, student, last, unit_grad, proto_grad


def summed_protos(keep, give):
    me = lax.axis_index("dp")
    along_y, along_x = (me // 2) % 4, me // 8
    blocks = (keep.astype(F32) + swapped(give, "dp", 1).astype(F32)).astype(BF16)
    blocks = yield blocks.reshape((2, 4) + keep.shape[1:])
    total = lax.dynamic_index_in_dim(blocks, along_y, 1, False).astype(F32)
    for step in range(1, 4):
        give = lax.dynamic_index_in_dim(blocks, (along_y + step) % 4, 1, False)
        pairs = [(one, (one & 9) | ((one + 2 * step) & 6)) for one in range(16)]
        total = total + lax.ppermute(give, "dp", pairs).astype(F32)
    blocks = yield total.astype(BF16)
    keep = lax.dynamic_index_in_dim(blocks, along_x, 0, False)
    give = lax.dynamic_index_in_dim(blocks, 1 - along_x, 0, False)
    yield keep.astype(F32) + swapped(give, "dp", 8).astype(F32)


def body(
    student_cls,
    teacher_cls,
    student_gain,
    teacher_gain,
    student_proj,
    teacher_proj,
    prototypes,
    partner,
):
    crops, width = student_cls.shape
    parts = lax.axis_size("proto")
    own = crops // parts
    size = student_proj.shape[1]
    start = lax.axis_index("proto") * width
    opposite = swapped(teacher_cls, "dp", 8)
    gain_s = lax.dynamic_slice_in_dim(student_gain, start, width)
    gain_t = lax.dynamic_slice_in_dim(teacher_gain, start, width)

    weight = (gain_s[:, None] * student_proj.astype(F32)).astype(BF16)
    gathered = lax.all_gather(jnp.concatenate([student_cls.T, weight], 1), "proto", axis=0, tiled=True)
    teacher_blocks = packed_shares(opposite, gain_t, teacher_proj, parts)
    teacher_hidden = summed_hidden(exchanged(teacher_blocks, "proto"))
    teacher_unit = unit_rows(teacher_hidden)[0].astype(BF16)
    teacher_all = from_all(teacher_unit, "proto").reshape(crops, size)
    pick = (partner[:, None] % crops == jnp.arange(crops, dtype=jnp.int32)[None]).astype(BF16)
    proto_unit32, proto_factor = unit_rows(prototypes.astype(F32))
    proto_unit = proto_unit32.astype(BF16)
    protos = proto_unit.shape[0]
    energy_call, row_call, col_call, student_call, last_call, unit_grad_call, proto_grad_call = make_calls(
        crops, protos, size, lax.axis_size("dp"), parts
    )
    energy, sums = energy_call(pick, teacher_all, proto_unit)
    for step in range(ITERS - 1):
        (sums,) = row_call(exchanged(sums, "dp"), energy)
        (sums,) = col_call(exchanged(sums, "proto"), energy)

    sums, gathered = lax.optimization_barrier((sums, gathered))
    values = gathered[:, :crops].astype(F32)
    student_center, student_scale = center_and_scale(
        jnp.sum(values, axis=0)[:, None], jnp.sum(values * values, axis=0)[:, None]
    )
    weight = gathered[:, crops:]
    student_hidden = student_scale * (
        contract_first(gathered[:, :crops], weight) - student_center * jnp.sum(weight.astype(F32), axis=0)[None]
    )
    student_unit32, student_factor = unit_rows(student_hidden)
    student_unit = student_unit32.astype(BF16)
    exponent, pulled, partition = student_call(student_unit, proto_unit)
    sums = exchanged(sums, "dp")
    sums, exponent, pulled, partition = lax.optimization_barrier((sums, exponent, pulled, partition))
    sums, coded, scale = last_call(sums, partition, energy, student_unit, proto_unit)
    unit_grad, crop_loss, wanted, given = unit_grad_call(exchanged(sums, "proto"), pulled, coded)
    crop_loss = crop_loss.reshape(crops)
    unit_grad = exchanged(unit_grad.reshape(parts, own, size), "proto")
    core = (lax.axis_index("dp") % 2).reshape(1)
    keep, give = proto_grad_call(core, student_unit.T, wanted, given, scale, exponent, energy)
    stages = summed_protos(keep, give)
    blocks = next(stages)
    student_unit32, student_factor, student_center, student_scale = (
        lax.dynamic_slice_in_dim(value, lax.axis_index("proto") * own, own, 0)
        for value in (student_unit32, student_factor, student_center, student_scale)
    )
    unit_grad = jnp.sum(unit_grad.astype(F32), axis=0)
    hidden_grad = student_factor * (
        unit_grad - student_unit32 * jnp.sum(student_unit32 * unit_grad, axis=1, keepdims=True)
    )
    sent = (hidden_grad * student_scale).astype(BF16)
    moved = jnp.stack(three_terms(jnp.sum(student_center * sent.astype(F32), axis=0)))
    packed = jnp.concatenate([sent, moved], 0)
    packed, blocks = lax.optimization_barrier((packed, blocks))
    blocks = stages.send(blocks)
    packed = from_all(packed, "proto")
    moved = jnp.sum(packed[:, own:].astype(F32), axis=(0, 1))
    sent = packed[:, :own].reshape(crops, size)
    share = (gain_s[:, None] * (contract_first(student_cls, sent) - moved[None])).astype(BF16)
    share, blocks = lax.optimization_barrier((share, blocks))
    proto_unit_grad = stages.send(blocks).T
    grad_proj = jnp.sum(from_all(share, "dp").astype(F32), axis=0)

    count = protos // lax.axis_size("dp")
    own_start = lax.axis_index("dp") * count
    own_unit, own_factor = unit_rows(
        lax.dynamic_slice_in_dim(prototypes, own_start, count, 0).astype(F32)
    )
    grad_protos = own_factor * (
        proto_unit_grad - own_unit * jnp.sum(own_unit * proto_unit_grad, axis=1, keepdims=True)
    )
    teacher_next = MOMENTUM * teacher_proj + (1.0 - MOMENTUM) * student_proj.astype(F32)
    return (crop_loss, grad_proj, grad_protos, teacher_next)


def solution(mesh):
    placed = (
        P("dp", "proto"),
        P("dp", "proto"),
        P(),
        P(),
        P("proto", None),
        P("proto", None),
        P("proto", None),
        P("dp"),
    )
    return jax.shard_map(
        body,
        mesh=mesh,
        in_specs=placed,
        out_specs=(P("dp"), P("proto", None), P(("proto", "dp"), None), P("proto", None)),
        check_vma=False,
    )
```

time: 298 us -> 294 us (0.987)
  matrix products: 32.2 us -> 3.44 us
  Pallas kernels: 0 us -> 27.8 us
  waiting for transfers between devices: 61.4 us -> 85 us
  other arithmetic: 49.9 us -> 29.1 us
  blocking collectives: 56 us -> 41 us
  starting transfers between devices: 72 us -> 57.1 us
  between operations: 1.28 us -> 14.6 us
  local copies, waits for them, and re-layouts: 22.1 us -> 34.3 us
    pallas_call x0 -> x9, Pallas kernels: none -> 27.8 us  [the longest x1 6.78 us: body(): exponent, pulled, partition = student_call(student_unit, proto_unit)]
    dot_general x4 -> x0, matrix products: 21.7 us -> none  [the longest x2 11.7 us: contract_last(): lax.dot_general(left, right, (((1,), (1,)), ((), ())), preferred_element_...]
    reduce_sum x12 -> x3, other arithmetic: 25.8 us -> 4.35 us  [the longest x1 1.88 us: body(): jnp.sum(values * values, axis=0)[:, None]]
    all_to_all x4 -> x3, blocking collectives: 56 us -> 41 us  [exchanged(): return lax.all_to_all(blocks, axis, 0, 0)]
    unnamed x48 -> x51, local copies, waits for them, and re-layouts: 4.6 us -> 19.1 us
    ppermute x3, waiting for transfers between devices: 4.53 us -> 18.3 us  [swapped(): return lax.ppermute(value, axis, [(one, one ^ bit) for one in range(count)])]
    all_to_all x9 -> x8, starting transfers between devices: 56.5 us -> 44.4 us  [exchanged(): return lax.all_to_all(blocks, axis, 0, 0)]
    dot_general x2, matrix products: 7.83 us -> 2.1 us  [contract_first(): lax.dot_general(left, right, (((0,), (0,)), ((), ())), preferred_element_...]
  transfers between devices with their start and end apart: 15 -> 15, of which waited for: 8 -> 10; matrix products, arithmetic and copies ran while one was open for 17% -> 11% of each run, Pallas kernels for 0% -> 6%
where the time goes in v3:
time: 294 us; the launch traced here: 292 us
  waiting for transfers between devices  85 us (29%)
  starting transfers between devices  57.1 us (19%)
  blocking collectives  41 us (14%)
  local copies, waits for them, and re-layouts  34.3 us (12%)
  other arithmetic  29.1 us (10%)
  Pallas kernels  27.8 us (9%)
  between operations  14.6 us (5%)
  matrix products  3.44 us (1%)
    all_to_all x8, waiting for transfers between devices, exchanged(): return lax.all_to_all(blocks, axis, 0, 0)  50.5 us
    all_to_all x8, starting transfers between devices, exchanged(): return lax.all_to_all(blocks, axis, 0, 0)  44.4 us
    all_to_all x3, blocking collectives, exchanged(): return lax.all_to_all(blocks, axis, 0, 0)  41 us
    unnamed x51, local copies, waits for them, and re-layouts  19.1 us
    ppermute x3, waiting for transfers between devices, swapped(): return lax.ppermute(value, axis, [(one, one ^ bit) for one in range(count)])  18.3 us
    ppermute x3, waiting for transfers between devices, summed_protos(): total = total + lax.ppermute(give, 'dp', pairs).astype(F32)  16.2 us
    ppermute x3, starting transfers between devices, swapped(): return lax.ppermute(value, axis, [(one, one ^ bit) for one in range(count)])  8.46 us
    pallas_call x1, Pallas kernels, body(): exponent, pulled, partition = student_call(student_unit, proto_unit)  6.78 us
  transfers between devices with their start and end apart: 15, of which 10 were waited for; matrix products, arithmetic and copies ran while one was open for 11% of the time, Pallas kernels for 6%

profile of v3, /device:TPU:1, one launch (start us, length us, event | category | flops | bytes accessed | tf_op | source)
XLA Modules:
  0.0 292.3 jit_solution(13108144581170640308)
XLA Ops:
  7.2 0.9 dynamic_slice.38
  8.9 1.7 fusion.29
  10.6 1.6 pad_maximum_fusion
  12.2 3.7 %collective-permute-start = (bf16[512,96]{0,1:T(8,128)(2,1)}, bf16[512,96]{0,1:T(8,128)(2,1)S(1)}, u32[]{:S(2)}, u32[]{:S(2)}) collective-permute-start(bf16[512,96]{0,1:T(8,128)(2,1)} %param.9), channel_id=1, source_target_pairs={{0,128},{16,144},{32,160},{48,176},{64,192},{80,208},{96,224},{112... | collective-permute-start | bytes 294920 | tf_op jit(solution)/shard_map/ppermute | solution.py:55
  16.5 1.6 collective-permute-done
  19.1 1.3 fusion.3
  22.0 1.9 fusion.19
  23.9 9.5 %all-to-all-start = ((bf16[16,36,384]{2,1,0:T(8,128)(2,1)}), bf16[16,36,384]{2,1,0:T(8,128)(2,1)}, u32[]{:S(2)}, u32[]{:S(2)}) async-start(bf16[16,36,384]{2,1,0:T(8,128)(2,1)} %fusion.19), calls=%async_computation | async-start | bytes 983040 | tf_op jit(solution)/shard_map/all_to_all | solution.py:37
  34.8 0.9 fusion.9.pick_ref
  35.7 15.0 %all-to-all-done = bf16[16,36,384]{2,1,0:T(8,128)(2,1)} async-done(((bf16[16,36,384]{2,1,0:T(8,128)(2,1)}), bf16[16,36,384]{2,1,0:T(8,128)(2,1)}, u32[]{:S(2)}, u32[]{:S(2)}) %all-to-all-start) | async-done | bytes 442400 | tf_op jit(solution)/shard_map/all_to_all | solution.py:37
  50.7 1.1 convert_reduce_fusion.3
  53.1 5.6 %all-to-all-start.1 = ((bf16[16,32,384]{2,1,0:T(8,128)(2,1)}), bf16[16,32,384]{2,1,0:T(8,128)(2,1)S(1)}, u32[]{:S(2)}, u32[]{:S(2)}) async-start(bf16[16,32,384]{2,1,0:T(8,128)(2,1)} %broadcast_in_dim.9), calls=%async_computation.1 | async-start | bytes 786432 | tf_op jit(solution)/shard_map/all_to_all | solution.py:37
  58.7 2.3 fusion.1.protos_ref
  61.0 12.6 %all-to-all-done.1 = bf16[16,32,384]{2,1,0:T(8,128)(2,1)S(1)} async-done(((bf16[16,32,384]{2,1,0:T(8,128)(2,1)}), bf16[16,32,384]{2,1,0:T(8,128)(2,1)S(1)}, u32[]{:S(2)}, u32[]{:S(2)}) %all-to-all-start.1) | async-done | bytes 393248 | tf_op jit(solution)/shard_map/all_to_all | solution.py:37
  73.5 1.0 copy-done.10
  74.6 3.8 %shard_map.111 = (bf16[512,4096]{1,0:T(8,128)(2,1)S(1)}, bf16[16,32,128]{2,1,0:T(8,128)(2,1)S(1)}) custom-call(bf16[512,512]{1,0:T(8,128)(2,1)S(1)} %copy-done.10, bf16[512,384]{1,0:T(8,128)(2,1)S(1)} %bitcast.54, bf16[4096,384]{1,0:T(8,128)(2,1)S(1)} %fusion.1.protos_ref), custom_call_target="tpu_custom_call" | custom-call | flops 1610612736 | bytes 4194304 | tf_op jit(solution)/shard_map/pallas_call | solution.py:394
  78.4 18.7 %all_to_all.55.got_ref = bf16[16,32,128]{2,1,0:T(8,128)(2,1)S(1)} all-to-all(bf16[16,32,128]{2,1,0:T(8,128)(2,1)S(1)} %get-tuple-element.28), channel_id=1, replica_groups=mesh['dp'=16,'proto'=16] {'dp'}, dimensions={0} | all-to-all | bytes 262144 | tf_op jit(solution)/shard_map/all_to_all | solution.py:37
  97.0 1.4 shard_map.112
  98.4 10.0 %all_to_all.56.got_ref = f32[16,4,128]{2,1,0:T(4,128)S(1)} all-to-all(f32[16,4,128]{2,1,0:T(4,128)S(1)} %shard_map.112), channel_id=1, replica_groups=mesh['dp'=16,'proto'=16] {'proto'}, dimensions={0} | all-to-all | bytes 65536 | tf_op jit(solution)/shard_map/all_to_all | solution.py:37
  108.4 1.6 shard_map.113
  110.1 12.4 %all_to_all.57.got_ref = bf16[16,32,128]{2,1,0:T(8,128)(2,1)S(1)} all-to-all(bf16[16,32,128]{2,1,0:T(8,128)(2,1)S(1)} %shard_map.113), channel_id=1, replica_groups=mesh['dp'=16,'proto'=16] {'dp'}, dimensions={0} | all-to-all | bytes 262144 | tf_op jit(solution)/shard_map/all_to_all | solution.py:37
  122.4 2.0 shard_map.114
  124.4 3.5 %all-to-all-start.5 = ((f32[16,4,128]{2,1,0:T(4,128)}), f32[16,4,128]{2,1,0:T(4,128)S(1)}, u32[]{:S(2)}, u32[]{:S(2)}) async-start(f32[16,4,128]{2,1,0:T(4,128)} %shard_map.114), calls=%async_computation.5 | async-start | bytes 65536 | tf_op jit(solution)/shard_map/all_to_all | solution.py:37
  127.9 7.3 %all-to-all-done.5.got_ref = f32[16,4,128]{2,1,0:T(4,128)S(1)} async-done(((f32[16,4,128]{2,1,0:T(4,128)}), f32[16,4,128]{2,1,0:T(4,128)S(1)}, u32[]{:S(2)}, u32[]{:S(2)}) %all-to-all-start.5) | async-done | bytes 32800 | tf_op jit(solution)/shard_map/all_to_all | solution.py:37
  135.2 2.2 copy-done.1
  137.4 2.3 shard_map.115
  139.7 1.7 convert_reduce_fusion.2
  141.3 1.9 fusion.2
  143.2 1.9 multiply_reduce_fusion
  145.1 5.7 %all-to-all-start.6 = ((bf16[16,32,128]{2,1,0:T(8,128)(2,1)}), bf16[16,32,128]{2,1,0:T(8,128)(2,1)}, u32[]{:S(2)}, u32[]{:S(2)}) async-start(bf16[16,32,128]{2,1,0:T(8,128)(2,1)} %shard_map.115), calls=%async_computation.6 | async-start | bytes 262144 | tf_op jit(solution)/shard_map/all_to_all | solution.py:37
  150.9 2.4 fusion.38
  153.2 6.8 %shard_map.116 = (bf16[512,4096]{1,0:T(8,128)(2,1)S(1)}, f32[512,384]{1,0:T(8,128)S(1)}, f32[4,128]{1,0:T(4,128)S(1)}) custom-call(bf16[512,384]{1,0:T(8,128)(2,1)S(1)} %get-tuple-element.58.student_ref, bf16[4096,384]{1,0:T(8,128)(2,1)S(1)} %fusion.1.protos_ref), custom_call_target="tpu_custom_call" | custom-call | flops 3221225472 | bytes 4194304 | tf_op jit(solution)/shard_map/pallas_call | solution.py:410
  160.0 2.0 copy-done.4
  163.5 2.3 copy.54
  165.8 2.2 copy-done.2
  168.7 4.4 %shard_map.117 = (f32[16,12,128]{2,1,0:T(8,128)S(1)}, f32[512,384]{1,0:T(8,128)S(1)}, f32[32,128]{1,0:T(8,128)S(1)}) custom-call(bf16[16,32,128]{2,1,0:T(8,128)(2,1)} %all-to-all-done.6.got_ref, f32[4,128]{1,0:T(4,128)S(1)} %copy-done.13, bf16[512,4096]{1,0:T(8,128)(2,1)S(1)} %copy-done.2, bf16[512,384]{1,0:T(8,128)(2,1)S(1)} %get-tuple-element.58.student_ref, ...), custom_call_target="tpu_custom_call" | custom-call | flops 1610612736 | bytes 4194304 | tf_op jit(solution)/shard_map/pallas_call | solution.py:413
  174.6 3.5 %all-to-all-start.7 = ((f32[16,12,128]{2,1,0:T(8,128)}), f32[16,12,128]{2,1,0:T(8,128)S(1)}, u32[]{:S(2)}, u32[]{:S(2)}) async-start(f32[16,12,128]{2,1,0:T(8,128)} %copy-done.11), calls=%async_computation.7 | async-start | bytes 262144 | tf_op jit(solution)/shard_map/all_to_all | solution.py:37
  178.1 1.3 fusion.17.turned_ref
  179.4 6.0 %all-to-all-done.7.got_ref = f32[16,12,128]{2,1,0:T(8,128)S(1)} async-done(((f32[16,12,128]{2,1,0:T(8,128)}), f32[16,12,128]{2,1,0:T(8,128)S(1)}, u32[]{:S(2)}, u32[]{:S(2)}) %all-to-all-start.7) | async-done | bytes 98336 | tf_op jit(solution)/shard_map/all_to_all | solution.py:37
  185.5 1.1 copy-done.7
  186.6 1.1 copy-done.9
  187.8 1.0 shard_map.118
  188.8 2.2 copy-done.3
  191.0 2.2 copy-done.5
  193.1 4.6 %shard_map.119 = (bf16[8,384,256]{2,1,0:T(8,128)(2,1)S(1)}, bf16[8,384,256]{2,1,0:T(8,128)(2,1)S(1)}) custom-call(s32[1]{0:T(128)} %bitcast.11.core_ref, bf16[384,512]{1,0:T(8,128)(2,1)S(1)} %fusion.17.turned_ref, f32[512,128]{1,0:T(8,128)S(1)} %get-tuple-element.42.wanted_ref, f32[512,128]{1,0:T(8,128)S(1)} %get-tuple-element.43.given_ref, ...), custom_call_target="tpu_custom_call" | custom-call | flops 1610612736 | bytes 11534336 | tf_op jit(solution)/shard_map/pallas_call | solution.py:418
  197.7 1.8 collective-permute-start.1
  199.6 3.6 %all-to-all-start.8 = ((bf16[16,32,384]{2,1,0:T(8,128)(2,1)}), bf16[16,32,384]{2,1,0:T(8,128)(2,1)S(1)}, u32[]{:S(2)}, u32[]{:S(2)}) async-start(bf16[16,32,384]{2,1,0:T(8,128)(2,1)} %bitcast.10), calls=%async_computation.8 | async-start | bytes 786432 | tf_op jit(solution)/shard_map/all_to_all | solution.py:37
  205.4 9.6 %all-to-all-done.8 = bf16[16,32,384]{2,1,0:T(8,128)(2,1)S(1)} async-done(((bf16[16,32,384]{2,1,0:T(8,128)(2,1)}), bf16[16,32,384]{2,1,0:T(8,128)(2,1)S(1)}, u32[]{:S(2)}, u32[]{:S(2)}) %all-to-all-start.8) | async-done | bytes 393248 | tf_op jit(solution)/shard_map/all_to_all | solution.py:37
  215.1 0.9 multiply_reduce_fusion.2
  216.9 1.8 add_convert_fusion
  219.6 5.7 %all-to-all-start.9 = ((bf16[16,35,384]{2,1,0:T(8,128)(2,1)}), bf16[16,35,384]{2,1,0:T(8,128)(2,1)}, u32[]{:S(2)}, u32[]{:S(2)}) async-start(bf16[16,35,384]{2,1,0:T(8,128)(2,1)} %broadcast_in_dim.10), calls=%async_computation.9 | async-start | bytes 983040 | tf_op jit(solution)/shard_map/all_to_all | solution.py:37
  227.5 2.7 collective-permute-start.3
  232.6 6.6 %collective-permute-done.3 = bf16[2,384,256]{1,2,0:T(8,128)(2,1)} collective-permute-done((bf16[2,384,256]{1,2,0:T(8,128)(2,1)}, bf16[2,384,256]{1,2,0:T(8,128)(2,1)}, u32[]{:S(2)}, u32[]{:S(2)}) %collective-permute-start.3) | collective-permute-done | bytes 393248 | tf_op jit(solution)/shard_map/ppermute | solution.py:355
  239.3 8.6 %collective-permute-done.4 = bf16[2,384,256]{1,2,0:T(8,128)(2,1)} collective-permute-done((bf16[2,384,256]{1,2,0:T(8,128)(2,1)}, bf16[2,384,256]{1,2,0:T(8,128)(2,1)}, u32[]{:S(2)}, u32[]{:S(2)}) %collective-permute-start.4) | collective-permute-done | bytes 393248 | tf_op jit(solution)/shard_map/ppermute | solution.py:355
  247.9 1.0 collective-permute-done.2
  248.8 1.4 fusion.14
  251.2 1.0 slice.40
  252.5 1.1 broadcast_in_dim.11
  253.6 7.3 %all-to-all-start.10 = ((bf16[16,96,384]{2,1,0:T(8,128)(2,1)}), bf16[16,96,384]{2,1,0:T(8,128)(2,1)S(1)}, u32[]{:S(2)}, u32[]{:S(2)}) async-start(bf16[16,96,384]{2,1,0:T(8,128)(2,1)} %broadcast_in_dim.11), calls=%async_computation.10 | async-start | bytes 2359296 | tf_op jit(solution)/shard_map/all_to_all | solution.py:37
  260.9 1.0 fusion.25
  262.0 3.0 %collective-permute-start.5 = (bf16[384,256]{0,1:T(8,128)(2,1)S(1)}, bf16[384,256]{0,1:T(8,128)(2,1)S(1)}, u32[]{:S(2)}, u32[]{:S(2)}) collective-permute-start(bf16[384,256]{0,1:T(8,128)(2,1)S(1)} %dynamic-slice_bitcast_fusion), channel_id=1, source_target_pairs={{0,128},{16,144},{32,160},{48,176},{64,192},{80,208},{96,224},{112... | collective-permute-start | bytes 589832 | tf_op jit(solution)/shard_map/ppermute | solution.py:55
  265.0 16.6 %collective-permute-done.5 = bf16[384,256]{0,1:T(8,128)(2,1)S(1)} collective-permute-done((bf16[384,256]{0,1:T(8,128)(2,1)S(1)}, bf16[384,256]{0,1:T(8,128)(2,1)S(1)}, u32[]{:S(2)}, u32[]{:S(2)}) %collective-permute-start.5) | collective-permute-done | bytes 196640 | tf_op jit(solution)/shard_map/ppermute | solution.py:55
  281.6 1.1 fusion.22
  282.8 1.9 fusion.24
  (99 shorter events, 20.9 us)
Async XLA Ops:
  7.2 26.9 %copy-start.14 = (bf16[4096,384]{1,0:T(8,128)(2,1)S(1)}, bf16[4096,384]{1,0:T(8,128)(2,1)}, u32[]{:S(2)}) copy-start(bf16[4096,384]{1,0:T(8,128)(2,1)} %param.14) | copy-start | bytes 9437188
  7.2 132.5 %all-gather.2.cloned.1.call-start = ((), (), s32[]{:S(2)}) async-start(), calls=%async_computation.11 | async-start | bytes 2924544 | tf_op jit(solution)/shard_map/all_gather | solution.py:382
  8.2 0.8 copy-start.22
  8.9 1.7 copy-start.24
  12.2 5.9 %collective-permute-start = (bf16[512,96]{0,1:T(8,128)(2,1)}, bf16[512,96]{0,1:T(8,128)(2,1)S(1)}, u32[]{:S(2)}, u32[]{:S(2)}) collective-permute-start(bf16[512,96]{0,1:T(8,128)(2,1)} %param.9), channel_id=1, source_target_pairs={{0,128},{16,144},{32,160},{48,176},{64,192},{80,208},{96,224},{112... | collective-permute-start | bytes 294920 | tf_op jit(solution)/shard_map/ppermute | solution.py:55
  18.1 0.6 copy-start.16
  23.9 26.8 %all-to-all-start = ((bf16[16,36,384]{2,1,0:T(8,128)(2,1)}), bf16[16,36,384]{2,1,0:T(8,128)(2,1)}, u32[]{:S(2)}, u32[]{:S(2)}) async-start(bf16[16,36,384]{2,1,0:T(8,128)(2,1)} %fusion.19), calls=%async_computation | async-start | bytes 983040 | tf_op jit(solution)/shard_map/all_to_all | solution.py:37
  53.1 20.4 %all-to-all-start.1 = ((bf16[16,32,384]{2,1,0:T(8,128)(2,1)}), bf16[16,32,384]{2,1,0:T(8,128)(2,1)S(1)}, u32[]{:S(2)}, u32[]{:S(2)}) async-start(bf16[16,32,384]{2,1,0:T(8,128)(2,1)} %broadcast_in_dim.9), calls=%async_computation.1 | async-start | bytes 786432 | tf_op jit(solution)/shard_map/all_to_all | solution.py:37
  73.5 1.0 copy-start.10
  78.4 44.1 %copy-start = (bf16[512,4096]{1,0:T(8,128)(2,1)}, bf16[512,4096]{1,0:T(8,128)(2,1)S(1)}, u32[]{:S(2)}) copy-start(bf16[512,4096]{1,0:T(8,128)(2,1)S(1)} %get-tuple-element.29.energy_ref) | copy-start | bytes 12582916
  124.4 10.8 %all-to-all-start.5 = ((f32[16,4,128]{2,1,0:T(4,128)}), f32[16,4,128]{2,1,0:T(4,128)S(1)}, u32[]{:S(2)}, u32[]{:S(2)}) async-start(f32[16,4,128]{2,1,0:T(4,128)} %shard_map.114), calls=%async_computation.5 | async-start | bytes 65536 | tf_op jit(solution)/shard_map/all_to_all | solution.py:37
  135.2 2.2 copy-start.1
  139.7 3.6 %copy-start.15 = (bf16[1536,896]{1,0:T(8,128)(2,1)S(1)}, bf16[1536,896]{1,0:T(8,128)(2,1)}, u32[]{:S(2)}) copy-start(bf16[1536,896]{1,0:T(8,128)(2,1)} %all-gather.2.cloned.1.call-done) | copy-start | bytes 8257540
  141.3 9.5 %copy-start.18 = (f32[384]{0:T(512)}, f32[384]{0:T(512)S(1)}, u32[]{:S(2)}) copy-start(f32[384]{0:T(512)S(1)} %convert_reduce_fusion.2) | copy-start | bytes 4612
  143.2 7.6 %copy-start.20 = (f32[512]{0:T(512)}, f32[512]{0:T(512)S(1)}, u32[]{:S(2)}) copy-start(f32[512]{0:T(512)S(1)} %get-tuple-element.71) | copy-start | bytes 6148
  143.2 7.6 %copy-start.21 = (f32[512]{0:T(512)}, f32[512]{0:T(512)S(1)}, u32[]{:S(2)}) copy-start(f32[512]{0:T(512)S(1)} %get-tuple-element.70) | copy-start | bytes 6148
  145.1 14.9 %copy-start.19 = (f32[512]{0:T(512)}, f32[512]{0:T(512)S(1)}, u32[]{:S(2)}) copy-start(f32[512]{0:T(512)S(1)} %add_rsqrt_fusion.1) | copy-start | bytes 6148
  145.1 20.7 %all-to-all-start.6 = ((bf16[16,32,128]{2,1,0:T(8,128)(2,1)}), bf16[16,32,128]{2,1,0:T(8,128)(2,1)}, u32[]{:S(2)}, u32[]{:S(2)}) async-start(bf16[16,32,128]{2,1,0:T(8,128)(2,1)} %shard_map.115), calls=%async_computation.6 | async-start | bytes 262144 | tf_op jit(solution)/shard_map/all_to_all | solution.py:37
  160.0 2.0 copy-start.4
  162.0 0.9 copy-start.6
  162.9 0.6 copy-start.12
  165.8 2.2 copy-start.2
  168.0 0.7 copy-start.13
  173.1 0.9 copy-start.8
  173.9 0.7 copy-start.11
  174.6 10.9 %all-to-all-start.7 = ((f32[16,12,128]{2,1,0:T(8,128)}), f32[16,12,128]{2,1,0:T(8,128)S(1)}, u32[]{:S(2)}, u32[]{:S(2)}) async-start(f32[16,12,128]{2,1,0:T(8,128)} %copy-done.11), calls=%async_computation.7 | async-start | bytes 262144 | tf_op jit(solution)/shard_map/all_to_all | solution.py:37
  185.5 1.1 copy-start.7
  186.6 1.1 copy-start.9
  188.8 2.2 copy-start.3
  191.0 2.2 copy-start.5
  197.7 19.2 %collective-permute-start.1 = (bf16[8,384,256]{2,1,0:T(8,128)(2,1)S(1)}, bf16[8,384,256]{2,1,0:T(8,128)(2,1)}, u32[]{:S(2)}, u32[]{:S(2)}) collective-permute-start(bf16[8,384,256]{2,1,0:T(8,128)(2,1)S(1)} %get-tuple-element.47), channel_id=1, source_target_pairs={{0,16},{16,0},{32,48},{48,32},{64,80},{80,64},{96,112},{112,96},{1... | collective-permute-start | bytes 4718600 | tf_op jit(solution)/shard_map/ppermute | solution.py:55
  199.6 15.4 %all-to-all-start.8 = ((bf16[16,32,384]{2,1,0:T(8,128)(2,1)}), bf16[16,32,384]{2,1,0:T(8,128)(2,1)S(1)}, u32[]{:S(2)}, u32[]{:S(2)}) async-start(bf16[16,32,384]{2,1,0:T(8,128)(2,1)} %bitcast.10), calls=%async_computation.8 | async-start | bytes 786432 | tf_op jit(solution)/shard_map/all_to_all | solution.py:37
  219.6 30.7 %all-to-all-start.9 = ((bf16[16,35,384]{2,1,0:T(8,128)(2,1)}), bf16[16,35,384]{2,1,0:T(8,128)(2,1)}, u32[]{:S(2)}, u32[]{:S(2)}) async-start(bf16[16,35,384]{2,1,0:T(8,128)(2,1)} %broadcast_in_dim.10), calls=%async_computation.9 | async-start | bytes 983040 | tf_op jit(solution)/shard_map/all_to_all | solution.py:37
  227.5 11.7 %collective-permute-start.3 = (bf16[2,384,256]{1,2,0:T(8,128)(2,1)}, bf16[2,384,256]{1,2,0:T(8,128)(2,1)}, u32[]{:S(2)}, u32[]{:S(2)}) collective-permute-start(bf16[2,384,256]{1,2,0:T(8,128)(2,1)} %bitcast.18), channel_id=1, source_target_pairs={{0,64},{16,80},{32,96},{48,112},{64,0},{80,16},{96,32},{112,48},{1... | collective-permute-start | bytes 1179656 | tf_op jit(solution)/shard_map/ppermute | solution.py:355
  230.3 17.6 %collective-permute-start.4 = (bf16[2,384,256]{1,2,0:T(8,128)(2,1)}, bf16[2,384,256]{1,2,0:T(8,128)(2,1)}, u32[]{:S(2)}, u32[]{:S(2)}) collective-permute-start(bf16[2,384,256]{1,2,0:T(8,128)(2,1)} %bitcast.19), channel_id=1, source_target_pairs={{0,96},{16,112},{32,0},{48,16},{64,32},{80,48},{96,64},{112,80},{1... | collective-permute-start | bytes 1179656 | tf_op jit(solution)/shard_map/ppermute | solution.py:355
  231.1 17.7 %collective-permute-start.2 = (bf16[2,384,256]{1,2,0:T(8,128)(2,1)S(1)}, bf16[2,384,256]{1,2,0:T(8,128)(2,1)}, u32[]{:S(2)}, u32[]{:S(2)}) collective-permute-start(bf16[2,384,256]{1,2,0:T(8,128)(2,1)S(1)} %bitcast.59), channel_id=1, source_target_pairs={{0,32},{16,48},{32,64},{48,80},{64,96},{80,112},{96,0},{112,16},{1... | collective-permute-start | bytes 1179656 | tf_op jit(solution)/shard_map/ppermute | solution.py:355
  231.7 20.5 %copy-start.23 = (f32[96]{0:T(128)S(1)}, f32[96]{0:T(128)}, u32[]{:S(2)}) copy-start(f32[96]{0:T(128)} %copy-done.22) | copy-start | bytes 1156
  232.6 19.7 %copy-start.17 = (bf16[512,96]{0,1:T(8,128)(2,1)S(1)}, bf16[512,96]{0,1:T(8,128)(2,1)}, u32[]{:S(2)}) copy-start(bf16[512,96]{0,1:T(8,128)(2,1)} %param.8) | copy-start | bytes 294916
  253.6 31.0 %all-to-all-start.10 = ((bf16[16,96,384]{2,1,0:T(8,128)(2,1)}), bf16[16,96,384]{2,1,0:T(8,128)(2,1)S(1)}, u32[]{:S(2)}, u32[]{:S(2)}) async-start(bf16[16,96,384]{2,1,0:T(8,128)(2,1)} %broadcast_in_dim.11), calls=%async_computation.10 | async-start | bytes 2359296 | tf_op jit(solution)/shard_map/all_to_all | solution.py:37
  262.0 19.6 %collective-permute-start.5 = (bf16[384,256]{0,1:T(8,128)(2,1)S(1)}, bf16[384,256]{0,1:T(8,128)(2,1)S(1)}, u32[]{:S(2)}, u32[]{:S(2)}) collective-permute-start(bf16[384,256]{0,1:T(8,128)(2,1)S(1)} %dynamic-slice_bitcast_fusion), channel_id=1, source_target_pairs={{0,128},{16,144},{32,160},{48,176},{64,192},{80,208},{96,224},{112... | collective-permute-start | bytes 589832 | tf_op jit(solution)/shard_map/ppermute | solution.py:55
Sparse Core Ops, SparseCore 0:
  12.4 80.0 all-gather.1

commit v4 on v3

--- a/solution.py
+++ b/solution.py
@@ -17,6 +17,7 @@
 F32 = jnp.float32
 LOG2E = 1.4426950408889634
 BLOCK = 1024
+GRANT = 24 * 1024 * 1024
 LANES = 128
 
 
@@ -111,17 +112,12 @@
     return total
 
 
-def energy_kernel(pick_ref, teacher_ref, protos_ref, energy_ref, sums_ref, paired, held):
+def energy_kernel(teacher_ref, protos_ref, energy_ref, sums_ref, held):
     step = pl.program_id(0)
-
-    @pl.when(step == 0)
-    def _():
-        paired[...] = jnp.dot(pick_ref[...], teacher_ref[...], preferred_element_type=F32).astype(BF16)
-
     rows = []
     for part in range(BLOCK // 256):
         cut = slice(part * 256, part * 256 + 256)
-        value = jnp.exp2(contract_last(paired[...], protos_ref[cut, :]) * (LOG2E / TEACHER_TEMP))
+        value = jnp.exp2(contract_last(teacher_ref[...], protos_ref[cut, :]) * (LOG2E / TEACHER_TEMP))
         energy_ref[:, cut] = value.astype(BF16)
         total = jnp.sum(value, axis=0, keepdims=True)
         rows += [total[:, :LANES], total[:, LANES:]]
@@ -187,16 +183,15 @@
         cut = slice(part * 256, part * 256 + 256)
         value = jnp.exp2(contract_last(student_ref[...], protos_ref[cut, :]) * (LOG2E / STUDENT_TEMP))
         held[...] += value[:, :LANES] + value[:, LANES:]
-        value = value.astype(BF16)
-        exponent_ref[:, cut] = value
-        pulled_ref[...] += jnp.dot(value, protos_ref[cut, :], preferred_element_type=F32)
+        exponent_ref[:, cut] = value.astype(BF16)
+    pulled_ref[...] += jnp.dot(exponent_ref[...], protos_ref[...], preferred_element_type=F32)
 
     @pl.when(step == pl.num_programs(0) - 1)
     def _():
         partition_ref[...] = row_form(held[...])
 
 
-def last_kernel(got_ref, partition_ref, energy_ref, student_ref, protos_ref, sums_ref, coded_ref, scale_ref, held):
+def last_kernel(got_ref, partition_ref, energy_ref, student_ref, protos_ref, sums_ref, coded_ref, scale_ref, held, scaled):
     step = pl.program_id(0)
 
     @pl.when(step == 0)
@@ -210,8 +205,9 @@
         left = energy_ref[:, part * 256 : part * 256 + LANES].astype(F32) * scale_ref[pl.ds(start + 2 * part, 1), :]
         right = energy_ref[:, part * 256 + LANES : part * 256 + 256].astype(F32) * scale_ref[pl.ds(start + 2 * part + 1, 1), :]
         held[...] += left + right
-        value = jnp.concatenate([left.astype(BF16), right.astype(BF16)], 1)
-        coded_ref[...] += jnp.dot(value, protos_ref[part * 256 : part * 256 + 256, :], preferred_element_type=F32)
+        scaled[:, part * 256 : part * 256 + LANES] = left.astype(BF16)
+        scaled[:, part * 256 + LANES : part * 256 + 256] = right.astype(BF16)
+    coded_ref[...] += jnp.dot(scaled[...], protos_ref[...], preferred_element_type=F32)
 
     @pl.when(step == pl.num_programs(0) - 1)
     def _():
@@ -241,17 +237,15 @@
         grad_ref[:, cut] = (pulled_ref[:, cut] * wanted - coded_ref[:, cut] * given).astype(BF16)
 
 
-def proto_grad_kernel(core_ref, turned_ref, wanted_ref, given_ref, scale_ref, exponent_ref, energy_ref, keep_ref, give_ref):
-    step = pl.program_id(0)
-    core = core_ref[0]
-    for out_ref, which in ((give_ref, 1 - core), (keep_ref, core)):
-        parts = []
-        for half in range(2):
-            cut = pl.ds(pl.multiple_of(which * 256 + half * LANES, LANES), LANES)
-            scale = scale_ref[pl.ds(step * 4 + which * 2 + half, 1), :]
-            score = exponent_ref[:, cut].astype(F32) * wanted_ref[...] - energy_ref[:, cut].astype(F32) * scale * given_ref[...]
-            parts.append(score.astype(BF16))
-        out_ref[0] = jnp.dot(turned_ref[...], jnp.concatenate(parts, 1), preferred_element_type=F32).astype(BF16)
+def proto_grad_kernel(core_ref, turned_ref, wanted_ref, given_ref, scale_ref, exponent_ref, energy_ref, out_ref):
+    line = pl.program_id(0) * 4 + core_ref[0] * 2
+    parts = []
+    for half in range(2):
+        cut = slice(half * LANES, half * LANES + LANES)
+        scale = scale_ref[pl.ds(line + half, 1), :]
+        score = exponent_ref[:, cut].astype(F32) * wanted_ref[...] - energy_ref[:, cut].astype(F32) * scale * given_ref[...]
+        parts.append(score.astype(BF16))
+    out_ref[0] = jnp.dot(turned_ref[...], jnp.concatenate(parts, 1), preferred_element_type=F32).astype(BF16)
 
 
 def whole(shape):
@@ -267,7 +261,7 @@
         out_shape=[shape for shape, _ in outs],
         scratch_shapes=scratch,
         compiler_params=pltpu.CompilerParams(
-            dimension_semantics=("arbitrary",), vmem_limit_bytes=24 * 1024 * 1024
+            dimension_semantics=("arbitrary",), vmem_limit_bytes=GRANT
         ),
         cost_estimate=pl.CostEstimate(flops=flops, bytes_accessed=moved, transcendentals=exps),
     )
@@ -289,9 +283,9 @@
     tall = pltpu.VMEM((crops, LANES), F32)
     short = pltpu.VMEM((tiles, LANES), F32)
     energy = called(
-        energy_kernel, steps, [whole((crops, crops)), whole((crops, size)), down],
+        energy_kernel, steps, [whole((crops, size)), down],
         [(array((crops, protos), BF16), across), col_sent],
-        [pltpu.VMEM((crops, size), BF16), short], product, 2 * matrix, matrix,
+        [short], product, 2 * matrix, matrix,
     )
     rows = called(
         row_kernel, steps, [whole((dps, tiles, LANES)), across], [row_sent], [short, tall], 2 * matrix, 2 * matrix
@@ -316,7 +310,7 @@
             (array((crops, size), F32), whole((crops, size))),
             (array((tiles, LANES), F32), whole((tiles, LANES))),
         ],
-        [tall], product, 2 * matrix,
+        [tall, pltpu.VMEM((crops, BLOCK), BF16)], product, 2 * matrix,
     )
     unit_grad = called(
         unit_grad_kernel, 1,
@@ -330,15 +324,25 @@
         [], 4 * crops * size, 10 * crops * size,
     )
     wide = protos // dps
-    pair = pl.BlockSpec((crops, 2 * wide), lambda step: (0, step))
-    block = (array((dps // 2, size, wide), BF16), pl.BlockSpec((1, size, wide), lambda step: (step, 0, 0)))
-    proto_grad = called(
-        proto_grad_kernel, dps // 2,
-        [
-            pl.BlockSpec(memory_space=pltpu.SMEM), whole((size, crops)), whole((crops, LANES)),
-            whole((crops, LANES)), whole((tiles, LANES)), pair, pair,
-        ],
-        [block, block], [], product, 4 * matrix + 2 * protos * size,
+    one = pl.BlockSpec((crops, wide), lambda step, core: (0, 2 * step + core[0]))
+    proto_grad = pl.pallas_call(
+        proto_grad_kernel,
+        grid_spec=pltpu.PrefetchScalarGridSpec(
+            num_scalar_prefetch=1,
+            grid=(dps // 2,),
+            in_specs=[
+                pl.BlockSpec((size, crops), lambda step, core: (0, 0)),
+                pl.BlockSpec((crops, LANES), lambda step, core: (0, 0)),
+                pl.BlockSpec((crops, LANES), lambda step, core: (0, 0)),
+                pl.BlockSpec((tiles, LANES), lambda step, core: (0, 0)),
+                one,
+                one,
+            ],
+            out_specs=pl.BlockSpec((1, size, wide), lambda step, core: (step, 0, 0)),
+        ),
+        out_shape=array((dps // 2, size, wide), BF16),
+        compiler_params=pltpu.CompilerParams(dimension_semantics=("arbitrary",), vmem_limit_bytes=GRANT),
+        cost_estimate=pl.CostEstimate(flops=product // 2, bytes_accessed=2 * matrix + protos * size, transcendentals=0),
     )
     return energy, rows, cols, student, last, unit_grad, proto_grad
 
@@ -374,29 +378,33 @@
     own = crops // parts
     size = student_proj.shape[1]
     start = lax.axis_index("proto") * width
-    opposite = swapped(teacher_cls, "dp", 8)
+    opposite = swapped(student_cls, "dp", 8)
     gain_s = lax.dynamic_slice_in_dim(student_gain, start, width)
     gain_t = lax.dynamic_slice_in_dim(teacher_gain, start, width)
 
-    weight = (gain_s[:, None] * student_proj.astype(F32)).astype(BF16)
-    gathered = lax.all_gather(jnp.concatenate([student_cls.T, weight], 1), "proto", axis=0, tiled=True)
-    teacher_blocks = packed_shares(opposite, gain_t, teacher_proj, parts)
+    teacher_blocks = packed_shares(teacher_cls, gain_t, teacher_proj, parts)
     teacher_hidden = summed_hidden(exchanged(teacher_blocks, "proto"))
     teacher_unit = unit_rows(teacher_hidden)[0].astype(BF16)
     teacher_all = from_all(teacher_unit, "proto").reshape(crops, size)
-    pick = (partner[:, None] % crops == jnp.arange(crops, dtype=jnp.int32)[None]).astype(BF16)
+
+    pick = partner[:, None] % crops == jnp.arange(crops, dtype=jnp.int32)[None]
+    turned = lax.dot_general(
+        opposite, pick.astype(BF16), (((0,), (1,)), ((), ())), preferred_element_type=F32
+    ).astype(BF16)
+    weight = (gain_s[:, None] * student_proj.astype(F32)).astype(BF16)
+    gathered = lax.all_gather(jnp.concatenate([turned, weight], 1), "proto", axis=0, tiled=True)
+
     proto_unit32, proto_factor = unit_rows(prototypes.astype(F32))
     proto_unit = proto_unit32.astype(BF16)
     protos = proto_unit.shape[0]
     energy_call, row_call, col_call, student_call, last_call, unit_grad_call, proto_grad_call = make_calls(
         crops, protos, size, lax.axis_size("dp"), parts
     )
-    energy, sums = energy_call(pick, teacher_all, proto_unit)
+    energy, sums = energy_call(teacher_all, proto_unit)
     for step in range(ITERS - 1):
         (sums,) = row_call(exchanged(sums, "dp"), energy)
         (sums,) = col_call(exchanged(sums, "proto"), energy)
 
-    sums, gathered = lax.optimization_barrier((sums, gathered))
     values = gathered[:, :crops].astype(F32)
     student_center, student_scale = center_and_scale(
         jnp.sum(values, axis=0)[:, None], jnp.sum(values * values, axis=0)[:, None]
@@ -407,17 +415,21 @@
     )
     student_unit32, student_factor = unit_rows(student_hidden)
     student_unit = student_unit32.astype(BF16)
+    sums, student_unit = lax.optimization_barrier((sums, student_unit))
     exponent, pulled, partition = student_call(student_unit, proto_unit)
     sums = exchanged(sums, "dp")
     sums, exponent, pulled, partition = lax.optimization_barrier((sums, exponent, pulled, partition))
     sums, coded, scale = last_call(sums, partition, energy, student_unit, proto_unit)
     unit_grad, crop_loss, wanted, given = unit_grad_call(exchanged(sums, "proto"), pulled, coded)
-    crop_loss = crop_loss.reshape(crops)
+    core = (lax.axis_index("dp") % 2).reshape(1)
+    details = (student_unit.T, wanted, given, scale, exponent, energy)
+    give = proto_grad_call(1 - core, *details)
+    give, unit_grad = lax.optimization_barrier((give, unit_grad))
     unit_grad = exchanged(unit_grad.reshape(parts, own, size), "proto")
-    core = (lax.axis_index("dp") % 2).reshape(1)
-    keep, give = proto_grad_call(core, student_unit.T, wanted, given, scale, exponent, energy)
-    stages = summed_protos(keep, give)
+    stages = summed_protos(proto_grad_call(core, *details), give)
     blocks = next(stages)
+    crop_loss = swapped(crop_loss, "dp", 8).reshape(1, crops)
+    crop_loss = jnp.sum(jnp.where(pick, crop_loss, 0.0), axis=1)
     student_unit32, student_factor, student_center, student_scale = (
         lax.dynamic_slice_in_dim(value, lax.axis_index("proto") * own, own, 0)
         for value in (student_unit32, student_factor, student_center, student_scale)
@@ -434,10 +446,13 @@
     packed = from_all(packed, "proto")
     moved = jnp.sum(packed[:, own:].astype(F32), axis=(0, 1))
     sent = packed[:, :own].reshape(crops, size)
-    share = (gain_s[:, None] * (contract_first(student_cls, sent) - moved[None])).astype(BF16)
+    share = (gain_s[:, None] * (jnp.dot(turned, sent, preferred_element_type=F32) - moved[None])).astype(BF16)
     share, blocks = lax.optimization_barrier((share, blocks))
+    near = [[8 * x + other for other in range(8)] for x in range(2)]
+    share = lax.all_to_all(jnp.broadcast_to(share[None], (8,) + share.shape), "dp", 0, 0, axis_index_groups=near)
+    share = jnp.sum(share.astype(F32), axis=0).astype(BF16)
     proto_unit_grad = stages.send(blocks).T
-    grad_proj = jnp.sum(from_all(share, "dp").astype(F32), axis=0)
+    grad_proj = share.astype(F32) + swapped(share, "dp", 8).astype(F32)
 
     count = protos // lax.axis_size("dp")
     own_start = lax.axis_index("dp") * count

time: 294 us -> 283 us (0.963)
  waiting for transfers between devices: 85 us -> 56.1 us
  blocking collectives: 41 us -> 51.1 us
  local copies, waits for them, and re-layouts: 34.3 us -> 41.2 us
    all_to_all x8 -> x6, waiting for transfers between devices: 50.5 us -> 36.1 us  [exchanged(): return lax.all_to_all(blocks, axis, 0, 0)]
    ppermute x3 -> x5, waiting for transfers between devices: 18.3 us -> 4.41 us  [swapped(): return lax.ppermute(value, axis, [(one, one ^ bit) for one in range(count)])]
    all_to_all x3 -> x4, blocking collectives: 41 us -> 51.1 us  [exchanged(): return lax.all_to_all(blocks, axis, 0, 0)]
    all_to_all x8 -> x6, starting transfers between devices: 44.4 us -> 36.4 us  [exchanged(): return lax.all_to_all(blocks, axis, 0, 0)]
    unnamed x51 -> x73, local copies, waits for them, and re-layouts: 19.1 us -> 26.8 us
    ppermute x3 -> x5, starting transfers between devices: 8.46 us -> 13.7 us  [swapped(): return lax.ppermute(value, axis, [(one, one ^ bit) for one in range(count)])]
    all_to_all x0 -> x1, starting transfers between devices: none -> 3.93 us  [body(): lax.all_to_all(jnp.broadcast_to(share[None], (8,) + share.shape), 'dp', 0...]
    pallas_call x2 -> x3, Pallas kernels: 8.39 us -> 10.4 us  [the longest x1 3.5 us: body(): give = proto_grad_call(1 - core, *details)]
  transfers between devices with their start and end apart: 15 -> 16, of which waited for: 10 -> 9; matrix products, arithmetic and copies ran while one was open for 11% -> 13% of each run, Pallas kernels for 6% -> 7%
where the time goes in v4:
time: 283 us; the launch traced here: 280 us
  starting transfers between devices  57.9 us (20%)
  waiting for transfers between devices  56.1 us (20%)
  blocking collectives  51.1 us (18%)
  local copies, waits for them, and re-layouts  41.2 us (15%)
  other arithmetic  28.5 us (10%)
  Pallas kernels  27.4 us (10%)
  between operations  14.7 us (5%)
  matrix products  2.84 us (1%)
    all_to_all x4, blocking collectives, exchanged(): return lax.all_to_all(blocks, axis, 0, 0)  51.1 us
    all_to_all x6, starting transfers between devices, exchanged(): return lax.all_to_all(blocks, axis, 0, 0)  36.4 us
    all_to_all x6, waiting for transfers between devices, exchanged(): return lax.all_to_all(blocks, axis, 0, 0)  36.1 us
    unnamed x73, local copies, waits for them, and re-layouts  26.8 us
    ppermute x3, waiting for transfers between devices, summed_protos(): total = total + lax.ppermute(give, 'dp', pairs).astype(F32)  14.5 us
    ppermute x5, starting transfers between devices, swapped(): return lax.ppermute(value, axis, [(one, one ^ bit) for one in range(count)])  13.7 us
  transfers between devices with their start and end apart: 16, of which 9 were waited for; matrix products, arithmetic and copies ran while one was open for 13% of the time, Pallas kernels for 7%

profile of v4, /device:TPU:1, one launch (start us, length us, event | category | flops | bytes accessed | tf_op | source)
XLA Modules:
  0.0 279.8 jit_solution(17796588684447257496)
XLA Ops:
  7.2 3.7 %collective-permute-start = (bf16[512,96]{0,1:T(8,128)(2,1)}, bf16[512,96]{0,1:T(8,128)(2,1)S(1)}, u32[]{:S(2)}, u32[]{:S(2)}) collective-permute-start(bf16[512,96]{0,1:T(8,128)(2,1)} %param.8), channel_id=1, source_target_pairs={{0,128},{16,144},{32,160},{48,176},{64,192},{80,208},{96,224},{112... | collective-permute-start | bytes 294920 | tf_op jit(solution)/shard_map/ppermute | solution.py:56
  13.0 1.7 fusion.24
  19.0 1.3 fusion.4
  22.7 1.8 fusion.14
  24.5 8.3 %all-to-all-start = ((bf16[16,36,384]{2,1,0:T(8,128)(2,1)}), bf16[16,36,384]{2,1,0:T(8,128)(2,1)}, u32[]{:S(2)}, u32[]{:S(2)}) async-start(bf16[16,36,384]{2,1,0:T(8,128)(2,1)} %fusion.14), calls=%async_computation | async-start | bytes 983040 | tf_op jit(solution)/shard_map/all_to_all | solution.py:38
  33.6 16.9 %all-to-all-done = bf16[16,36,384]{2,1,0:T(8,128)(2,1)} async-done(((bf16[16,36,384]{2,1,0:T(8,128)(2,1)}), bf16[16,36,384]{2,1,0:T(8,128)(2,1)}, u32[]{:S(2)}, u32[]{:S(2)}) %all-to-all-start) | async-done | bytes 442400 | tf_op jit(solution)/shard_map/all_to_all | solution.py:38
  50.5 1.1 convert_reduce_fusion.2
  52.8 6.9 %all-to-all-start.1 = ((bf16[16,32,384]{2,1,0:T(8,128)(2,1)}), bf16[16,32,384]{2,1,0:T(8,128)(2,1)S(1)}, u32[]{:S(2)}, u32[]{:S(2)}) async-start(bf16[16,32,384]{2,1,0:T(8,128)(2,1)} %broadcast_in_dim.19), calls=%async_computation.1 | async-start | bytes 786432 | tf_op jit(solution)/shard_map/all_to_all | solution.py:38
  59.7 2.3 fusion.1.protos_ref
  62.0 11.9 %all-to-all-done.1 = bf16[16,32,384]{2,1,0:T(8,128)(2,1)S(1)} async-done(((bf16[16,32,384]{2,1,0:T(8,128)(2,1)}), bf16[16,32,384]{2,1,0:T(8,128)(2,1)S(1)}, u32[]{:S(2)}, u32[]{:S(2)}) %all-to-all-start.1) | async-done | bytes 393248 | tf_op jit(solution)/shard_map/all_to_all | solution.py:38
  74.0 3.4 %shard_map.111 = (bf16[512,4096]{1,0:T(8,128)(2,1)S(1)}, bf16[16,32,128]{2,1,0:T(8,128)(2,1)S(1)}) custom-call(bf16[512,384]{1,0:T(8,128)(2,1)S(1)} %bitcast.48, bf16[4096,384]{1,0:T(8,128)(2,1)S(1)} %fusion.1.protos_ref), custom_call_target="tpu_custom_call" | custom-call | flops 1610612736 | bytes 4194304 | tf_op jit(solution)/shard_map/pallas_call | solution.py:403
  77.3 17.9 %all_to_all.55.got_ref = bf16[16,32,128]{2,1,0:T(8,128)(2,1)S(1)} all-to-all(bf16[16,32,128]{2,1,0:T(8,128)(2,1)S(1)} %get-tuple-element.28), channel_id=1, replica_groups=mesh['dp'=16,'proto'=16] {'dp'}, dimensions={0} | all-to-all | bytes 262144 | tf_op jit(solution)/shard_map/all_to_all | solution.py:38
  95.2 1.4 shard_map.112
  96.6 9.9 %all_to_all.56.got_ref = f32[16,4,128]{2,1,0:T(4,128)S(1)} all-to-all(f32[16,4,128]{2,1,0:T(4,128)S(1)} %shard_map.112), channel_id=1, replica_groups=mesh['dp'=16,'proto'=16] {'proto'}, dimensions={0} | all-to-all | bytes 65536 | tf_op jit(solution)/shard_map/all_to_all | solution.py:38
  106.5 1.6 shard_map.113
  108.1 13.3 %all_to_all.57.got_ref = bf16[16,32,128]{2,1,0:T(8,128)(2,1)S(1)} all-to-all(bf16[16,32,128]{2,1,0:T(8,128)(2,1)S(1)} %shard_map.113), channel_id=1, replica_groups=mesh['dp'=16,'proto'=16] {'dp'}, dimensions={0} | all-to-all | bytes 262144 | tf_op jit(solution)/shard_map/all_to_all | solution.py:38
  121.5 1.4 shard_map.114
  122.9 9.9 %all_to_all.58.got_ref = f32[16,4,128]{2,1,0:T(4,128)S(1)} all-to-all(f32[16,4,128]{2,1,0:T(4,128)S(1)} %shard_map.114), channel_id=1, replica_groups=mesh['dp'=16,'proto'=16] {'proto'}, dimensions={0} | all-to-all | bytes 65536 | tf_op jit(solution)/shard_map/all_to_all | solution.py:38
  132.8 1.6 shard_map.115
  135.1 2.0 fusion.2
  137.1 1.5 convert_reduce_fusion.1
  139.6 1.0 fusion.33
  140.6 5.7 %all-to-all-start.6 = ((bf16[16,32,128]{2,1,0:T(8,128)(2,1)}), bf16[16,32,128]{2,1,0:T(8,128)(2,1)}, u32[]{:S(2)}, u32[]{:S(2)}) async-start(bf16[16,32,128]{2,1,0:T(8,128)(2,1)} %copy-done.17), calls=%async_computation.6 | async-start | bytes 262144 | tf_op jit(solution)/shard_map/all_to_all | solution.py:38
  148.2 5.7 %shard_map.116 = (bf16[512,4096]{1,0:T(8,128)(2,1)S(1)}, f32[512,384]{1,0:T(8,128)S(1)}, f32[4,128]{1,0:T(4,128)S(1)}) custom-call(bf16[512,384]{1,0:T(8,128)(2,1)S(1)} %copy-done.7, bf16[4096,384]{1,0:T(8,128)(2,1)S(1)} %fusion.1.protos_ref), custom_call_target="tpu_custom_call" | custom-call | flops 3221225472 | bytes 4194304 | tf_op jit(solution)/shard_map/pallas_call | solution.py:419
  153.9 2.0 copy-done.4
  157.4 2.2 copy-done.1
  159.6 1.0 copy-done.8
  161.3 4.4 %shard_map.117 = (f32[16,12,128]{2,1,0:T(8,128)S(1)}, f32[512,384]{1,0:T(8,128)S(1)}, f32[32,128]{1,0:T(8,128)S(1)}) custom-call(bf16[16,32,128]{2,1,0:T(8,128)(2,1)} %all-to-all-done.6.got_ref, f32[4,128]{1,0:T(4,128)S(1)} %copy-done.20, bf16[512,4096]{1,0:T(8,128)(2,1)S(1)} %copy-done.1, bf16[512,384]{1,0:T(8,128)(2,1)S(1)} %copy-done.8, ...), custom_call_target="tpu_custom_call" | custom-call | flops 1610612736 | bytes 4194304 | tf_op jit(solution)/shard_map/pallas_call | solution.py:422
  167.3 3.7 %all-to-all-start.7 = ((f32[16,12,128]{2,1,0:T(8,128)}), f32[16,12,128]{2,1,0:T(8,128)S(1)}, u32[]{:S(2)}, u32[]{:S(2)}) async-start(f32[16,12,128]{2,1,0:T(8,128)} %copy-done.18), calls=%async_computation.7 | async-start | bytes 262144 | tf_op jit(solution)/shard_map/all_to_all | solution.py:38
  171.0 7.3 %all-to-all-done.7.got_ref = f32[16,12,128]{2,1,0:T(8,128)S(1)} async-done(((f32[16,12,128]{2,1,0:T(8,128)}), f32[16,12,128]{2,1,0:T(8,128)S(1)}, u32[]{:S(2)}, u32[]{:S(2)}) %all-to-all-start.7) | async-done | bytes 98336 | tf_op jit(solution)/shard_map/all_to_all | solution.py:38
  178.3 1.1 copy-done.14
  179.4 1.1 copy-done.16
  180.5 1.0 shard_map.118
  182.1 2.4 copy-done.2
  184.5 2.2 copy-done.5
  186.7 3.5 %shard_map.119 = bf16[8,384,256]{2,1,0:T(8,128)(2,1)S(1)} custom-call(s32[1]{0:T(128)S(6)} %sub.134.core_ref, bf16[384,512]{1,0:T(8,128)(2,1)S(1)} %bitcast.46, f32[512,128]{1,0:T(8,128)S(1)} %get-tuple-element.41.wanted_ref, f32[512,128]{1,0:T(8,128)S(1)} %get-tuple-element.42.given_ref, f32[32,128]{1,0:T(8,128)S(1)} %get-tuple-element.43.scale_ref, ...), custom_call_target="tpu_custom_call" | custom-call | flops 805306368 | bytes 5767168 | tf_op jit(solution)/shard_map/pallas_call | solution.py:426
  190.2 1.5 collective-permute-start.2
  191.7 4.2 %all-to-all-start.8 = ((bf16[16,32,384]{2,1,0:T(8,128)(2,1)}), bf16[16,32,384]{2,1,0:T(8,128)(2,1)}, u32[]{:S(2)}, u32[]{:S(2)}) async-start(bf16[16,32,384]{2,1,0:T(8,128)(2,1)} %bitcast.12), calls=%async_computation.8 | async-start | bytes 786432 | tf_op jit(solution)/shard_map/all_to_all | solution.py:38
  196.0 1.3 dynamic-slice.7
  197.2 1.3 dynamic-slice.8
  198.5 1.3 dynamic-slice.6
  199.8 2.2 copy-done.3
  202.0 2.2 copy-done.6
  206.0 3.5 %shard_map.120 = bf16[8,384,256]{2,1,0:T(8,128)(2,1)S(1)} custom-call(s32[1]{0:T(128)} %bitcast.10.core_ref, bf16[384,512]{1,0:T(8,128)(2,1)S(1)} %bitcast.47, f32[512,128]{1,0:T(8,128)S(1)} %copy-done.10, f32[512,128]{1,0:T(8,128)S(1)} %copy-done.12, f32[32,128]{1,0:T(8,128)S(1)} %get-tuple-element.43.scale_ref, bf16[512,4096]{1,0:T(8,128)(2,1)S(1)} %copy-done.6, ...), custom_call_target="tpu_custom_call" | custom-call | flops 805306368 | bytes 5767168 | tf_op jit(solution)/shard_map/pallas_call | solution.py:429
  209.6 1.1 convert_reduce_fusion.3
  210.8 1.1 multiply_reduce_fusion.2
  211.8 1.2 multiply_reduce_fusion.1
  213.2 1.8 add_convert_fusion
  215.8 7.5 %all-to-all-start.9 = ((bf16[16,35,384]{2,1,0:T(8,128)(2,1)}), bf16[16,35,384]{2,1,0:T(8,128)(2,1)}, u32[]{:S(2)}, u32[]{:S(2)}) async-start(bf16[16,35,384]{2,1,0:T(8,128)(2,1)} %broadcast_in_dim.27), calls=%async_computation.9 | async-start | bytes 983040 | tf_op jit(solution)/shard_map/all_to_all | solution.py:38
  223.7 2.8 collective-permute-start.5
  229.4 1.0 fusion.20
  230.5 2.8 %collective-permute-start.1 = (f32[4,128]{1,0:T(4,128)S(1)}, f32[4,128]{1,0:T(4,128)S(1)}, u32[]{:S(2)}, u32[]{:S(2)}) collective-permute-start(f32[4,128]{1,0:T(4,128)S(1)} %copy-done.22), channel_id=1, source_target_pairs={{0,128},{16,144},{32,160},{48,176},{64,192},{80,208},{96,224},{112... | collective-permute-start | bytes 6152 | tf_op jit(solution)/shard_map/ppermute | solution.py:56
  234.2 1.0 collective-permute-done.5
  235.2 3.8 %collective-permute-done.4 = bf16[2,384,256]{1,2,0:T(8,128)(2,1)} collective-permute-done((bf16[2,384,256]{1,2,0:T(8,128)(2,1)}, bf16[2,384,256]{1,2,0:T(8,128)(2,1)}, u32[]{:S(2)}, u32[]{:S(2)}) %collective-permute-start.4) | collective-permute-done | bytes 393248 | tf_op jit(solution)/shard_map/ppermute | solution.py:359
  239.0 9.7 %collective-permute-done.3 = bf16[2,384,256]{1,2,0:T(8,128)(2,1)} collective-permute-done((bf16[2,384,256]{1,2,0:T(8,128)(2,1)}, bf16[2,384,256]{1,2,0:T(8,128)(2,1)}, u32[]{:S(2)}, u32[]{:S(2)}) %collective-permute-start.3) | collective-permute-done | bytes 393248 | tf_op jit(solution)/shard_map/ppermute | solution.py:359
  248.7 1.4 fusion.12
  251.1 1.0 slice.42
  253.2 3.9 %all-to-all-start.10 = ((bf16[8,96,384]{2,1,0:T(8,128)(2,1)}), bf16[8,96,384]{2,1,0:T(8,128)(2,1)S(1)}, u32[]{:S(2)}, u32[]{:S(2)}) async-start(bf16[8,96,384]{2,1,0:T(8,128)(2,1)} %broadcast_in_dim.28), calls=%async_computation.10 | async-start | bytes 1179648 | tf_op jit(solution)/shard_map/all_to_all | solution.py:452
  257.2 2.8 %collective-permute-start.7 = (bf16[384,256]{0,1:T(8,128)(2,1)S(1)}, bf16[384,256]{0,1:T(8,128)(2,1)S(1)}, u32[]{:S(2)}, u32[]{:S(2)}) collective-permute-start(bf16[384,256]{0,1:T(8,128)(2,1)S(1)} %dynamic-slice_bitcast_fusion), channel_id=1, source_target_pairs={{0,128},{16,144},{32,160},{48,176},{64,192},{80,208},{96,224},{112... | collective-permute-start | bytes 589832 | tf_op jit(solution)/shard_map/ppermute | solution.py:56
  260.8 4.3 %collective-permute-done.7 = bf16[384,256]{0,1:T(8,128)(2,1)S(1)} collective-permute-done((bf16[384,256]{0,1:T(8,128)(2,1)S(1)}, bf16[384,256]{0,1:T(8,128)(2,1)S(1)}, u32[]{:S(2)}, u32[]{:S(2)}) %collective-permute-start.7) | collective-permute-done | bytes 196640 | tf_op jit(solution)/shard_map/ppermute | solution.py:56
  265.1 1.1 fusion.17
  266.3 1.1 all-to-all-done.10
  267.4 2.8 %collective-permute-start.6 = (bf16[96,384]{1,0:T(8,128)(2,1)S(1)}, bf16[96,384]{1,0:T(8,128)(2,1)S(1)}, u32[]{:S(2)}, u32[]{:S(2)}) collective-permute-start(bf16[96,384]{1,0:T(8,128)(2,1)S(1)} %reduce_sum.206), channel_id=1, source_target_pairs={{0,128},{16,144},{32,160},{48,176},{64,192},{80,208},{96,224},{112... | collective-permute-start | bytes 221192 | tf_op jit(solution)/shard_map/ppermute | solution.py:56
  270.3 1.8 fusion.19
  (128 shorter events, 29.3 us)
Async XLA Ops:
  7.2 25.7 %copy-start.23 = (bf16[4096,384]{1,0:T(8,128)(2,1)S(1)}, bf16[4096,384]{1,0:T(8,128)(2,1)}, u32[]{:S(2)}) copy-start(bf16[4096,384]{1,0:T(8,128)(2,1)} %param.14) | copy-start | bytes 9437188
  7.2 127.9 %all-gather.2.cloned.1.call-start = ((), (), s32[]{:S(2)}) async-start(), calls=%async_computation.11 | async-start | bytes 2924544 | tf_op jit(solution)/shard_map/all_gather | solution.py:395
  7.2 8.2 %collective-permute-start = (bf16[512,96]{0,1:T(8,128)(2,1)}, bf16[512,96]{0,1:T(8,128)(2,1)S(1)}, u32[]{:S(2)}, u32[]{:S(2)}) collective-permute-start(bf16[512,96]{0,1:T(8,128)(2,1)} %param.8), channel_id=1, source_target_pairs={{0,128},{16,144},{32,160},{48,176},{64,192},{80,208},{96,224},{112... | collective-permute-start | bytes 294920 | tf_op jit(solution)/shard_map/ppermute | solution.py:56
  11.7 5.5 %copy-start.35 = (f32[96]{0:T(128)}, f32[96]{0:T(128)S(1)}, u32[]{:S(2)}) copy-start(f32[96]{0:T(128)S(1)} %dynamic_slice.37) | copy-start | bytes 1156
  12.4 0.6 copy-start.33
  14.7 3.7 %copy-start.27 = (f32[384]{0:T(512)}, f32[384]{0:T(512)S(1)}, u32[]{:S(2)}) copy-start(f32[384]{0:T(512)S(1)} %get-tuple-element.64) | copy-start | bytes 4612
  15.4 1.8 copy-start.29
  15.9 0.6 copy-start.25
  24.5 26.0 %all-to-all-start = ((bf16[16,36,384]{2,1,0:T(8,128)(2,1)}), bf16[16,36,384]{2,1,0:T(8,128)(2,1)}, u32[]{:S(2)}, u32[]{:S(2)}) async-start(bf16[16,36,384]{2,1,0:T(8,128)(2,1)} %fusion.14), calls=%async_computation | async-start | bytes 983040 | tf_op jit(solution)/shard_map/all_to_all | solution.py:38
  52.8 21.1 %all-to-all-start.1 = ((bf16[16,32,384]{2,1,0:T(8,128)(2,1)}), bf16[16,32,384]{2,1,0:T(8,128)(2,1)S(1)}, u32[]{:S(2)}, u32[]{:S(2)}) async-start(bf16[16,32,384]{2,1,0:T(8,128)(2,1)} %broadcast_in_dim.19), calls=%async_computation.1 | async-start | bytes 786432 | tf_op jit(solution)/shard_map/all_to_all | solution.py:38
  77.3 55.5 %copy-start = (bf16[512,4096]{1,0:T(8,128)(2,1)}, bf16[512,4096]{1,0:T(8,128)(2,1)S(1)}, u32[]{:S(2)}) copy-start(bf16[512,4096]{1,0:T(8,128)(2,1)S(1)} %get-tuple-element.29.energy_ref) | copy-start | bytes 12582916
  134.4 0.7 copy-start.17
  135.1 3.6 %copy-start.24 = (bf16[1536,896]{1,0:T(8,128)(2,1)S(1)}, bf16[1536,896]{1,0:T(8,128)(2,1)}, u32[]{:S(2)}) copy-start(bf16[1536,896]{1,0:T(8,128)(2,1)} %all-gather.2.cloned.1.call-done) | copy-start | bytes 8257540
  137.1 2.4 copy-start.31
  137.1 2.4 copy-start.32
  139.5 6.8 %copy-start.28 = (f32[512]{0:T(512)}, f32[512]{0:T(512)S(1)}, u32[]{:S(2)}) copy-start(f32[512]{0:T(512)S(1)} %add_rsqrt_fusion.1) | copy-start | bytes 6148
  140.6 16.8 %all-to-all-start.6 = ((bf16[16,32,128]{2,1,0:T(8,128)(2,1)}), bf16[16,32,128]{2,1,0:T(8,128)(2,1)}, u32[]{:S(2)}, u32[]{:S(2)}) async-start(bf16[16,32,128]{2,1,0:T(8,128)(2,1)} %copy-done.17), calls=%async_computation.6 | async-start | bytes 262144 | tf_op jit(solution)/shard_map/all_to_all | solution.py:38
  147.2 1.0 copy-start.7
  153.9 2.0 copy-start.4
  155.9 1.0 copy-start.13
  156.8 0.6 copy-start.19
  157.4 2.2 copy-start.1
  159.6 1.0 copy-start.8
  160.6 0.7 copy-start.20
  165.7 0.9 copy-start.15
  166.6 0.7 copy-start.18
  167.3 11.0 %all-to-all-start.7 = ((f32[16,12,128]{2,1,0:T(8,128)}), f32[16,12,128]{2,1,0:T(8,128)S(1)}, u32[]{:S(2)}, u32[]{:S(2)}) async-start(f32[16,12,128]{2,1,0:T(8,128)} %copy-done.18), calls=%async_computation.7 | async-start | bytes 262144 | tf_op jit(solution)/shard_map/all_to_all | solution.py:38
  178.3 1.1 copy-start.14
  179.4 1.1 copy-start.16
  181.5 0.6 copy-start.21
  182.1 8.1 %copy-start.9 = (f32[512,128]{1,0:T(8,128)}, f32[512,128]{1,0:T(8,128)S(1)}, u32[]{:S(2)}) copy-start(f32[512,128]{1,0:T(8,128)S(1)} %get-tuple-element.41.wanted_ref) | copy-start | bytes 786436
  182.1 8.1 %copy-start.11 = (f32[512,128]{1,0:T(8,128)}, f32[512,128]{1,0:T(8,128)S(1)}, u32[]{:S(2)}) copy-start(f32[512,128]{1,0:T(8,128)S(1)} %get-tuple-element.42.given_ref) | copy-start | bytes 786436
  182.1 2.4 copy-start.2
  184.5 2.2 copy-start.5
  190.2 22.9 %collective-permute-start.2 = (bf16[8,384,256]{2,1,0:T(8,128)(2,1)S(1)}, bf16[8,384,256]{2,1,0:T(8,128)(2,1)}, u32[]{:S(2)}, u32[]{:S(2)}) collective-permute-start(bf16[8,384,256]{2,1,0:T(8,128)(2,1)S(1)} %shard_map.119), channel_id=1, source_target_pairs={{0,16},{16,0},{32,48},{48,32},{64,80},{80,64},{96,112},{112,96},{1... | collective-permute-start | bytes 4718600 | tf_op jit(solution)/shard_map/ppermute | solution.py:56
  191.7 17.8 %all-to-all-start.8 = ((bf16[16,32,384]{2,1,0:T(8,128)(2,1)}), bf16[16,32,384]{2,1,0:T(8,128)(2,1)}, u32[]{:S(2)}, u32[]{:S(2)}) async-start(bf16[16,32,384]{2,1,0:T(8,128)(2,1)} %bitcast.12), calls=%async_computation.8 | async-start | bytes 786432 | tf_op jit(solution)/shard_map/all_to_all | solution.py:38
  199.8 2.2 copy-start.3
  202.0 2.2 copy-start.6
  204.1 0.9 copy-start.10
  205.1 0.9 copy-start.12
  215.8 34.3 %all-to-all-start.9 = ((bf16[16,35,384]{2,1,0:T(8,128)(2,1)}), bf16[16,35,384]{2,1,0:T(8,128)(2,1)}, u32[]{:S(2)}, u32[]{:S(2)}) async-start(bf16[16,35,384]{2,1,0:T(8,128)(2,1)} %broadcast_in_dim.27), calls=%async_computation.9 | async-start | bytes 983040 | tf_op jit(solution)/shard_map/all_to_all | solution.py:38
  223.3 7.2 %copy-start.22 = (f32[4,128]{1,0:T(4,128)S(1)}, f32[4,128]{1,0:T(4,128)}, u32[]{:S(2)}) copy-start(f32[4,128]{1,0:T(4,128)} %copy-done.21) | copy-start | bytes 6148
  223.7 11.6 %collective-permute-start.5 = (bf16[2,384,256]{1,2,0:T(8,128)(2,1)S(1)}, bf16[2,384,256]{1,2,0:T(8,128)(2,1)}, u32[]{:S(2)}, u32[]{:S(2)}) collective-permute-start(bf16[2,384,256]{1,2,0:T(8,128)(2,1)S(1)} %bitcast.53), channel_id=1, source_target_pairs={{0,96},{16,112},{32,0},{48,16},{64,32},{80,48},{96,64},{112,80},{1... | collective-permute-start | bytes 1179656 | tf_op jit(solution)/shard_map/ppermute | solution.py:359
  227.4 11.6 %collective-permute-start.4 = (bf16[2,384,256]{1,2,0:T(8,128)(2,1)}, bf16[2,384,256]{1,2,0:T(8,128)(2,1)}, u32[]{:S(2)}, u32[]{:S(2)}) collective-permute-start(bf16[2,384,256]{1,2,0:T(8,128)(2,1)} %bitcast.17), channel_id=1, source_target_pairs={{0,64},{16,80},{32,96},{48,112},{64,0},{80,16},{96,32},{112,48},{1... | collective-permute-start | bytes 1179656 | tf_op jit(solution)/shard_map/ppermute | solution.py:359
  228.8 19.8 %collective-permute-start.3 = (bf16[2,384,256]{1,2,0:T(8,128)(2,1)}, bf16[2,384,256]{1,2,0:T(8,128)(2,1)}, u32[]{:S(2)}, u32[]{:S(2)}) collective-permute-start(bf16[2,384,256]{1,2,0:T(8,128)(2,1)} %bitcast.16), channel_id=1, source_target_pairs={{0,32},{16,48},{32,64},{48,80},{64,96},{80,112},{96,0},{112,16},{1... | collective-permute-start | bytes 1179656 | tf_op jit(solution)/shard_map/ppermute | solution.py:359
  230.5 21.6 %copy-start.34 = (f32[96]{0:T(128)S(1)}, f32[96]{0:T(128)}, u32[]{:S(2)}) copy-start(f32[96]{0:T(128)} %copy-done.33) | copy-start | bytes 1156
  230.5 29.5 %collective-permute-start.1 = (f32[4,128]{1,0:T(4,128)S(1)}, f32[4,128]{1,0:T(4,128)S(1)}, u32[]{:S(2)}, u32[]{:S(2)}) collective-permute-start(f32[4,128]{1,0:T(4,128)S(1)} %copy-done.22), channel_id=1, source_target_pairs={{0,128},{16,144},{32,160},{48,176},{64,192},{80,208},{96,224},{112... | collective-permute-start | bytes 6152 | tf_op jit(solution)/shard_map/ppermute | solution.py:56
  234.2 17.9 %copy-start.26 = (bf16[512,96]{0,1:T(8,128)(2,1)S(1)}, bf16[512,96]{0,1:T(8,128)(2,1)}, u32[]{:S(2)}) copy-start(bf16[512,96]{0,1:T(8,128)(2,1)} %copy-done.25) | copy-start | bytes 294916
  234.2 25.8 %copy-start.30 = (s32[512]{0:T(512)S(1)}, s32[512]{0:T(512)}, u32[]{:S(2)}) copy-start(s32[512]{0:T(512)} %copy-done.29) | copy-start | bytes 6148
  253.2 14.1 %all-to-all-start.10 = ((bf16[8,96,384]{2,1,0:T(8,128)(2,1)}), bf16[8,96,384]{2,1,0:T(8,128)(2,1)S(1)}, u32[]{:S(2)}, u32[]{:S(2)}) async-start(bf16[8,96,384]{2,1,0:T(8,128)(2,1)} %broadcast_in_dim.28), calls=%async_computation.10 | async-start | bytes 1179648 | tf_op jit(solution)/shard_map/all_to_all | solution.py:452
  257.2 8.0 %collective-permute-start.7 = (bf16[384,256]{0,1:T(8,128)(2,1)S(1)}, bf16[384,256]{0,1:T(8,128)(2,1)S(1)}, u32[]{:S(2)}, u32[]{:S(2)}) collective-permute-start(bf16[384,256]{0,1:T(8,128)(2,1)S(1)} %dynamic-slice_bitcast_fusion), channel_id=1, source_target_pairs={{0,128},{16,144},{32,160},{48,176},{64,192},{80,208},{96,224},{112... | collective-permute-start | bytes 589832 | tf_op jit(solution)/shard_map/ppermute | solution.py:56
  267.4 4.8 %collective-permute-start.6 = (bf16[96,384]{1,0:T(8,128)(2,1)S(1)}, bf16[96,384]{1,0:T(8,128)(2,1)S(1)}, u32[]{:S(2)}, u32[]{:S(2)}) collective-permute-start(bf16[96,384]{1,0:T(8,128)(2,1)S(1)} %reduce_sum.206), channel_id=1, source_target_pairs={{0,128},{16,144},{32,160},{48,176},{64,192},{80,208},{96,224},{112... | collective-permute-start | bytes 221192 | tf_op jit(solution)/shard_map/ppermute | solution.py:56
Sparse Core Ops, SparseCore 0:
  17.3 78.1 all-gather.1

commit v5 on v4

--- a/solution.py
+++ b/solution.py
@@ -17,7 +17,7 @@
 F32 = jnp.float32
 LOG2E = 1.4426950408889634
 BLOCK = 1024
-GRANT = 24 * 1024 * 1024
+GRANT = 56 * 1024 * 1024
 LANES = 128
 
 
@@ -246,6 +246,15 @@
         score = exponent_ref[:, cut].astype(F32) * wanted_ref[...] - energy_ref[:, cut].astype(F32) * scale * given_ref[...]
         parts.append(score.astype(BF16))
     out_ref[0] = jnp.dot(turned_ref[...], jnp.concatenate(parts, 1), preferred_element_type=F32).astype(BF16)
+
+
+def hidden_grad_kernel(got_ref, unit_ref, factor_ref, out_ref):
+    grad = stack_sum(got_ref)
+    unit = unit_ref[...]
+    grad = factor_ref[...] * (grad - unit * jnp.sum(unit * grad, axis=1, keepdims=True))
+    grad = grad.astype(BF16)
+    for one in range(out_ref.shape[0]):
+        out_ref[one] = grad
 
 
 def whole(shape):
@@ -322,6 +331,11 @@
             (array((crops, LANES), F32), whole((crops, LANES))),
         ],
         [], 4 * crops * size, 10 * crops * size,
+    )
+    own = crops // parts
+    hidden_grad = called(
+        hidden_grad_kernel, 1, [whole((parts, own, size)), whole((own, size)), whole((own, 1))],
+        [(array((parts, own, size), BF16), whole((parts, own, size)))], [], 6 * own * size, 4 * crops * size,
     )
     wide = protos // dps
     one = pl.BlockSpec((crops, wide), lambda step, core: (0, 2 * step + core[0]))
@@ -344,7 +358,7 @@
         compiler_params=pltpu.CompilerParams(dimension_semantics=("arbitrary",), vmem_limit_bytes=GRANT),
         cost_estimate=pl.CostEstimate(flops=product // 2, bytes_accessed=2 * matrix + protos * size, transcendentals=0),
     )
-    return energy, rows, cols, student, last, unit_grad, proto_grad
+    return energy, rows, cols, student, last, unit_grad, hidden_grad, proto_grad
 
 
 def summed_protos(keep, give):
@@ -352,12 +366,13 @@
     along_y, along_x = (me // 2) % 4, me // 8
     blocks = (keep.astype(F32) + swapped(give, "dp", 1).astype(F32)).astype(BF16)
     blocks = yield blocks.reshape((2, 4) + keep.shape[1:])
-    total = lax.dynamic_index_in_dim(blocks, along_y, 1, False).astype(F32)
+    terms = [lax.dynamic_index_in_dim(blocks, along_y, 1, False)]
     for step in range(1, 4):
         give = lax.dynamic_index_in_dim(blocks, (along_y + step) % 4, 1, False)
         pairs = [(one, (one & 9) | ((one + 2 * step) & 6)) for one in range(16)]
-        total = total + lax.ppermute(give, "dp", pairs).astype(F32)
-    blocks = yield total.astype(BF16)
+        terms.append(lax.ppermute(give, "dp", pairs))
+    terms = yield terms
+    blocks = sum(term.astype(F32) for term in terms).astype(BF16)
     keep = lax.dynamic_index_in_dim(blocks, along_x, 0, False)
     give = lax.dynamic_index_in_dim(blocks, 1 - along_x, 0, False)
     yield keep.astype(F32) + swapped(give, "dp", 8).astype(F32)
@@ -397,14 +412,9 @@
     proto_unit32, proto_factor = unit_rows(prototypes.astype(F32))
     proto_unit = proto_unit32.astype(BF16)
     protos = proto_unit.shape[0]
-    energy_call, row_call, col_call, student_call, last_call, unit_grad_call, proto_grad_call = make_calls(
-        crops, protos, size, lax.axis_size("dp"), parts
-    )
+    calls = make_calls(crops, protos, size, lax.axis_size("dp"), parts)
+    energy_call, row_call, col_call, student_call, last_call, unit_grad_call, hidden_grad_call, proto_grad_call = calls
     energy, sums = energy_call(teacher_all, proto_unit)
-    for step in range(ITERS - 1):
-        (sums,) = row_call(exchanged(sums, "dp"), energy)
-        (sums,) = col_call(exchanged(sums, "proto"), energy)
-
     values = gathered[:, :crops].astype(F32)
     student_center, student_scale = center_and_scale(
         jnp.sum(values, axis=0)[:, None], jnp.sum(values * values, axis=0)[:, None]
@@ -415,6 +425,20 @@
     )
     student_unit32, student_factor = unit_rows(student_hidden)
     student_unit = student_unit32.astype(BF16)
+    normed = turned.astype(F32) - student_center.reshape(1, crops)
+    normed = (normed * student_scale.reshape(1, crops) * gain_s[:, None]).astype(BF16)
+    student_unit32, student_factor = (
+        lax.dynamic_slice_in_dim(value, lax.axis_index("proto") * own, own, 0)
+        for value in (student_unit32, student_factor)
+    )
+    student = (student_unit, student_unit32, student_factor, normed)
+    for step in range(ITERS - 1):
+        (sums,) = row_call(exchanged(sums, "dp"), energy)
+        sums = exchanged(sums, "proto")
+        if step == ITERS - 2:
+            sums, student = lax.optimization_barrier((sums, student))
+        (sums,) = col_call(sums, energy)
+    student_unit, student_unit32, student_factor, normed = student
     sums, student_unit = lax.optimization_barrier((sums, student_unit))
     exponent, pulled, partition = student_call(student_unit, proto_unit)
     sums = exchanged(sums, "dp")
@@ -430,28 +454,17 @@
     blocks = next(stages)
     crop_loss = swapped(crop_loss, "dp", 8).reshape(1, crops)
     crop_loss = jnp.sum(jnp.where(pick, crop_loss, 0.0), axis=1)
-    student_unit32, student_factor, student_center, student_scale = (
-        lax.dynamic_slice_in_dim(value, lax.axis_index("proto") * own, own, 0)
-        for value in (student_unit32, student_factor, student_center, student_scale)
-    )
-    unit_grad = jnp.sum(unit_grad.astype(F32), axis=0)
-    hidden_grad = student_factor * (
-        unit_grad - student_unit32 * jnp.sum(student_unit32 * unit_grad, axis=1, keepdims=True)
-    )
-    sent = (hidden_grad * student_scale).astype(BF16)
-    moved = jnp.stack(three_terms(jnp.sum(student_center * sent.astype(F32), axis=0)))
-    packed = jnp.concatenate([sent, moved], 0)
-    packed, blocks = lax.optimization_barrier((packed, blocks))
+    unit_grad, blocks = lax.optimization_barrier((unit_grad, blocks))
+    (sent,) = hidden_grad_call(unit_grad, student_unit32, student_factor)
     blocks = stages.send(blocks)
-    packed = from_all(packed, "proto")
-    moved = jnp.sum(packed[:, own:].astype(F32), axis=(0, 1))
-    sent = packed[:, :own].reshape(crops, size)
-    share = (gain_s[:, None] * (jnp.dot(turned, sent, preferred_element_type=F32) - moved[None])).astype(BF16)
-    share, blocks = lax.optimization_barrier((share, blocks))
+    sent = exchanged(sent, "proto").reshape(crops, size)
+    share = jnp.dot(normed, sent, preferred_element_type=F32).astype(BF16)
     near = [[8 * x + other for other in range(8)] for x in range(2)]
     share = lax.all_to_all(jnp.broadcast_to(share[None], (8,) + share.shape), "dp", 0, 0, axis_index_groups=near)
+    share, blocks = lax.optimization_barrier((share, blocks))
+    blocks = stages.send(blocks)
     share = jnp.sum(share.astype(F32), axis=0).astype(BF16)
-    proto_unit_grad = stages.send(blocks).T
+    proto_unit_grad = blocks.T
     grad_proj = share.astype(F32) + swapped(share, "dp", 8).astype(F32)
 
     count = protos // lax.axis_size("dp")

time: 283 us -> 297 us (1.049)
  Pallas kernels: 27.4 us -> 57.6 us
  blocking collectives: 51.1 us -> 27 us
  local copies, waits for them, and re-layouts: 41.2 us -> 21.1 us
  waiting for transfers between devices: 56.1 us -> 71.5 us
  starting transfers between devices: 57.9 us -> 70.9 us
    all_to_all x4 -> x2, blocking collectives: 51.1 us -> 27 us  [exchanged(): return lax.all_to_all(blocks, axis, 0, 0)]
    unnamed x73 -> x34, local copies, waits for them, and re-layouts: 26.8 us -> 4.65 us
    all_to_all x6 -> x8, waiting for transfers between devices: 36.1 us -> 56.8 us  [exchanged(): return lax.all_to_all(blocks, axis, 0, 0)]
    all_to_all x6 -> x8, starting transfers between devices: 36.4 us -> 46.1 us  [exchanged(): return lax.all_to_all(blocks, axis, 0, 0)]
    pallas_call x2 -> x3, Pallas kernels: 3.24 us -> 10.4 us  [the longest x2 8.47 us: body(): sums, = col_call(sums, energy)]
    ppermute x3, waiting for transfers between devices: 14.5 us -> 7.82 us  [summed_protos(): terms.append(lax.ppermute(give, 'dp', pairs))]
    dynamic_slice x4, local copies, waits for them, and re-layouts: 2.13 us -> 8.16 us  [summed_protos(): give = lax.dynamic_index_in_dim(blocks, (along_y + step) % 4, 1, False)]
    pallas_call x2, Pallas kernels: 2.72 us -> 8.13 us  [body(): sums, = row_call(exchanged(sums, 'dp'), energy)]
  transfers between devices with their start and end apart: 16 -> 18, of which waited for: 9 -> 11; matrix products, arithmetic and copies ran while one was open for 13% -> 14% of each run, Pallas kernels for 7% -> 12%
where the time goes in v5:
time: 297 us; the launch traced here: 292 us
  waiting for transfers between devices  71.5 us (24%)
  starting transfers between devices  70.9 us (24%)
  Pallas kernels  57.6 us (19%)
  blocking collectives  27 us (9%)
  other arithmetic  25.7 us (9%)
  local copies, waits for them, and re-layouts  21.1 us (7%)
  between operations  14.4 us (5%)
  matrix products  3.95 us (1%)
    all_to_all x8, waiting for transfers between devices, exchanged(): return lax.all_to_all(blocks, axis, 0, 0)  56.8 us
    all_to_all x8, starting transfers between devices, exchanged(): return lax.all_to_all(blocks, axis, 0, 0)  46.1 us
    all_to_all x2, blocking collectives, exchanged(): return lax.all_to_all(blocks, axis, 0, 0)  27 us
    ppermute x5, starting transfers between devices, swapped(): return lax.ppermute(value, axis, [(one, one ^ bit) for one in range(count)])  12.4 us
    pallas_call x2, Pallas kernels, body(): sums, = col_call(sums, energy)  8.47 us
    pallas_call x1, Pallas kernels, body(): exponent, pulled, partition = student_call(student_unit, proto_unit)  8.26 us
    dynamic_slice x4, local copies, waits for them, and re-layouts, summed_protos(): give = lax.dynamic_index_in_dim(blocks, (along_y + step) % 4, 1, False)  8.16 us
    pallas_call x2, Pallas kernels, body(): sums, = row_call(exchanged(sums, 'dp'), energy)  8.13 us
  transfers between devices with their start and end apart: 18, of which 11 were waited for; matrix products, arithmetic and copies ran while one was open for 14% of the time, Pallas kernels for 12%

profile of v5, /device:TPU:1, one launch (start us, length us, event | category | flops | bytes accessed | tf_op | source)
XLA Modules:
  0.0 292.2 jit_solution(17706962789829867522)
XLA Ops:
  7.2 3.7 %collective-permute-start = (bf16[512,96]{0,1:T(8,128)(2,1)}, bf16[512,96]{0,1:T(8,128)(2,1)S(1)}, u32[]{:S(2)}, u32[]{:S(2)}) collective-permute-start(bf16[512,96]{0,1:T(8,128)(2,1)} %param.8), channel_id=1, source_target_pairs={{0,128},{16,144},{32,160},{48,176},{64,192},{80,208},{96,224},{112... | collective-permute-start | bytes 294920 | tf_op jit(solution)/shard_map/ppermute | solution.py:56
  10.9 0.8 dynamic_slice.35
  11.7 0.8 dynamic_slice.36
  12.4 1.7 fusion.20
  17.2 0.9 convert_reduce_fusion.3
  19.0 1.3 fusion.4
  20.3 0.9 copy.29
  22.6 1.9 fusion.10
  24.5 8.3 %all-to-all-start = ((bf16[16,36,384]{2,1,0:T(8,128)(2,1)}), bf16[16,36,384]{2,1,0:T(8,128)(2,1)}, u32[]{:S(2)}, u32[]{:S(2)}) async-start(bf16[16,36,384]{2,1,0:T(8,128)(2,1)} %fusion.10), calls=%async_computation | async-start | bytes 983040 | tf_op jit(solution)/shard_map/all_to_all | solution.py:38
  33.6 17.0 %all-to-all-done = bf16[16,36,384]{2,1,0:T(8,128)(2,1)} async-done(((bf16[16,36,384]{2,1,0:T(8,128)(2,1)}), bf16[16,36,384]{2,1,0:T(8,128)(2,1)}, u32[]{:S(2)}, u32[]{:S(2)}) %all-to-all-start) | async-done | bytes 442400 | tf_op jit(solution)/shard_map/all_to_all | solution.py:38
  50.5 1.1 convert_reduce_fusion.2
  52.1 0.8 broadcast_in_dim.17
  52.9 7.1 %all-to-all-start.1 = ((bf16[16,32,384]{2,1,0:T(8,128)(2,1)}), bf16[16,32,384]{2,1,0:T(8,128)(2,1)S(1)}, u32[]{:S(2)}, u32[]{:S(2)}) async-start(bf16[16,32,384]{2,1,0:T(8,128)(2,1)} %broadcast_in_dim.17), calls=%async_computation.1 | async-start | bytes 786432 | tf_op jit(solution)/shard_map/all_to_all | solution.py:38
  60.0 2.1 fusion.1.protos_ref
  62.1 13.8 %all-to-all-done.1 = bf16[16,32,384]{2,1,0:T(8,128)(2,1)S(1)} async-done(((bf16[16,32,384]{2,1,0:T(8,128)(2,1)}), bf16[16,32,384]{2,1,0:T(8,128)(2,1)S(1)}, u32[]{:S(2)}, u32[]{:S(2)}) %all-to-all-start.1) | async-done | bytes 393248 | tf_op jit(solution)/shard_map/all_to_all | solution.py:38
  76.7 6.2 %shard_map.111 = (bf16[512,4096]{1,0:T(8,128)(2,1)}, bf16[16,32,128]{2,1,0:T(8,128)(2,1)}) custom-call(bf16[512,384]{1,0:T(8,128)(2,1)} %bitcast.56, bf16[4096,384]{1,0:T(8,128)(2,1)} %fusion.1.protos_ref), custom_call_target="tpu_custom_call" | custom-call | flops 1610612736 | bytes 4194304 | tf_op jit(solution)/shard_map/pallas_call | solution.py:417
  82.8 15.5 %all_to_all.55.got_ref = bf16[16,32,128]{2,1,0:T(8,128)(2,1)} all-to-all(bf16[16,32,128]{2,1,0:T(8,128)(2,1)} %get-tuple-element.36), channel_id=1, replica_groups=mesh['dp'=16,'proto'=16] {'dp'}, dimensions={0} | all-to-all | bytes 262144 | tf_op jit(solution)/shard_map/all_to_all | solution.py:38
  98.4 4.1 %shard_map.112 = f32[16,4,128]{2,1,0:T(4,128)} custom-call(bf16[16,32,128]{2,1,0:T(8,128)(2,1)} %all_to_all.55.got_ref, bf16[512,4096]{1,0:T(8,128)(2,1)} %get-tuple-element.37.energy_ref), custom_call_target="tpu_custom_call" | custom-call | flops 4194304 | bytes 4194304 | tf_op jit(solution)/shard_map/pallas_call | solution.py:436
  102.4 11.5 %all_to_all.56.got_ref = f32[16,4,128]{2,1,0:T(4,128)} all-to-all(f32[16,4,128]{2,1,0:T(4,128)} %shard_map.112), channel_id=1, replica_groups=mesh['dp'=16,'proto'=16] {'proto'}, dimensions={0} | all-to-all | bytes 65536 | tf_op jit(solution)/shard_map/all_to_all | solution.py:38
  113.9 4.2 %shard_map.113 = bf16[16,32,128]{2,1,0:T(8,128)(2,1)} custom-call(f32[16,4,128]{2,1,0:T(4,128)} %all_to_all.56.got_ref, bf16[512,4096]{1,0:T(8,128)(2,1)} %get-tuple-element.37.energy_ref), custom_call_target="tpu_custom_call" | custom-call | flops 4194304 | bytes 4194304 | tf_op jit(solution)/shard_map/pallas_call | solution.py:440
  118.2 5.1 %all-to-all-start.4 = ((bf16[16,32,128]{2,1,0:T(8,128)(2,1)}), bf16[16,32,128]{2,1,0:T(8,128)(2,1)S(1)}, u32[]{:S(2)}, u32[]{:S(2)}) async-start(bf16[16,32,128]{2,1,0:T(8,128)(2,1)} %shard_map.113), calls=%async_computation.4 | async-start | bytes 262144 | tf_op jit(solution)/shard_map/all_to_all | solution.py:38
  123.3 7.7 %all-to-all-done.4.got_ref = bf16[16,32,128]{2,1,0:T(8,128)(2,1)S(1)} async-done(((bf16[16,32,128]{2,1,0:T(8,128)(2,1)}), bf16[16,32,128]{2,1,0:T(8,128)(2,1)S(1)}, u32[]{:S(2)}, u32[]{:S(2)}) %all-to-all-start.4) | async-done | bytes 131104 | tf_op jit(solution)/shard_map/all_to_all | solution.py:38
  131.7 4.1 %shard_map.114 = f32[16,4,128]{2,1,0:T(4,128)} custom-call(bf16[16,32,128]{2,1,0:T(8,128)(2,1)} %copy-done.5, bf16[512,4096]{1,0:T(8,128)(2,1)} %get-tuple-element.37.energy_ref), custom_call_target="tpu_custom_call" | custom-call | flops 4194304 | bytes 4194304 | tf_op jit(solution)/shard_map/pallas_call | solution.py:436
  135.7 3.5 %all-to-all-start.5 = ((f32[16,4,128]{2,1,0:T(4,128)}), f32[16,4,128]{2,1,0:T(4,128)S(1)}, u32[]{:S(2)}, u32[]{:S(2)}) async-start(f32[16,4,128]{2,1,0:T(4,128)} %shard_map.114), calls=%async_computation.5 | async-start | bytes 65536 | tf_op jit(solution)/shard_map/all_to_all | solution.py:38
  139.2 2.0 fusion.2
  142.0 1.5 convert_reduce_fusion.1
  143.5 1.1 multiply_reduce_fusion
  144.6 0.9 fusion.28
  147.1 4.2 %shard_map.115 = bf16[16,32,128]{2,1,0:T(8,128)(2,1)} custom-call(f32[16,4,128]{2,1,0:T(4,128)} %copy-done.9, bf16[512,4096]{1,0:T(8,128)(2,1)} %get-tuple-element.37.energy_ref), custom_call_target="tpu_custom_call" | custom-call | flops 4194304 | bytes 4194304 | tf_op jit(solution)/shard_map/pallas_call | solution.py:440
  151.4 5.1 %all-to-all-start.6 = ((bf16[16,32,128]{2,1,0:T(8,128)(2,1)}), bf16[16,32,128]{2,1,0:T(8,128)(2,1)S(1)}, u32[]{:S(2)}, u32[]{:S(2)}) async-start(bf16[16,32,128]{2,1,0:T(8,128)(2,1)} %shard_map.115), calls=%async_computation.6 | async-start | bytes 262144 | tf_op jit(solution)/shard_map/all_to_all | solution.py:38
  156.5 8.3 %shard_map.116 = (bf16[512,4096]{1,0:T(8,128)(2,1)}, f32[512,384]{1,0:T(8,128)}, f32[4,128]{1,0:T(4,128)}) custom-call(bf16[512,384]{1,0:T(8,128)(2,1)} %get-tuple-element.41.student_ref, bf16[4096,384]{1,0:T(8,128)(2,1)} %fusion.1.protos_ref), custom_call_target="tpu_custom_call" | custom-call | flops 3221225472 | bytes 4194304 | tf_op jit(solution)/shard_map/pallas_call | solution.py:443
  165.4 7.2 %shard_map.117 = (f32[16,12,128]{2,1,0:T(8,128)}, f32[512,384]{1,0:T(8,128)}, f32[32,128]{1,0:T(8,128)}) custom-call(bf16[16,32,128]{2,1,0:T(8,128)(2,1)} %copy-done.4, f32[4,128]{1,0:T(4,128)} %get-tuple-element.46.partition_ref, bf16[512,4096]{1,0:T(8,128)(2,1)} %get-tuple-element.37.energy_ref, bf16[512,384]{1,0:T(8,128)(2,1)} %get-tuple-element.41.student_ref, ...), custom_call_target="tpu_custom_call" | custom-call | flops 1610612736 | bytes 4194304 | tf_op jit(solution)/shard_map/pallas_call | solution.py:446
  172.6 6.4 %all-to-all-start.7 = ((f32[16,12,128]{2,1,0:T(8,128)}), f32[16,12,128]{2,1,0:T(8,128)}, u32[]{:S(2)}, u32[]{:S(2)}) async-start(f32[16,12,128]{2,1,0:T(8,128)} %get-tuple-element.47), calls=%async_computation.7 | async-start | bytes 262144 | tf_op jit(solution)/shard_map/all_to_all | solution.py:38
  179.1 1.0 copy.32.turned_ref
  180.0 6.5 %all-to-all-done.7.got_ref = f32[16,12,128]{2,1,0:T(8,128)} async-done(((f32[16,12,128]{2,1,0:T(8,128)}), f32[16,12,128]{2,1,0:T(8,128)}, u32[]{:S(2)}, u32[]{:S(2)}) %all-to-all-start.7) | async-done | bytes 98336 | tf_op jit(solution)/shard_map/all_to_all | solution.py:38
  186.5 2.6 shard_map.118
  189.1 7.5 %shard_map.119 = bf16[8,384,256]{2,1,0:T(8,128)(2,1)} custom-call(s32[1]{0:T(128)S(6)} %sub.108.core_ref, bf16[384,512]{1,0:T(8,128)(2,1)} %copy.32.turned_ref, f32[512,128]{1,0:T(8,128)} %get-tuple-element.52.wanted_ref, f32[512,128]{1,0:T(8,128)} %get-tuple-element.53.given_ref, f32[32,128]{1,0:T(8,128)} %get-tuple-element.54.scale_ref, ...), custom_call_target="tpu_custom_call" | custom-call | flops 805306368 | bytes 5767168 | tf_op jit(solution)/shard_map/pallas_call | solution.py:450
  196.6 1.8 collective-permute-start.2
  198.4 3.6 %all-to-all-start.8 = ((bf16[16,32,384]{2,1,0:T(8,128)(2,1)}), bf16[16,32,384]{2,1,0:T(8,128)(2,1)S(1)}, u32[]{:S(2)}, u32[]{:S(2)}) async-start(bf16[16,32,384]{2,1,0:T(8,128)(2,1)} %bitcast.55), calls=%async_computation.8 | async-start | bytes 786432 | tf_op jit(solution)/shard_map/all_to_all | solution.py:38
  202.6 7.5 %shard_map.120 = bf16[8,384,256]{2,1,0:T(8,128)(2,1)} custom-call(s32[1]{0:T(128)} %bitcast.11.core_ref, bf16[384,512]{1,0:T(8,128)(2,1)} %copy.32.turned_ref, f32[512,128]{1,0:T(8,128)} %get-tuple-element.52.wanted_ref, f32[512,128]{1,0:T(8,128)} %get-tuple-element.53.given_ref, f32[32,128]{1,0:T(8,128)} %get-tuple-element.54.scale_ref, ...), custom_call_target="tpu_custom_call" | custom-call | flops 805306368 | bytes 5767168 | tf_op jit(solution)/shard_map/pallas_call | solution.py:453
  210.1 3.5 %add_convert_fusion = bf16[8,384,256]{2,1,0:T(8,128)(2,1)} fusion(bf16[8,384,256]{2,1,0:T(8,128)(2,1)} %collective-permute-done.2, bf16[8,384,256]{2,1,0:T(8,128)(2,1)} %shard_map.120), kind=kLoop, calls=%fused_computation.7 | loop fusion | flops 3145728 | bytes 4718592 | tf_op jit(solution)/shard_map/convert_element_type | solution.py:367
  214.8 1.9 shard_map.121
  216.8 7.0 %all-to-all-start.9 = ((bf16[16,32,384]{2,1,0:T(8,128)(2,1)}), bf16[16,32,384]{2,1,0:T(8,128)(2,1)S(1)}, u32[]{:S(2)}, u32[]{:S(2)}) async-start(bf16[16,32,384]{2,1,0:T(8,128)(2,1)} %shard_map.121), calls=%async_computation.9 | async-start | bytes 786432 | tf_op jit(solution)/shard_map/all_to_all | solution.py:38
  223.8 11.0 %all-to-all-done.9 = bf16[16,32,384]{2,1,0:T(8,128)(2,1)S(1)} async-done(((bf16[16,32,384]{2,1,0:T(8,128)(2,1)}), bf16[16,32,384]{2,1,0:T(8,128)(2,1)S(1)}, u32[]{:S(2)}, u32[]{:S(2)}) %all-to-all-start.9) | async-done | bytes 393248 | tf_op jit(solution)/shard_map/all_to_all | solution.py:38
  234.9 1.1 convolution_convert_fusion.2
  236.0 0.9 broadcast_in_dim.21
  236.9 7.4 %all-to-all-start.10 = ((bf16[8,96,384]{2,1,0:T(8,128)(2,1)}), bf16[8,96,384]{2,1,0:T(8,128)(2,1)}, u32[]{:S(2)}, u32[]{:S(2)}) async-start(bf16[8,96,384]{2,1,0:T(8,128)(2,1)} %broadcast_in_dim.21), calls=%async_computation.10 | async-start | bytes 1179648 | tf_op jit(solution)/shard_map/all_to_all | solution.py:463
  244.2 2.4 constant_dynamic-slice_fusion
  246.6 1.9 copy.36
  248.6 1.4 collective-permute-start.3
  249.9 1.9 copy.37
  251.9 2.4 collective-permute-start.4
  254.3 1.9 copy.38
  256.2 1.2 collective-permute-start.5
  257.5 3.4 %collective-permute-start.1 = (f32[4,128]{1,0:T(4,128)S(1)}, f32[4,128]{1,0:T(4,128)S(1)}, u32[]{:S(2)}, u32[]{:S(2)}) collective-permute-start(f32[4,128]{1,0:T(4,128)S(1)} %copy-done.16), channel_id=1, source_target_pairs={{0,128},{16,144},{32,160},{48,176},{64,192},{80,208},{96,224},{112... | collective-permute-start | bytes 6152 | tf_op jit(solution)/shard_map/ppermute | solution.py:56
  260.9 1.0 collective-permute-done.1
  261.9 0.8 select_reduce_fusion
  262.7 0.9 copy.35
  263.6 7.8 %collective-permute-done.4 = bf16[2,384,256]{1,2,0:T(8,128)(2,1)} collective-permute-done((bf16[2,384,256]{1,2,0:T(8,128)(2,1)}, bf16[2,384,256]{1,2,0:T(8,128)(2,1)}, u32[]{:S(2)}, u32[]{:S(2)}) %collective-permute-start.4) | collective-permute-done | bytes 393248 | tf_op jit(solution)/shard_map/ppermute | solution.py:373
  271.5 1.1 reduce_sum.163
  272.6 3.4 %collective-permute-start.6 = (bf16[96,384]{1,0:T(8,128)(2,1)S(1)}, bf16[96,384]{1,0:T(8,128)(2,1)S(1)}, u32[]{:S(2)}, u32[]{:S(2)}) collective-permute-start(bf16[96,384]{1,0:T(8,128)(2,1)S(1)} %reduce_sum.163), channel_id=1, source_target_pairs={{0,128},{16,144},{32,160},{48,176},{64,192},{80,208},{96,224},{112... | collective-permute-start | bytes 221192 | tf_op jit(solution)/shard_map/ppermute | solution.py:56
  276.0 1.6 add_convert_fusion.1
  278.5 5.8 %collective-permute-done.7 = bf16[384,256]{0,1:T(8,128)(2,1)S(1)} collective-permute-done((bf16[384,256]{0,1:T(8,128)(2,1)S(1)}, bf16[384,256]{0,1:T(8,128)(2,1)S(1)}, u32[]{:S(2)}, u32[]{:S(2)}) %collective-permute-start.7) | collective-permute-done | bytes 196640 | tf_op jit(solution)/shard_map/ppermute | solution.py:56
  284.4 0.9 fusion.15
  (82 shorter events, 14.1 us)
Async XLA Ops:
  7.2 25.7 %copy-start = (bf16[4096,384]{1,0:T(8,128)(2,1)S(1)}, bf16[4096,384]{1,0:T(8,128)(2,1)}, u32[]{:S(2)}) copy-start(bf16[4096,384]{1,0:T(8,128)(2,1)} %param.14) | copy-start | bytes 9437188
  7.2 132.1 %all-gather.2.cloned.1.call-start = ((), (), s32[]{:S(2)}) async-start(), calls=%async_computation.11 | async-start | bytes 2924544 | tf_op jit(solution)/shard_map/all_gather | solution.py:410
  7.2 7.6 %collective-permute-start = (bf16[512,96]{0,1:T(8,128)(2,1)}, bf16[512,96]{0,1:T(8,128)(2,1)S(1)}, u32[]{:S(2)}, u32[]{:S(2)}) collective-permute-start(bf16[512,96]{0,1:T(8,128)(2,1)} %param.8), channel_id=1, source_target_pairs={{0,128},{16,144},{32,160},{48,176},{64,192},{80,208},{96,224},{112... | collective-permute-start | bytes 294920 | tf_op jit(solution)/shard_map/ppermute | solution.py:56
  11.7 3.2 %copy-start.15 = (f32[96]{0:T(128)}, f32[96]{0:T(128)S(1)}, u32[]{:S(2)}) copy-start(f32[96]{0:T(128)S(1)} %dynamic_slice.35) | copy-start | bytes 1156
  12.4 2.4 copy-start.13
  14.1 4.3 %copy-start.10 = (f32[384]{0:T(512)}, f32[384]{0:T(512)S(1)}, u32[]{:S(2)}) copy-start(f32[384]{0:T(512)S(1)} %get-tuple-element.79) | copy-start | bytes 4612
  14.8 0.6 copy-start.11
  15.9 0.6 copy-start.7
  24.5 26.0 %all-to-all-start = ((bf16[16,36,384]{2,1,0:T(8,128)(2,1)}), bf16[16,36,384]{2,1,0:T(8,128)(2,1)}, u32[]{:S(2)}, u32[]{:S(2)}) async-start(bf16[16,36,384]{2,1,0:T(8,128)(2,1)} %fusion.10), calls=%async_computation | async-start | bytes 983040 | tf_op jit(solution)/shard_map/all_to_all | solution.py:38
  52.9 23.0 %all-to-all-start.1 = ((bf16[16,32,384]{2,1,0:T(8,128)(2,1)}), bf16[16,32,384]{2,1,0:T(8,128)(2,1)S(1)}, u32[]{:S(2)}, u32[]{:S(2)}) async-start(bf16[16,32,384]{2,1,0:T(8,128)(2,1)} %broadcast_in_dim.17), calls=%async_computation.1 | async-start | bytes 786432 | tf_op jit(solution)/shard_map/all_to_all | solution.py:38
  75.9 0.7 copy-start.6
  118.2 12.8 %all-to-all-start.4 = ((bf16[16,32,128]{2,1,0:T(8,128)(2,1)}), bf16[16,32,128]{2,1,0:T(8,128)(2,1)S(1)}, u32[]{:S(2)}, u32[]{:S(2)}) async-start(bf16[16,32,128]{2,1,0:T(8,128)(2,1)} %shard_map.113), calls=%async_computation.4 | async-start | bytes 262144 | tf_op jit(solution)/shard_map/all_to_all | solution.py:38
  123.3 18.0 %copy-start.8 = (bf16[96,512]{1,0:T(8,128)(2,1)S(1)}, bf16[96,512]{1,0:T(8,128)(2,1)}, u32[]{:S(2)}) copy-start(bf16[96,512]{1,0:T(8,128)(2,1)} %copy-done.7) | copy-start | bytes 294916
  123.3 18.0 %copy-start.14 = (f32[96]{0:T(128)S(1)}, f32[96]{0:T(128)}, u32[]{:S(2)}) copy-start(f32[96]{0:T(128)} %copy-done.13) | copy-start | bytes 1156
  131.0 0.7 copy-start.5
  135.7 10.8 %all-to-all-start.5 = ((f32[16,4,128]{2,1,0:T(4,128)}), f32[16,4,128]{2,1,0:T(4,128)S(1)}, u32[]{:S(2)}, u32[]{:S(2)}) async-start(f32[16,4,128]{2,1,0:T(4,128)} %shard_map.114), calls=%async_computation.5 | async-start | bytes 65536 | tf_op jit(solution)/shard_map/all_to_all | solution.py:38
  139.2 4.3 %copy-start.2 = (bf16[1536,896]{1,0:T(8,128)(2,1)S(1)}, bf16[1536,896]{1,0:T(8,128)(2,1)}, u32[]{:S(2)}) copy-start(bf16[1536,896]{1,0:T(8,128)(2,1)} %all-gather.2.cloned.1.call-done) | copy-start | bytes 8257540
  146.5 0.6 copy-start.9
  151.4 13.4 %all-to-all-start.6 = ((bf16[16,32,128]{2,1,0:T(8,128)(2,1)}), bf16[16,32,128]{2,1,0:T(8,128)(2,1)S(1)}, u32[]{:S(2)}, u32[]{:S(2)}) async-start(bf16[16,32,128]{2,1,0:T(8,128)(2,1)} %shard_map.115), calls=%async_computation.6 | async-start | bytes 262144 | tf_op jit(solution)/shard_map/all_to_all | solution.py:38
  164.8 0.7 copy-start.4
  165.4 13.6 %copy-start.1 = (bf16[512,384]{1,0:T(8,128)(2,1)S(1)}, bf16[512,384]{1,0:T(8,128)(2,1)}, u32[]{:S(2)}) copy-start(bf16[512,384]{1,0:T(8,128)(2,1)} %get-tuple-element.41.student_ref) | copy-start | bytes 1179652
  172.6 13.9 %all-to-all-start.7 = ((f32[16,12,128]{2,1,0:T(8,128)}), f32[16,12,128]{2,1,0:T(8,128)}, u32[]{:S(2)}, u32[]{:S(2)}) async-start(f32[16,12,128]{2,1,0:T(8,128)} %get-tuple-element.47), calls=%async_computation.7 | async-start | bytes 262144 | tf_op jit(solution)/shard_map/all_to_all | solution.py:38
  196.6 13.5 %collective-permute-start.2 = (bf16[8,384,256]{2,1,0:T(8,128)(2,1)}, bf16[8,384,256]{2,1,0:T(8,128)(2,1)}, u32[]{:S(2)}, u32[]{:S(2)}) collective-permute-start(bf16[8,384,256]{2,1,0:T(8,128)(2,1)} %shard_map.119), channel_id=1, source_target_pairs={{0,16},{16,0},{32,48},{48,32},{64,80},{80,64},{96,112},{112,96},{1... | collective-permute-start | bytes 4718600 | tf_op jit(solution)/shard_map/ppermute | solution.py:56
  198.4 15.7 %all-to-all-start.8 = ((bf16[16,32,384]{2,1,0:T(8,128)(2,1)}), bf16[16,32,384]{2,1,0:T(8,128)(2,1)S(1)}, u32[]{:S(2)}, u32[]{:S(2)}) async-start(bf16[16,32,384]{2,1,0:T(8,128)(2,1)} %bitcast.55), calls=%async_computation.8 | async-start | bytes 786432 | tf_op jit(solution)/shard_map/all_to_all | solution.py:38
  214.1 0.7 copy-start.3
  216.8 18.1 %all-to-all-start.9 = ((bf16[16,32,384]{2,1,0:T(8,128)(2,1)}), bf16[16,32,384]{2,1,0:T(8,128)(2,1)S(1)}, u32[]{:S(2)}, u32[]{:S(2)}) async-start(bf16[16,32,384]{2,1,0:T(8,128)(2,1)} %shard_map.121), calls=%async_computation.9 | async-start | bytes 786432 | tf_op jit(solution)/shard_map/all_to_all | solution.py:38
  236.9 34.6 %all-to-all-start.10 = ((bf16[8,96,384]{2,1,0:T(8,128)(2,1)}), bf16[8,96,384]{2,1,0:T(8,128)(2,1)}, u32[]{:S(2)}, u32[]{:S(2)}) async-start(bf16[8,96,384]{2,1,0:T(8,128)(2,1)} %broadcast_in_dim.21), calls=%async_computation.10 | async-start | bytes 1179648 | tf_op jit(solution)/shard_map/all_to_all | solution.py:463
  244.2 13.2 %copy-start.16 = (f32[4,128]{1,0:T(4,128)S(1)}, f32[4,128]{1,0:T(4,128)}, u32[]{:S(2)}) copy-start(f32[4,128]{1,0:T(4,128)} %get-tuple-element.50) | copy-start | bytes 6148
  244.2 17.7 %copy-start.12 = (s32[512]{0:T(512)S(1)}, s32[512]{0:T(512)}, u32[]{:S(2)}) copy-start(s32[512]{0:T(512)} %copy-done.11) | copy-start | bytes 6148
  248.6 15.1 %collective-permute-start.3 = (bf16[2,384,256]{1,2,0:T(8,128)(2,1)}, bf16[2,384,256]{1,2,0:T(8,128)(2,1)}, u32[]{:S(2)}, u32[]{:S(2)}) collective-permute-start(bf16[2,384,256]{1,2,0:T(8,128)(2,1)} %bitcast.52), channel_id=1, source_target_pairs={{0,32},{16,48},{32,64},{48,80},{64,96},{80,112},{96,0},{112,16},{1... | collective-permute-start | bytes 1179656 | tf_op jit(solution)/shard_map/ppermute | solution.py:373
  251.9 19.5 %collective-permute-start.4 = (bf16[2,384,256]{1,2,0:T(8,128)(2,1)}, bf16[2,384,256]{1,2,0:T(8,128)(2,1)}, u32[]{:S(2)}, u32[]{:S(2)}) collective-permute-start(bf16[2,384,256]{1,2,0:T(8,128)(2,1)} %bitcast.53), channel_id=1, source_target_pairs={{0,64},{16,80},{32,96},{48,112},{64,0},{80,16},{96,32},{112,48},{1... | collective-permute-start | bytes 1179656 | tf_op jit(solution)/shard_map/ppermute | solution.py:373
  256.2 15.3 %collective-permute-start.5 = (bf16[2,384,256]{1,2,0:T(8,128)(2,1)}, bf16[2,384,256]{1,2,0:T(8,128)(2,1)}, u32[]{:S(2)}, u32[]{:S(2)}) collective-permute-start(bf16[2,384,256]{1,2,0:T(8,128)(2,1)} %bitcast.54), channel_id=1, source_target_pairs={{0,96},{16,112},{32,0},{48,16},{64,32},{80,48},{96,64},{112,80},{1... | collective-permute-start | bytes 1179656 | tf_op jit(solution)/shard_map/ppermute | solution.py:373
  257.5 4.4 %collective-permute-start.1 = (f32[4,128]{1,0:T(4,128)S(1)}, f32[4,128]{1,0:T(4,128)S(1)}, u32[]{:S(2)}, u32[]{:S(2)}) collective-permute-start(f32[4,128]{1,0:T(4,128)S(1)} %copy-done.16), channel_id=1, source_target_pairs={{0,128},{16,144},{32,160},{48,176},{64,192},{80,208},{96,224},{112... | collective-permute-start | bytes 6152 | tf_op jit(solution)/shard_map/ppermute | solution.py:56
  272.6 5.2 %collective-permute-start.6 = (bf16[96,384]{1,0:T(8,128)(2,1)S(1)}, bf16[96,384]{1,0:T(8,128)(2,1)S(1)}, u32[]{:S(2)}, u32[]{:S(2)}) collective-permute-start(bf16[96,384]{1,0:T(8,128)(2,1)S(1)} %reduce_sum.163), channel_id=1, source_target_pairs={{0,128},{16,144},{32,160},{48,176},{64,192},{80,208},{96,224},{112... | collective-permute-start | bytes 221192 | tf_op jit(solution)/shard_map/ppermute | solution.py:56
  277.6 6.6 %collective-permute-start.7 = (bf16[384,256]{0,1:T(8,128)(2,1)S(1)}, bf16[384,256]{0,1:T(8,128)(2,1)S(1)}, u32[]{:S(2)}, u32[]{:S(2)}) collective-permute-start(bf16[384,256]{0,1:T(8,128)(2,1)S(1)} %dynamic-slice_bitcast_fusion), channel_id=1, source_target_pairs={{0,128},{16,144},{32,160},{48,176},{64,192},{80,208},{96,224},{112... | collective-permute-start | bytes 589832 | tf_op jit(solution)/shard_map/ppermute | solution.py:56
Sparse Core Ops, SparseCore 0:
  17.3 77.1 all-gather.1

commit v6 on v5

--- a/solution.py
+++ b/solution.py
@@ -17,7 +17,7 @@
 F32 = jnp.float32
 LOG2E = 1.4426950408889634
 BLOCK = 1024
-GRANT = 56 * 1024 * 1024
+GRANT = 16 * 1024 * 1024
 LANES = 128
 
 
@@ -222,23 +222,7 @@
             sums_ref[one] = total
 
 
-def unit_grad_kernel(got_ref, pulled_ref, coded_ref, grad_ref, loss_ref, wanted_ref, given_ref):
-    total = stack_sum(got_ref)
-    count = total.shape[0] // 3
-    row = 1.0 / total[:count]
-    partition = total[count : 2 * count]
-    loss_ref[...] = jnp.log(partition) - total[2 * count :] * row
-    wanted = column_form(1.0 / (partition * STUDENT_TEMP))
-    given = column_form(row * (1.0 / STUDENT_TEMP))
-    wanted_ref[...] = wanted
-    given_ref[...] = given
-    for tile in range(pulled_ref.shape[1] // LANES):
-        cut = slice(tile * LANES, (tile + 1) * LANES)
-        grad_ref[:, cut] = (pulled_ref[:, cut] * wanted - coded_ref[:, cut] * given).astype(BF16)
-
-
-def proto_grad_kernel(core_ref, turned_ref, wanted_ref, given_ref, scale_ref, exponent_ref, energy_ref, out_ref):
-    line = pl.program_id(0) * 4 + core_ref[0] * 2
+def proto_block(line, turned_ref, wanted_ref, given_ref, scale_ref, exponent_ref, energy_ref, out_ref):
     parts = []
     for half in range(2):
         cut = slice(half * LANES, half * LANES + LANES)
@@ -246,6 +230,34 @@
         score = exponent_ref[:, cut].astype(F32) * wanted_ref[...] - energy_ref[:, cut].astype(F32) * scale * given_ref[...]
         parts.append(score.astype(BF16))
     out_ref[0] = jnp.dot(turned_ref[...], jnp.concatenate(parts, 1), preferred_element_type=F32).astype(BF16)
+
+
+def unit_grad_kernel(
+    core_ref, got_ref, pulled_ref, coded_ref, turned_ref, scale_ref, exponent_ref, energy_ref,
+    grad_ref, loss_ref, wanted_ref, given_ref, out_ref,
+):
+    @pl.when(pl.program_id(0) == 0)
+    def _():
+        total = stack_sum(got_ref)
+        count = total.shape[0] // 3
+        row = 1.0 / total[:count]
+        partition = total[count : 2 * count]
+        loss_ref[...] = jnp.log(partition) - total[2 * count :] * row
+        wanted = column_form(1.0 / (partition * STUDENT_TEMP))
+        given = column_form(row * (1.0 / STUDENT_TEMP))
+        wanted_ref[...] = wanted
+        given_ref[...] = given
+        for tile in range(pulled_ref.shape[1] // LANES):
+            cut = slice(tile * LANES, (tile + 1) * LANES)
+            grad_ref[:, cut] = (pulled_ref[:, cut] * wanted - coded_ref[:, cut] * given).astype(BF16)
+
+    line = pl.program_id(0) * 4 + core_ref[0] * 2
+    proto_block(line, turned_ref, wanted_ref, given_ref, scale_ref, exponent_ref, energy_ref, out_ref)
+
+
+def proto_grad_kernel(core_ref, turned_ref, wanted_ref, given_ref, scale_ref, exponent_ref, energy_ref, out_ref):
+    line = pl.program_id(0) * 4 + core_ref[0] * 2
+    proto_block(line, turned_ref, wanted_ref, given_ref, scale_ref, exponent_ref, energy_ref, out_ref)
 
 
 def hidden_grad_kernel(got_ref, unit_ref, factor_ref, out_ref):
@@ -321,17 +333,6 @@
         ],
         [tall, pltpu.VMEM((crops, BLOCK), BF16)], product, 2 * matrix,
     )
-    unit_grad = called(
-        unit_grad_kernel, 1,
-        [whole((parts, 3 * lines, LANES)), whole((crops, size)), whole((crops, size))],
-        [
-            (array((crops, size), BF16), whole((crops, size))),
-            (array((lines, LANES), F32), whole((lines, LANES))),
-            (array((crops, LANES), F32), whole((crops, LANES))),
-            (array((crops, LANES), F32), whole((crops, LANES))),
-        ],
-        [], 4 * crops * size, 10 * crops * size,
-    )
     own = crops // parts
     hidden_grad = called(
         hidden_grad_kernel, 1, [whole((parts, own, size)), whole((own, size)), whole((own, 1))],
@@ -339,24 +340,42 @@
     )
     wide = protos // dps
     one = pl.BlockSpec((crops, wide), lambda step, core: (0, 2 * step + core[0]))
+    out = pl.BlockSpec((1, size, wide), lambda step, core: (step, 0, 0))
+    params = pltpu.CompilerParams(dimension_semantics=("arbitrary",), vmem_limit_bytes=GRANT)
+    cost = pl.CostEstimate(flops=product // 2, bytes_accessed=2 * matrix + protos * size, transcendentals=0)
+
+    def fixed(shape):
+        return pl.BlockSpec(shape, lambda step, core: (0,) * len(shape))
+
     proto_grad = pl.pallas_call(
         proto_grad_kernel,
         grid_spec=pltpu.PrefetchScalarGridSpec(
             num_scalar_prefetch=1,
             grid=(dps // 2,),
-            in_specs=[
-                pl.BlockSpec((size, crops), lambda step, core: (0, 0)),
-                pl.BlockSpec((crops, LANES), lambda step, core: (0, 0)),
-                pl.BlockSpec((crops, LANES), lambda step, core: (0, 0)),
-                pl.BlockSpec((tiles, LANES), lambda step, core: (0, 0)),
-                one,
-                one,
-            ],
-            out_specs=pl.BlockSpec((1, size, wide), lambda step, core: (step, 0, 0)),
+            in_specs=[fixed((size, crops)), fixed((crops, LANES)), fixed((crops, LANES)), fixed((tiles, LANES)), one, one],
+            out_specs=out,
         ),
         out_shape=array((dps // 2, size, wide), BF16),
-        compiler_params=pltpu.CompilerParams(dimension_semantics=("arbitrary",), vmem_limit_bytes=GRANT),
-        cost_estimate=pl.CostEstimate(flops=product // 2, bytes_accessed=2 * matrix + protos * size, transcendentals=0),
+        compiler_params=params,
+        cost_estimate=cost,
+    )
+    unit_grad = pl.pallas_call(
+        unit_grad_kernel,
+        grid_spec=pltpu.PrefetchScalarGridSpec(
+            num_scalar_prefetch=1,
+            grid=(dps // 2,),
+            in_specs=[
+                fixed((parts, 3 * lines, LANES)), fixed((crops, size)), fixed((crops, size)),
+                fixed((size, crops)), fixed((tiles, LANES)), one, one,
+            ],
+            out_specs=[fixed((crops, size)), fixed((lines, LANES)), fixed((crops, LANES)), fixed((crops, LANES)), out],
+        ),
+        out_shape=[
+            array((crops, size), BF16), array((lines, LANES), F32), array((crops, LANES), F32),
+            array((crops, LANES), F32), array((dps // 2, size, wide), BF16),
+        ],
+        compiler_params=params,
+        cost_estimate=cost,
     )
     return energy, rows, cols, student, last, unit_grad, hidden_grad, proto_grad
 
@@ -431,38 +450,41 @@
         lax.dynamic_slice_in_dim(value, lax.axis_index("proto") * own, own, 0)
         for value in (student_unit32, student_factor)
     )
-    student = (student_unit, student_unit32, student_factor, normed)
+    student = (student_unit, student_unit32, student_factor, normed, student_unit.T)
     for step in range(ITERS - 1):
-        (sums,) = row_call(exchanged(sums, "dp"), energy)
+        sums = exchanged(sums, "dp")
+        if step == ITERS - 2:
+            sums, student = lax.optimization_barrier((sums, student))
+            student_unit, student_unit32, student_factor, normed, turned_unit = student
+        (sums,) = row_call(sums, energy)
+        if step == ITERS - 2:
+            sums, student_unit = lax.optimization_barrier((sums, student_unit))
+            fields = student_call(student_unit, proto_unit)
         sums = exchanged(sums, "proto")
         if step == ITERS - 2:
-            sums, student = lax.optimization_barrier((sums, student))
+            sums, fields = lax.optimization_barrier((sums, fields))
         (sums,) = col_call(sums, energy)
-    student_unit, student_unit32, student_factor, normed = student
-    sums, student_unit = lax.optimization_barrier((sums, student_unit))
-    exponent, pulled, partition = student_call(student_unit, proto_unit)
+    exponent, pulled, partition = fields
     sums = exchanged(sums, "dp")
-    sums, exponent, pulled, partition = lax.optimization_barrier((sums, exponent, pulled, partition))
     sums, coded, scale = last_call(sums, partition, energy, student_unit, proto_unit)
-    unit_grad, crop_loss, wanted, given = unit_grad_call(exchanged(sums, "proto"), pulled, coded)
     core = (lax.axis_index("dp") % 2).reshape(1)
-    details = (student_unit.T, wanted, given, scale, exponent, energy)
-    give = proto_grad_call(1 - core, *details)
-    give, unit_grad = lax.optimization_barrier((give, unit_grad))
+    unit_grad, crop_loss, wanted, given, give = unit_grad_call(
+        1 - core, exchanged(sums, "proto"), pulled, coded, turned_unit, scale, exponent, energy
+    )
     unit_grad = exchanged(unit_grad.reshape(parts, own, size), "proto")
-    stages = summed_protos(proto_grad_call(core, *details), give)
+    stages = summed_protos(proto_grad_call(core, turned_unit, wanted, given, scale, exponent, energy), give)
     blocks = next(stages)
     crop_loss = swapped(crop_loss, "dp", 8).reshape(1, crops)
     crop_loss = jnp.sum(jnp.where(pick, crop_loss, 0.0), axis=1)
-    unit_grad, blocks = lax.optimization_barrier((unit_grad, blocks))
     (sent,) = hidden_grad_call(unit_grad, student_unit32, student_factor)
+    sent, blocks = lax.optimization_barrier((sent, blocks))
     blocks = stages.send(blocks)
     sent = exchanged(sent, "proto").reshape(crops, size)
     share = jnp.dot(normed, sent, preferred_element_type=F32).astype(BF16)
+    share, blocks = lax.optimization_barrier((share, blocks))
+    blocks = stages.send(blocks)
     near = [[8 * x + other for other in range(8)] for x in range(2)]
     share = lax.all_to_all(jnp.broadcast_to(share[None], (8,) + share.shape), "dp", 0, 0, axis_index_groups=near)
-    share, blocks = lax.optimization_barrier((share, blocks))
-    blocks = stages.send(blocks)
     share = jnp.sum(share.astype(F32), axis=0).astype(BF16)
     proto_unit_grad = blocks.T
     grad_proj = share.astype(F32) + swapped(share, "dp", 8).astype(F32)

time: 297 us -> 285 us (0.960)
  Pallas kernels: 57.6 us -> 31.2 us
  local copies, waits for them, and re-layouts: 21.1 us -> 38.4 us
  starting transfers between devices: 70.9 us -> 63.3 us
  blocking collectives: 27 us -> 30.8 us
  other arithmetic: 25.7 us -> 29.4 us
    unnamed x34 -> x66, local copies, waits for them, and re-layouts: 4.65 us -> 27.4 us
    pallas_call x6 -> x5, Pallas kernels: 33.9 us -> 18.6 us  [the longest x1 5.66 us: body(): fields = student_call(student_unit, proto_unit)]
    dynamic_slice x4, local copies, waits for them, and re-layouts: 8.16 us -> 2.13 us  [summed_protos(): give = lax.dynamic_index_in_dim(blocks, (along_y + step) % 4, 1, False)]
    all_to_all x8, waiting for transfers between devices: 56.8 us -> 52.3 us  [exchanged(): return lax.all_to_all(blocks, axis, 0, 0)]
    all_to_all x2, blocking collectives: 27 us -> 30.8 us  [exchanged(): return lax.all_to_all(blocks, axis, 0, 0)]
    pallas_call x2, Pallas kernels: 8.47 us -> 4.73 us  [body(): sums, = col_call(sums, energy)]
    pallas_call x1, Pallas kernels: 7.2 us -> 3.59 us  [body(): last_call(sums, partition, energy, student_unit, proto_unit)]
    ppermute x3, waiting for transfers between devices: 7.82 us -> 11 us  [summed_protos(): terms.append(lax.ppermute(give, 'dp', pairs))]
  transfers between devices with their start and end apart: 18 -> 18, of which waited for: 11 -> 11; matrix products, arithmetic and copies ran while one was open for 14% -> 14% of each run, Pallas kernels for 12% -> 6%
where the time goes in v6:
time: 285 us; the launch traced here: 283 us
  waiting for transfers between devices  71.2 us (25%)
  starting transfers between devices  63.3 us (22%)
  local copies, waits for them, and re-layouts  38.4 us (13%)
  Pallas kernels  31.2 us (11%)
  blocking collectives  30.8 us (11%)
  other arithmetic  29.4 us (10%)
  between operations  14.6 us (5%)
  matrix products  3.84 us (1%)
    all_to_all x8, waiting for transfers between devices, exchanged(): return lax.all_to_all(blocks, axis, 0, 0)  52.3 us
    all_to_all x8, starting transfers between devices, exchanged(): return lax.all_to_all(blocks, axis, 0, 0)  45.4 us
    all_to_all x2, blocking collectives, exchanged(): return lax.all_to_all(blocks, axis, 0, 0)  30.8 us
    unnamed x66, local copies, waits for them, and re-layouts  27.4 us
    ppermute x3, waiting for transfers between devices, summed_protos(): terms.append(lax.ppermute(give, 'dp', pairs))  11 us
    ppermute x5, starting transfers between devices, swapped(): return lax.ppermute(value, axis, [(one, one ^ bit) for one in range(count)])  9.28 us
    ppermute x5, waiting for transfers between devices, swapped(): return lax.ppermute(value, axis, [(one, one ^ bit) for one in range(count)])  7.92 us
  transfers between devices with their start and end apart: 18, of which 11 were waited for; matrix products, arithmetic and copies ran while one was open for 14% of the time, Pallas kernels for 6%

profile of v6, /device:TPU:1, one launch (start us, length us, event | category | flops | bytes accessed | tf_op | source)
XLA Modules:
  0.0 282.7 jit_solution(14115385161146568939)
XLA Ops:
  7.2 3.7 %collective-permute-start = (bf16[512,96]{0,1:T(8,128)(2,1)}, bf16[512,96]{0,1:T(8,128)(2,1)S(1)}, u32[]{:S(2)}, u32[]{:S(2)}) collective-permute-start(bf16[512,96]{0,1:T(8,128)(2,1)} %param.8), channel_id=1, source_target_pairs={{0,128},{16,144},{32,160},{48,176},{64,192},{80,208},{96,224},{112... | collective-permute-start | bytes 294920 | tf_op jit(solution)/shard_map/ppermute | solution.py:56
  13.0 1.7 fusion.24
  18.9 1.3 fusion.3
  22.6 1.9 fusion.14
  24.4 8.3 %all-to-all-start = ((bf16[16,36,384]{2,1,0:T(8,128)(2,1)}), bf16[16,36,384]{2,1,0:T(8,128)(2,1)}, u32[]{:S(2)}, u32[]{:S(2)}) async-start(bf16[16,36,384]{2,1,0:T(8,128)(2,1)} %fusion.14), calls=%async_computation | async-start | bytes 983040 | tf_op jit(solution)/shard_map/all_to_all | solution.py:38
  33.5 17.4 %all-to-all-done = bf16[16,36,384]{2,1,0:T(8,128)(2,1)} async-done(((bf16[16,36,384]{2,1,0:T(8,128)(2,1)}), bf16[16,36,384]{2,1,0:T(8,128)(2,1)}, u32[]{:S(2)}, u32[]{:S(2)}) %all-to-all-start) | async-done | bytes 442400 | tf_op jit(solution)/shard_map/all_to_all | solution.py:38
  51.0 1.1 convert_reduce_fusion.2
  53.3 6.4 %all-to-all-start.1 = ((bf16[16,32,384]{2,1,0:T(8,128)(2,1)}), bf16[16,32,384]{2,1,0:T(8,128)(2,1)S(1)}, u32[]{:S(2)}, u32[]{:S(2)}) async-start(bf16[16,32,384]{2,1,0:T(8,128)(2,1)} %broadcast_in_dim.17), calls=%async_computation.1 | async-start | bytes 786432 | tf_op jit(solution)/shard_map/all_to_all | solution.py:38
  59.7 2.3 fusion.1.protos_ref
  62.0 12.4 %all-to-all-done.1 = bf16[16,32,384]{2,1,0:T(8,128)(2,1)S(1)} async-done(((bf16[16,32,384]{2,1,0:T(8,128)(2,1)}), bf16[16,32,384]{2,1,0:T(8,128)(2,1)S(1)}, u32[]{:S(2)}, u32[]{:S(2)}) %all-to-all-start.1) | async-done | bytes 393248 | tf_op jit(solution)/shard_map/all_to_all | solution.py:38
  74.4 3.4 %shard_map.111 = (bf16[512,4096]{1,0:T(8,128)(2,1)S(1)}, bf16[16,32,128]{2,1,0:T(8,128)(2,1)S(1)}) custom-call(bf16[512,384]{1,0:T(8,128)(2,1)S(1)} %bitcast.54, bf16[4096,384]{1,0:T(8,128)(2,1)S(1)} %fusion.1.protos_ref), custom_call_target="tpu_custom_call" | custom-call | flops 1610612736 | bytes 4194304 | tf_op jit(solution)/shard_map/pallas_call | solution.py:436
  77.8 16.0 %all_to_all.55.got_ref = bf16[16,32,128]{2,1,0:T(8,128)(2,1)S(1)} all-to-all(bf16[16,32,128]{2,1,0:T(8,128)(2,1)S(1)} %get-tuple-element.36), channel_id=1, replica_groups=mesh['dp'=16,'proto'=16] {'dp'}, dimensions={0} | all-to-all | bytes 262144 | tf_op jit(solution)/shard_map/all_to_all | solution.py:38
  93.8 2.0 shard_map.112
  95.8 1.9 copy-done
  97.7 3.9 %all-to-all-start.3 = ((f32[16,4,128]{2,1,0:T(4,128)}), f32[16,4,128]{2,1,0:T(4,128)S(1)}, u32[]{:S(2)}, u32[]{:S(2)}) async-start(f32[16,4,128]{2,1,0:T(4,128)} %shard_map.112), calls=%async_computation.3 | async-start | bytes 65536 | tf_op jit(solution)/shard_map/all_to_all | solution.py:38
  101.7 7.3 %all-to-all-done.3.got_ref = f32[16,4,128]{2,1,0:T(4,128)S(1)} async-done(((f32[16,4,128]{2,1,0:T(4,128)}), f32[16,4,128]{2,1,0:T(4,128)S(1)}, u32[]{:S(2)}, u32[]{:S(2)}) %all-to-all-start.3) | async-done | bytes 32800 | tf_op jit(solution)/shard_map/all_to_all | solution.py:38
  109.0 2.2 copy-done.1
  111.2 2.3 shard_map.113
  113.5 6.6 %all-to-all-start.4 = ((bf16[16,32,128]{2,1,0:T(8,128)(2,1)}), bf16[16,32,128]{2,1,0:T(8,128)(2,1)}, u32[]{:S(2)}, u32[]{:S(2)}) async-start(bf16[16,32,128]{2,1,0:T(8,128)(2,1)} %shard_map.113), calls=%async_computation.4 | async-start | bytes 262144 | tf_op jit(solution)/shard_map/all_to_all | solution.py:38
  120.1 2.0 fusion.2
  122.8 1.5 convert_reduce_fusion.1
  124.3 1.9 multiply_reduce_fusion
  126.2 2.3 copy.30
  128.6 2.2 fusion.32
  130.7 1.3 fusion.11.turned_ref
  133.3 2.2 copy-done.2
  135.5 2.2 shard_map.114
  138.3 4.2 %all-to-all-start.5 = ((f32[16,4,128]{2,1,0:T(4,128)}), f32[16,4,128]{2,1,0:T(4,128)}, u32[]{:S(2)}, u32[]{:S(2)}) async-start(f32[16,4,128]{2,1,0:T(4,128)} %copy-done.17), calls=%async_computation.5 | async-start | bytes 65536 | tf_op jit(solution)/shard_map/all_to_all | solution.py:38
  143.5 5.7 %shard_map.115 = (bf16[512,4096]{1,0:T(8,128)(2,1)S(1)}, f32[512,384]{1,0:T(8,128)S(1)}, f32[4,128]{1,0:T(4,128)S(1)}) custom-call(bf16[512,384]{1,0:T(8,128)(2,1)S(1)} %copy-done.10, bf16[4096,384]{1,0:T(8,128)(2,1)S(1)} %fusion.1.protos_ref), custom_call_target="tpu_custom_call" | custom-call | flops 3221225472 | bytes 4194304 | tf_op jit(solution)/shard_map/pallas_call | solution.py:462
  149.1 2.0 copy-done.7
  152.7 2.2 copy-done.3
  154.9 2.5 shard_map.116
  157.3 14.7 %all_to_all.56.got_ref = bf16[16,32,128]{2,1,0:T(8,128)(2,1)S(1)} all-to-all(bf16[16,32,128]{2,1,0:T(8,128)(2,1)S(1)} %shard_map.116), channel_id=1, replica_groups=mesh['dp'=16,'proto'=16] {'dp'}, dimensions={0} | all-to-all | bytes 262144 | tf_op jit(solution)/shard_map/all_to_all | solution.py:38
  172.1 3.6 %shard_map.117 = (f32[16,12,128]{2,1,0:T(8,128)S(1)}, f32[512,384]{1,0:T(8,128)S(1)}, f32[32,128]{1,0:T(8,128)S(1)}) custom-call(bf16[16,32,128]{2,1,0:T(8,128)(2,1)S(1)} %all_to_all.56.got_ref, f32[4,128]{1,0:T(4,128)S(1)} %copy-done.20, bf16[512,4096]{1,0:T(8,128)(2,1)S(1)} %copy-done.4, bf16[512,384]{1,0:T(8,128)(2,1)S(1)} %copy-done.11, ...), custom_call_target="tpu_custom_call" | custom-call | flops 1610612736 | bytes 4194304 | tf_op jit(solution)/shard_map/pallas_call | solution.py:469
  177.2 7.1 %all-to-all-start.7 = ((f32[16,12,128]{2,1,0:T(8,128)}), f32[16,12,128]{2,1,0:T(8,128)S(1)}, u32[]{:S(2)}, u32[]{:S(2)}) async-start(f32[16,12,128]{2,1,0:T(8,128)} %copy-done.18), calls=%async_computation.7 | async-start | bytes 262144 | tf_op jit(solution)/shard_map/all_to_all | solution.py:38
  184.4 7.4 %all-to-all-done.7.got_ref = f32[16,12,128]{2,1,0:T(8,128)S(1)} async-done(((f32[16,12,128]{2,1,0:T(8,128)}), f32[16,12,128]{2,1,0:T(8,128)S(1)}, u32[]{:S(2)}, u32[]{:S(2)}) %all-to-all-start.7) | async-done | bytes 98336 | tf_op jit(solution)/shard_map/all_to_all | solution.py:38
  191.8 2.2 copy-done.5
  194.0 2.2 copy-done.8
  196.2 1.1 copy-done.13
  197.3 1.1 copy-done.15
  198.4 5.3 %shard_map.118 = (bf16[512,384]{1,0:T(8,128)(2,1)}, f32[4,128]{1,0:T(4,128)S(1)}, f32[512,128]{1,0:T(8,128)S(1)}, f32[512,128]{1,0:T(8,128)S(1)}, bf16[8,384,256]{2,1,0:T(8,128)(2,1)}) custom-call(s32[1]{0:T(128)S(6)} %sub.101.core_ref, f32[16,12,128]{2,1,0:T(8,128)S(1)} %all-to-all-done.7.got_ref, f32[512,384]{1,0:T(8,128)S(1)} %copy-done.13, ...), custom_call_target="tpu_custom_call" | custom-call | flops 805306368 | bytes 5767168 | tf_op jit(solution)/shard_map/pallas_call | solution.py:471
  203.7 2.1 collective-permute-start.2
  205.8 3.6 %all-to-all-start.8 = ((bf16[16,32,384]{2,1,0:T(8,128)(2,1)}), bf16[16,32,384]{2,1,0:T(8,128)(2,1)S(1)}, u32[]{:S(2)}, u32[]{:S(2)}) async-start(bf16[16,32,384]{2,1,0:T(8,128)(2,1)} %bitcast.13), calls=%async_computation.8 | async-start | bytes 786432 | tf_op jit(solution)/shard_map/all_to_all | solution.py:38
  209.4 2.2 copy-done.6
  211.6 2.2 copy-done.9
  213.8 3.5 %shard_map.120 = bf16[8,384,256]{2,1,0:T(8,128)(2,1)S(1)} custom-call(s32[1]{0:T(128)} %bitcast.core_ref, bf16[384,512]{1,0:T(8,128)(2,1)S(1)} %fusion.11.turned_ref, f32[512,128]{1,0:T(8,128)S(1)} %get-tuple-element.58.wanted_ref, f32[512,128]{1,0:T(8,128)S(1)} %get-tuple-element.59.given_ref, f32[32,128]{1,0:T(8,128)S(1)} %get-tuple-element.51.scale_ref, ...), custom_call_target="tpu_custom_call" | custom-call | flops 805306368 | bytes 5767168 | tf_op jit(solution)/shard_map/pallas_call | solution.py:475
  217.4 4.2 %all-to-all-done.8.got_ref = bf16[16,32,384]{2,1,0:T(8,128)(2,1)S(1)} async-done(((bf16[16,32,384]{2,1,0:T(8,128)(2,1)}), bf16[16,32,384]{2,1,0:T(8,128)(2,1)S(1)}, u32[]{:S(2)}, u32[]{:S(2)}) %all-to-all-start.8) | async-done | bytes 393248 | tf_op jit(solution)/shard_map/all_to_all | solution.py:38
  222.4 3.0 %add_convert_fusion = bf16[8,384,256]{2,1,0:T(8,128)(2,1)} fusion(bf16[8,384,256]{2,1,0:T(8,128)(2,1)} %collective-permute-done.2, bf16[8,384,256]{2,1,0:T(8,128)(2,1)S(1)} %shard_map.120), kind=kLoop, calls=%fused_computation.7 | loop fusion | flops 3145728 | bytes 4718592 | tf_op jit(solution)/shard_map/convert_element_type | solution.py:386
  225.4 5.4 %all-to-all-start.9 = ((bf16[16,32,384]{2,1,0:T(8,128)(2,1)}), bf16[16,32,384]{2,1,0:T(8,128)(2,1)S(1)}, u32[]{:S(2)}, u32[]{:S(2)}) async-start(bf16[16,32,384]{2,1,0:T(8,128)(2,1)} %shard_map.119), calls=%async_computation.9 | async-start | bytes 786432 | tf_op jit(solution)/shard_map/all_to_all | solution.py:38
  230.9 1.5 constant_dynamic-slice_fusion
  232.9 2.2 collective-permute-start.4
  237.1 1.2 collective-permute-start.1
  238.5 3.5 %all-to-all-done.9 = bf16[16,32,384]{2,1,0:T(8,128)(2,1)S(1)} async-done(((bf16[16,32,384]{2,1,0:T(8,128)(2,1)}), bf16[16,32,384]{2,1,0:T(8,128)(2,1)S(1)}, u32[]{:S(2)}, u32[]{:S(2)}) %all-to-all-start.9) | async-done | bytes 393248 | tf_op jit(solution)/shard_map/all_to_all | solution.py:38
  242.2 2.1 collective-permute-done.3
  244.3 7.5 %collective-permute-done.4 = bf16[2,384,256]{1,2,0:T(8,128)(2,1)} collective-permute-done((bf16[2,384,256]{1,2,0:T(8,128)(2,1)S(1)}, bf16[2,384,256]{1,2,0:T(8,128)(2,1)}, u32[]{:S(2)}, u32[]{:S(2)}) %collective-permute-start.4) | collective-permute-done | bytes 393248 | tf_op jit(solution)/shard_map/ppermute | solution.py:392
  251.8 1.4 collective-permute-done.5
  254.1 5.6 %all-to-all-start.10 = ((bf16[8,96,384]{2,1,0:T(8,128)(2,1)}), bf16[8,96,384]{2,1,0:T(8,128)(2,1)S(1)}, u32[]{:S(2)}, u32[]{:S(2)}) async-start(bf16[8,96,384]{2,1,0:T(8,128)(2,1)} %broadcast_in_dim.21), calls=%async_computation.10 | async-start | bytes 1179648 | tf_op jit(solution)/shard_map/all_to_all | solution.py:487
  259.7 1.3 add_convert_fusion.1
  261.1 1.2 collective-permute-start.7
  263.1 6.1 %collective-permute-done.7 = bf16[384,256]{0,1:T(8,128)(2,1)S(1)} collective-permute-done((bf16[384,256]{0,1:T(8,128)(2,1)S(1)}, bf16[384,256]{0,1:T(8,128)(2,1)S(1)}, u32[]{:S(2)}, u32[]{:S(2)}) %collective-permute-start.7) | collective-permute-done | bytes 196640 | tf_op jit(solution)/shard_map/ppermute | solution.py:56
  269.2 1.1 fusion.17
  270.4 1.2 collective-permute-start.6
  271.6 1.8 fusion.19
  273.4 1.8 collective-permute-done.6
  (114 shorter events, 23.7 us)
Async XLA Ops:
  7.2 25.6 %copy-start.21 = (bf16[4096,384]{1,0:T(8,128)(2,1)S(1)}, bf16[4096,384]{1,0:T(8,128)(2,1)}, u32[]{:S(2)}) copy-start(bf16[4096,384]{1,0:T(8,128)(2,1)} %param.14) | copy-start | bytes 9437188
  7.2 112.9 %all-gather.2.cloned.1.call-start = ((), (), s32[]{:S(2)}) async-start(), calls=%async_computation.11 | async-start | bytes 2924544 | tf_op jit(solution)/shard_map/all_gather | solution.py:429
  7.2 8.2 %collective-permute-start = (bf16[512,96]{0,1:T(8,128)(2,1)}, bf16[512,96]{0,1:T(8,128)(2,1)S(1)}, u32[]{:S(2)}, u32[]{:S(2)}) collective-permute-start(bf16[512,96]{0,1:T(8,128)(2,1)} %param.8), channel_id=1, source_target_pairs={{0,128},{16,144},{32,160},{48,176},{64,192},{80,208},{96,224},{112... | collective-permute-start | bytes 294920 | tf_op jit(solution)/shard_map/ppermute | solution.py:56
  11.7 5.5 %copy-start.31 = (f32[96]{0:T(128)}, f32[96]{0:T(128)S(1)}, u32[]{:S(2)}) copy-start(f32[96]{0:T(128)S(1)} %dynamic_slice.35) | copy-start | bytes 1156
  12.4 0.5 copy-start.29
  14.7 3.7 %copy-start.26 = (f32[384]{0:T(512)}, f32[384]{0:T(512)S(1)}, u32[]{:S(2)}) copy-start(f32[384]{0:T(512)S(1)} %get-tuple-element.79) | copy-start | bytes 4612
  15.4 1.8 copy-start.27
  15.8 0.6 copy-start.23
  24.4 26.5 %all-to-all-start = ((bf16[16,36,384]{2,1,0:T(8,128)(2,1)}), bf16[16,36,384]{2,1,0:T(8,128)(2,1)}, u32[]{:S(2)}, u32[]{:S(2)}) async-start(bf16[16,36,384]{2,1,0:T(8,128)(2,1)} %fusion.14), calls=%async_computation | async-start | bytes 983040 | tf_op jit(solution)/shard_map/all_to_all | solution.py:38
  53.3 21.1 %all-to-all-start.1 = ((bf16[16,32,384]{2,1,0:T(8,128)(2,1)}), bf16[16,32,384]{2,1,0:T(8,128)(2,1)S(1)}, u32[]{:S(2)}, u32[]{:S(2)}) async-start(bf16[16,32,384]{2,1,0:T(8,128)(2,1)} %broadcast_in_dim.17), calls=%async_computation.1 | async-start | bytes 786432 | tf_op jit(solution)/shard_map/all_to_all | solution.py:38
  95.8 1.9 copy-start
  97.7 11.3 %all-to-all-start.3 = ((f32[16,4,128]{2,1,0:T(4,128)}), f32[16,4,128]{2,1,0:T(4,128)S(1)}, u32[]{:S(2)}, u32[]{:S(2)}) async-start(f32[16,4,128]{2,1,0:T(4,128)} %shard_map.112), calls=%async_computation.3 | async-start | bytes 65536 | tf_op jit(solution)/shard_map/all_to_all | solution.py:38
  109.0 2.2 copy-start.1
  111.2 10.9 %copy-start.24 = (bf16[96,512]{1,0:T(8,128)(2,1)S(1)}, bf16[96,512]{1,0:T(8,128)(2,1)}, u32[]{:S(2)}) copy-start(bf16[96,512]{1,0:T(8,128)(2,1)} %copy-done.23) | copy-start | bytes 294916
  111.2 10.9 %copy-start.30 = (f32[96]{0:T(128)S(1)}, f32[96]{0:T(128)}, u32[]{:S(2)}) copy-start(f32[96]{0:T(128)} %copy-done.29) | copy-start | bytes 1156
  113.5 19.8 %all-to-all-start.4 = ((bf16[16,32,128]{2,1,0:T(8,128)(2,1)}), bf16[16,32,128]{2,1,0:T(8,128)(2,1)}, u32[]{:S(2)}, u32[]{:S(2)}) async-start(bf16[16,32,128]{2,1,0:T(8,128)(2,1)} %shard_map.113), calls=%async_computation.4 | async-start | bytes 262144 | tf_op jit(solution)/shard_map/all_to_all | solution.py:38
  120.0 4.3 %copy-start.22 = (bf16[1536,896]{1,0:T(8,128)(2,1)S(1)}, bf16[1536,896]{1,0:T(8,128)(2,1)}, u32[]{:S(2)}) copy-start(bf16[1536,896]{1,0:T(8,128)(2,1)} %all-gather.2.cloned.1.call-done) | copy-start | bytes 8257540
  133.3 2.2 copy-start.2
  137.7 0.6 copy-start.17
  138.3 14.4 %all-to-all-start.5 = ((f32[16,4,128]{2,1,0:T(4,128)}), f32[16,4,128]{2,1,0:T(4,128)}, u32[]{:S(2)}, u32[]{:S(2)}) async-start(f32[16,4,128]{2,1,0:T(4,128)} %copy-done.17), calls=%async_computation.5 | async-start | bytes 65536 | tf_op jit(solution)/shard_map/all_to_all | solution.py:38
  142.5 1.0 copy-start.10
  149.1 2.0 copy-start.7
  151.1 1.0 copy-start.12
  152.1 0.6 copy-start.19
  152.7 19.4 %copy-start.20 = (f32[4,128]{1,0:T(4,128)S(1)}, f32[4,128]{1,0:T(4,128)}, u32[]{:S(2)}) copy-start(f32[4,128]{1,0:T(4,128)} %copy-done.19) | copy-start | bytes 6148
  152.7 2.2 copy-start.3
  154.9 17.2 %copy-start.4 = (bf16[512,4096]{1,0:T(8,128)(2,1)S(1)}, bf16[512,4096]{1,0:T(8,128)(2,1)}, u32[]{:S(2)}) copy-start(bf16[512,4096]{1,0:T(8,128)(2,1)} %copy-done) | copy-start | bytes 12582916
  154.9 17.2 %copy-start.11 = (bf16[512,384]{1,0:T(8,128)(2,1)S(1)}, bf16[512,384]{1,0:T(8,128)(2,1)}, u32[]{:S(2)}) copy-start(bf16[512,384]{1,0:T(8,128)(2,1)} %get-tuple-element.41.student_ref) | copy-start | bytes 1179652
  175.7 0.9 copy-start.14
  176.6 0.7 copy-start.18
  177.2 14.6 %all-to-all-start.7 = ((f32[16,12,128]{2,1,0:T(8,128)}), f32[16,12,128]{2,1,0:T(8,128)S(1)}, u32[]{:S(2)}, u32[]{:S(2)}) async-start(f32[16,12,128]{2,1,0:T(8,128)} %copy-done.18), calls=%async_computation.7 | async-start | bytes 262144 | tf_op jit(solution)/shard_map/all_to_all | solution.py:38
  191.8 2.2 copy-start.5
  194.0 2.2 copy-start.8
  196.2 1.1 copy-start.13
  197.3 1.1 copy-start.15
  198.4 10.9 %copy-start.32 = (f32[32,1]{0,1:T(1,128)S(1)}, f32[32,1]{0,1:T(1,128)}, u32[]{:S(2)}) copy-start(f32[32,1]{0,1:T(1,128)} %dynamic-slice_bitcast_fusion.1) | copy-start | bytes 388
  203.7 18.7 %collective-permute-start.2 = (bf16[8,384,256]{2,1,0:T(8,128)(2,1)}, bf16[8,384,256]{2,1,0:T(8,128)(2,1)}, u32[]{:S(2)}, u32[]{:S(2)}) collective-permute-start(bf16[8,384,256]{2,1,0:T(8,128)(2,1)} %get-tuple-element.60), channel_id=1, source_target_pairs={{0,16},{16,0},{32,48},{48,32},{64,80},{80,64},{96,112},{112,96},{1... | collective-permute-start | bytes 4718600 | tf_op jit(solution)/shard_map/ppermute | solution.py:56
  205.8 15.7 %all-to-all-start.8 = ((bf16[16,32,384]{2,1,0:T(8,128)(2,1)}), bf16[16,32,384]{2,1,0:T(8,128)(2,1)S(1)}, u32[]{:S(2)}, u32[]{:S(2)}) async-start(bf16[16,32,384]{2,1,0:T(8,128)(2,1)} %bitcast.13), calls=%async_computation.8 | async-start | bytes 786432 | tf_op jit(solution)/shard_map/all_to_all | solution.py:38
  209.4 2.2 copy-start.6
  211.6 2.2 copy-start.9
  213.8 7.7 %copy-start.16 = (f32[32,384]{1,0:T(8,128)S(1)}, f32[32,384]{1,0:T(8,128)}, u32[]{:S(2)}) copy-start(f32[32,384]{1,0:T(8,128)} %constant_dynamic-slice_fusion.4.unit_ref) | copy-start | bytes 147460
  225.4 16.6 %all-to-all-start.9 = ((bf16[16,32,384]{2,1,0:T(8,128)(2,1)}), bf16[16,32,384]{2,1,0:T(8,128)(2,1)S(1)}, u32[]{:S(2)}, u32[]{:S(2)}) async-start(bf16[16,32,384]{2,1,0:T(8,128)(2,1)} %shard_map.119), calls=%async_computation.9 | async-start | bytes 786432 | tf_op jit(solution)/shard_map/all_to_all | solution.py:38
  230.9 11.1 %copy-start.25 = (bf16[96,512]{1,0:T(8,128)(2,1)S(1)}, bf16[96,512]{1,0:T(8,128)(2,1)}, u32[]{:S(2)}) copy-start(bf16[96,512]{1,0:T(8,128)(2,1)} %multiply_convert_fusion) | copy-start | bytes 294916
  232.6 11.7 %collective-permute-start.3 = (bf16[2,384,256]{1,2,0:T(8,128)(2,1)S(1)}, bf16[2,384,256]{1,2,0:T(8,128)(2,1)S(1)}, u32[]{:S(2)}, u32[]{:S(2)}) collective-permute-start(bf16[2,384,256]{1,2,0:T(8,128)(2,1)S(1)} %bitcast.59), channel_id=1, source_target_pairs={{0,32},{16,48},{32,64},{48,80},{64,96},{80,112},{96,0},{112,16},{1... | collective-permute-start | bytes 1179656 | tf_op jit(solution)/shard_map/ppermute | solution.py:392
  232.9 18.9 %collective-permute-start.4 = (bf16[2,384,256]{1,2,0:T(8,128)(2,1)S(1)}, bf16[2,384,256]{1,2,0:T(8,128)(2,1)}, u32[]{:S(2)}, u32[]{:S(2)}) collective-permute-start(bf16[2,384,256]{1,2,0:T(8,128)(2,1)S(1)} %bitcast.60), channel_id=1, source_target_pairs={{0,64},{16,80},{32,96},{48,112},{64,0},{80,16},{96,32},{112,48},{1... | collective-permute-start | bytes 1179656 | tf_op jit(solution)/shard_map/ppermute | solution.py:392
  235.3 17.9 %collective-permute-start.5 = (bf16[2,384,256]{1,2,0:T(8,128)(2,1)S(1)}, bf16[2,384,256]{1,2,0:T(8,128)(2,1)}, u32[]{:S(2)}, u32[]{:S(2)}) collective-permute-start(bf16[2,384,256]{1,2,0:T(8,128)(2,1)S(1)} %bitcast.61), channel_id=1, source_target_pairs={{0,96},{16,112},{32,0},{48,16},{64,32},{80,48},{96,64},{112,80},{1... | collective-permute-start | bytes 1179656 | tf_op jit(solution)/shard_map/ppermute | solution.py:392
  237.1 25.1 %collective-permute-start.1 = (f32[4,128]{1,0:T(4,128)S(1)}, f32[4,128]{1,0:T(4,128)S(1)}, u32[]{:S(2)}, u32[]{:S(2)}) collective-permute-start(f32[4,128]{1,0:T(4,128)S(1)} %get-tuple-element.53), channel_id=1, source_target_pairs={{0,128},{16,144},{32,160},{48,176},{64,192},{80,208},{96,224},{112... | collective-permute-start | bytes 6152 | tf_op jit(solution)/shard_map/ppermute | solution.py:56
  238.3 23.9 %copy-start.28 = (s32[512]{0:T(512)S(1)}, s32[512]{0:T(512)}, u32[]{:S(2)}) copy-start(s32[512]{0:T(512)} %copy-done.27) | copy-start | bytes 6148
  254.1 16.2 %all-to-all-start.10 = ((bf16[8,96,384]{2,1,0:T(8,128)(2,1)}), bf16[8,96,384]{2,1,0:T(8,128)(2,1)S(1)}, u32[]{:S(2)}, u32[]{:S(2)}) async-start(bf16[8,96,384]{2,1,0:T(8,128)(2,1)} %broadcast_in_dim.21), calls=%async_computation.10 | async-start | bytes 1179648 | tf_op jit(solution)/shard_map/all_to_all | solution.py:487
  261.1 8.1 %collective-permute-start.7 = (bf16[384,256]{0,1:T(8,128)(2,1)S(1)}, bf16[384,256]{0,1:T(8,128)(2,1)S(1)}, u32[]{:S(2)}, u32[]{:S(2)}) collective-permute-start(bf16[384,256]{0,1:T(8,128)(2,1)S(1)} %dynamic-slice_bitcast_fusion), channel_id=1, source_target_pairs={{0,128},{16,144},{32,160},{48,176},{64,192},{80,208},{96,224},{112... | collective-permute-start | bytes 589832 | tf_op jit(solution)/shard_map/ppermute | solution.py:56
  270.4 4.8 %collective-permute-start.6 = (bf16[96,384]{1,0:T(8,128)(2,1)S(1)}, bf16[96,384]{1,0:T(8,128)(2,1)S(1)}, u32[]{:S(2)}, u32[]{:S(2)}) collective-permute-start(bf16[96,384]{1,0:T(8,128)(2,1)S(1)} %reduce_sum.163), channel_id=1, source_target_pairs={{0,128},{16,144},{32,160},{48,176},{64,192},{80,208},{96,224},{112... | collective-permute-start | bytes 221192 | tf_op jit(solution)/shard_map/ppermute | solution.py:56
Sparse Core Ops, SparseCore 0:
  17.3 78.9 all-gather.1

commit v7 on v6

--- a/solution.py
+++ b/solution.py
@@ -222,14 +222,14 @@
             sums_ref[one] = total
 
 
-def proto_block(line, turned_ref, wanted_ref, given_ref, scale_ref, exponent_ref, energy_ref, out_ref):
+def proto_block(line, turned_ref, wanted_ref, given_ref, scale_ref, exponent_ref, energy_ref):
     parts = []
     for half in range(2):
         cut = slice(half * LANES, half * LANES + LANES)
         scale = scale_ref[pl.ds(line + half, 1), :]
         score = exponent_ref[:, cut].astype(F32) * wanted_ref[...] - energy_ref[:, cut].astype(F32) * scale * given_ref[...]
         parts.append(score.astype(BF16))
-    out_ref[0] = jnp.dot(turned_ref[...], jnp.concatenate(parts, 1), preferred_element_type=F32).astype(BF16)
+    return jnp.dot(turned_ref[...], jnp.concatenate(parts, 1), preferred_element_type=F32)
 
 
 def unit_grad_kernel(
@@ -252,12 +252,23 @@
             grad_ref[:, cut] = (pulled_ref[:, cut] * wanted - coded_ref[:, cut] * given).astype(BF16)
 
     line = pl.program_id(0) * 4 + core_ref[0] * 2
-    proto_block(line, turned_ref, wanted_ref, given_ref, scale_ref, exponent_ref, energy_ref, out_ref)
+    value = proto_block(line, turned_ref, wanted_ref, given_ref, scale_ref, exponent_ref, energy_ref)
+    out_ref[0] = value.astype(BF16)
 
 
 def proto_grad_kernel(core_ref, turned_ref, wanted_ref, given_ref, scale_ref, exponent_ref, energy_ref, out_ref):
     line = pl.program_id(0) * 4 + core_ref[0] * 2
-    proto_block(line, turned_ref, wanted_ref, given_ref, scale_ref, exponent_ref, energy_ref, out_ref)
+    value = proto_block(line, turned_ref, wanted_ref, given_ref, scale_ref, exponent_ref, energy_ref)
+    out_ref[0] = value.astype(BF16)
+
+
+def pair_sum_kernel(place_ref, kept_ref, got_ref, *out_refs):
+    value = (kept_ref[:, 0].astype(F32) + got_ref[:, 0].astype(F32)).astype(BF16)
+    for turn, out_ref in enumerate(out_refs):
+
+        @pl.when(pl.program_id(0) == turn)
+        def _():
+            out_ref[...] = value
 
 
 def hidden_grad_kernel(got_ref, unit_ref, factor_ref, out_ref):
@@ -358,6 +369,19 @@
         out_shape=array((dps // 2, size, wide), BF16),
         compiler_params=params,
         cost_estimate=cost,
+    )
+    turned = pl.BlockSpec((2, 1, size, wide), lambda step, place: (0, (place[0] + step) % 4, 0, 0))
+    pair_sum = pl.pallas_call(
+        pair_sum_kernel,
+        grid_spec=pltpu.PrefetchScalarGridSpec(
+            num_scalar_prefetch=1,
+            grid=(4,),
+            in_specs=[turned, turned],
+            out_specs=[fixed((2, size, wide)) for _ in range(4)],
+        ),
+        out_shape=[array((2, size, wide), BF16) for _ in range(4)],
+        compiler_params=params,
+        cost_estimate=pl.CostEstimate(flops=protos * size, bytes_accessed=3 * protos * size, transcendentals=0),
     )
     unit_grad = pl.pallas_call(
         unit_grad_kernel,
@@ -377,24 +401,11 @@
         compiler_params=params,
         cost_estimate=cost,
     )
-    return energy, rows, cols, student, last, unit_grad, hidden_grad, proto_grad
-
-
-def summed_protos(keep, give):
-    me = lax.axis_index("dp")
-    along_y, along_x = (me // 2) % 4, me // 8
-    blocks = (keep.astype(F32) + swapped(give, "dp", 1).astype(F32)).astype(BF16)
-    blocks = yield blocks.reshape((2, 4) + keep.shape[1:])
-    terms = [lax.dynamic_index_in_dim(blocks, along_y, 1, False)]
-    for step in range(1, 4):
-        give = lax.dynamic_index_in_dim(blocks, (along_y + step) % 4, 1, False)
-        pairs = [(one, (one & 9) | ((one + 2 * step) & 6)) for one in range(16)]
-        terms.append(lax.ppermute(give, "dp", pairs))
-    terms = yield terms
-    blocks = sum(term.astype(F32) for term in terms).astype(BF16)
-    keep = lax.dynamic_index_in_dim(blocks, along_x, 0, False)
-    give = lax.dynamic_index_in_dim(blocks, 1 - along_x, 0, False)
-    yield keep.astype(F32) + swapped(give, "dp", 8).astype(F32)
+    return energy, rows, cols, student, last, unit_grad, hidden_grad, proto_grad, pair_sum
+
+
+def along_y(value, step):
+    return lax.ppermute(value, "dp", [(one, (one & 9) | ((one + 2 * step) & 6)) for one in range(16)])
 
 
 def body(
@@ -432,8 +443,24 @@
     proto_unit = proto_unit32.astype(BF16)
     protos = proto_unit.shape[0]
     calls = make_calls(crops, protos, size, lax.axis_size("dp"), parts)
-    energy_call, row_call, col_call, student_call, last_call, unit_grad_call, hidden_grad_call, proto_grad_call = calls
+    energy_call, row_call, col_call, student_call, last_call = calls[:5]
+    unit_grad_call, hidden_grad_call, proto_grad_call, pair_sum_call = calls[5:]
+    me = lax.axis_index("dp")
+    count = protos // lax.axis_size("dp")
+    across = me // 8
+    places = (
+        (1 - me % 2).reshape(1),
+        (me % 2).reshape(1),
+        ((me // 2) % 4).reshape(1),
+        *(value.astype(jnp.uint32) for value in (lax.axis_index("proto") * own, across, 1 - across, me * count)),
+    )
     energy, sums = energy_call(teacher_all, proto_unit)
+    sums, places = lax.optimization_barrier((sums, places))
+    other, core, place, own_at, kept_at, given_at, protos_at = places
+    for step in range(ITERS - 1):
+        (sums,) = row_call(exchanged(sums, "dp"), energy)
+        (sums,) = col_call(exchanged(sums, "proto"), energy)
+    sums, gathered, turned = lax.optimization_barrier((sums, gathered, turned))
     values = gathered[:, :crops].astype(F32)
     student_center, student_scale = center_and_scale(
         jnp.sum(values, axis=0)[:, None], jnp.sum(values * values, axis=0)[:, None]
@@ -447,53 +474,48 @@
     normed = turned.astype(F32) - student_center.reshape(1, crops)
     normed = (normed * student_scale.reshape(1, crops) * gain_s[:, None]).astype(BF16)
     student_unit32, student_factor = (
-        lax.dynamic_slice_in_dim(value, lax.axis_index("proto") * own, own, 0)
+        lax.dynamic_slice(value, (own_at, jnp.uint32(0)), (own, value.shape[1]))
         for value in (student_unit32, student_factor)
     )
+    fields = student_call(student_unit, proto_unit)
     student = (student_unit, student_unit32, student_factor, normed, student_unit.T)
-    for step in range(ITERS - 1):
-        sums = exchanged(sums, "dp")
-        if step == ITERS - 2:
-            sums, student = lax.optimization_barrier((sums, student))
-            student_unit, student_unit32, student_factor, normed, turned_unit = student
-        (sums,) = row_call(sums, energy)
-        if step == ITERS - 2:
-            sums, student_unit = lax.optimization_barrier((sums, student_unit))
-            fields = student_call(student_unit, proto_unit)
-        sums = exchanged(sums, "proto")
-        if step == ITERS - 2:
-            sums, fields = lax.optimization_barrier((sums, fields))
-        (sums,) = col_call(sums, energy)
+    sums, fields, student = lax.optimization_barrier((sums, fields, student))
+    student_unit, student_unit32, student_factor, normed, turned_unit = student
     exponent, pulled, partition = fields
     sums = exchanged(sums, "dp")
     sums, coded, scale = last_call(sums, partition, energy, student_unit, proto_unit)
-    core = (lax.axis_index("dp") % 2).reshape(1)
     unit_grad, crop_loss, wanted, given, give = unit_grad_call(
-        1 - core, exchanged(sums, "proto"), pulled, coded, turned_unit, scale, exponent, energy
-    )
+        other, exchanged(sums, "proto"), pulled, coded, turned_unit, scale, exponent, energy
+    )
+    give, unit_grad, crop_loss, prototypes = lax.optimization_barrier((give, unit_grad, crop_loss, prototypes))
+    got = swapped(give, "dp", 1)
     unit_grad = exchanged(unit_grad.reshape(parts, own, size), "proto")
-    stages = summed_protos(proto_grad_call(core, turned_unit, wanted, given, scale, exponent, energy), give)
-    blocks = next(stages)
+    kept = proto_grad_call(core, turned_unit, wanted, given, scale, exponent, energy)
+    quads = (2, 4) + kept.shape[1:]
+    blocks = pair_sum_call(place, kept.reshape(quads), got.reshape(quads))
     crop_loss = swapped(crop_loss, "dp", 8).reshape(1, crops)
     crop_loss = jnp.sum(jnp.where(pick, crop_loss, 0.0), axis=1)
     (sent,) = hidden_grad_call(unit_grad, student_unit32, student_factor)
     sent, blocks = lax.optimization_barrier((sent, blocks))
-    blocks = stages.send(blocks)
     sent = exchanged(sent, "proto").reshape(crops, size)
     share = jnp.dot(normed, sent, preferred_element_type=F32).astype(BF16)
-    share, blocks = lax.optimization_barrier((share, blocks))
-    blocks = stages.send(blocks)
+    far = along_y(blocks[2], 2)
+    share, far = lax.optimization_barrier((share, far))
     near = [[8 * x + other for other in range(8)] for x in range(2)]
     share = lax.all_to_all(jnp.broadcast_to(share[None], (8,) + share.shape), "dp", 0, 0, axis_index_groups=near)
+    terms = (blocks[0], along_y(blocks[1], 1), along_y(blocks[3], 3), far)
+    share, terms = lax.optimization_barrier((share, terms))
+    total = sum(term.astype(F32) for term in terms).astype(BF16)
+    keep, give = (
+        lax.dynamic_slice(total, (at, jnp.uint32(0), jnp.uint32(0)), (1,) + total.shape[1:])[0]
+        for at in (kept_at, given_at)
+    )
     share = jnp.sum(share.astype(F32), axis=0).astype(BF16)
-    proto_unit_grad = blocks.T
+    proto_unit_grad = (keep.astype(F32) + swapped(give, "dp", 8).astype(F32)).T
     grad_proj = share.astype(F32) + swapped(share, "dp", 8).astype(F32)
 
-    count = protos // lax.axis_size("dp")
-    own_start = lax.axis_index("dp") * count
-    own_unit, own_factor = unit_rows(
-        lax.dynamic_slice_in_dim(prototypes, own_start, count, 0).astype(F32)
-    )
+    own_protos = lax.dynamic_slice(prototypes, (protos_at, jnp.uint32(0)), (count, size))
+    own_unit, own_factor = unit_rows(own_protos.astype(F32))
     grad_protos = own_factor * (
         proto_unit_grad - own_unit * jnp.sum(own_unit * proto_unit_grad, axis=1, keepdims=True)
     )

time: 285 us -> 270 us (0.947)
  blocking collectives: 30.8 us -> 72.4 us
  starting transfers between devices: 63.3 us -> 42.2 us
  local copies, waits for them, and re-layouts: 38.4 us -> 20.5 us
  waiting for transfers between devices: 71.2 us -> 58.8 us
  other arithmetic: 29.4 us -> 23.7 us
    all_to_all x2 -> x6, blocking collectives: 30.8 us -> 72.4 us  [exchanged(): return lax.all_to_all(blocks, axis, 0, 0)]
    all_to_all x8 -> x4, starting transfers between devices: 45.4 us -> 24.2 us  [exchanged(): return lax.all_to_all(blocks, axis, 0, 0)]
    unnamed x66 -> x43, local copies, waits for them, and re-layouts: 27.4 us -> 7.21 us
    all_to_all x8 -> x4, waiting for transfers between devices: 52.3 us -> 45 us  [exchanged(): return lax.all_to_all(blocks, axis, 0, 0)]
    optimization_barrier x1 -> x2, local copies, waits for them, and re-layouts: 0.09 us -> 4.79 us  [the longest x1 4.71 us: body(): lax.optimization_barrier((give, unit_grad, crop_loss, prototypes))]
    convert_element_type x2 -> x1, other arithmetic: 4.32 us -> 0.2 us  [body(): total = sum((term.astype(F32) for term in terms)).astype(BF16)]
    ppermute x5, waiting for transfers between devices: 7.92 us -> 4.85 us  [swapped(): return lax.ppermute(value, axis, [(one, one ^ bit) for one in range(count)])]
    pallas_call x5 -> x6, Pallas kernels: 14.2 us -> 14 us  [the longest x1 5.22 us: body(): unit_grad_call(other, exchanged(sums, 'proto'), pulled, coded, turned_uni...]
  transfers between devices with their start and end apart: 18 -> 14, of which waited for: 11 -> 7; matrix products, arithmetic and copies ran while one was open for 14% -> 9% of each run, Pallas kernels for 6% -> 5%
where the time goes in v7:
time: 270 us; the launch traced here: 269 us
  blocking collectives  72.4 us (27%)
  waiting for transfers between devices  58.8 us (22%)
  starting transfers between devices  42.2 us (16%)
  Pallas kernels  31 us (11%)
  other arithmetic  23.7 us (9%)
  local copies, waits for them, and re-layouts  20.5 us (8%)
  between operations  14.5 us (5%)
  matrix products  5.65 us (2%)
    all_to_all x6, blocking collectives, exchanged(): return lax.all_to_all(blocks, axis, 0, 0)  72.4 us
    all_to_all x4, waiting for transfers between devices, exchanged(): return lax.all_to_all(blocks, axis, 0, 0)  45 us
    all_to_all x4, starting transfers between devices, exchanged(): return lax.all_to_all(blocks, axis, 0, 0)  24.2 us
    ppermute x5, starting transfers between devices, swapped(): return lax.ppermute(value, axis, [(one, one ^ bit) for one in range(count)])  9.11 us
    ppermute x3, waiting for transfers between devices, along_y(): lax.ppermute(value, 'dp', [(one, one & 9 | one + 2 * step & 6) for one in...  8.94 us
    unnamed x43, local copies, waits for them, and re-layouts  7.21 us
    all_to_all x1, starting transfers between devices, body(): lax.all_to_all(jnp.broadcast_to(share[None], (8,) + share.shape), 'dp', 0...  5.74 us
    pallas_call x1, Pallas kernels, body(): fields = student_call(student_unit, proto_unit)  5.7 us
  transfers between devices with their start and end apart: 14, of which 7 were waited for; matrix products, arithmetic and copies ran while one was open for 9% of the time, Pallas kernels for 5%

profile of v7, /device:TPU:1, one launch (start us, length us, event | category | flops | bytes accessed | tf_op | source)
XLA Modules:
  0.0 268.8 jit_solution(7279022851980790755)
XLA Ops:
  7.2 3.7 %collective-permute-start = (bf16[512,96]{0,1:T(8,128)(2,1)}, bf16[512,96]{0,1:T(8,128)(2,1)S(1)}, u32[]{:S(2)}, u32[]{:S(2)}) collective-permute-start(bf16[512,96]{0,1:T(8,128)(2,1)} %param.8), channel_id=1, source_target_pairs={{0,128},{16,144},{32,160},{48,176},{64,192},{80,208},{96,224},{112... | collective-permute-start | bytes 294920 | tf_op jit(solution)/shard_map/ppermute | solution.py:56
  10.9 0.8 dynamic_slice.22
  11.7 0.8 dynamic_slice.21
  12.4 1.7 fusion.24
  14.1 0.7 add_select_fusion
  16.6 0.9 convert_reduce_fusion.3
  18.4 1.3 fusion.3
  19.7 0.9 copy.23
  20.6 0.7 fusion.30
  21.3 0.7 pad_maximum_fusion.3
  22.0 1.9 fusion.14
  23.9 8.3 %all-to-all-start = ((bf16[16,36,384]{2,1,0:T(8,128)(2,1)}), bf16[16,36,384]{2,1,0:T(8,128)(2,1)}, u32[]{:S(2)}, u32[]{:S(2)}) async-start(bf16[16,36,384]{2,1,0:T(8,128)(2,1)} %fusion.14), calls=%async_computation | async-start | bytes 983040 | tf_op jit(solution)/shard_map/all_to_all | solution.py:38
  32.3 0.7 fusion
  33.0 16.2 %all-to-all-done = bf16[16,36,384]{2,1,0:T(8,128)(2,1)} async-done(((bf16[16,36,384]{2,1,0:T(8,128)(2,1)}), bf16[16,36,384]{2,1,0:T(8,128)(2,1)}, u32[]{:S(2)}, u32[]{:S(2)}) %all-to-all-start) | async-done | bytes 442400 | tf_op jit(solution)/shard_map/all_to_all | solution.py:38
  49.2 1.1 convert_reduce_fusion.2
  50.8 0.8 broadcast_in_dim.17
  51.6 6.8 %all-to-all-start.1 = ((bf16[16,32,384]{2,1,0:T(8,128)(2,1)}), bf16[16,32,384]{2,1,0:T(8,128)(2,1)S(1)}, u32[]{:S(2)}, u32[]{:S(2)}) async-start(bf16[16,32,384]{2,1,0:T(8,128)(2,1)} %broadcast_in_dim.17), calls=%async_computation.1 | async-start | bytes 786432 | tf_op jit(solution)/shard_map/all_to_all | solution.py:38
  58.4 2.3 fusion.1.protos_ref
  60.7 13.9 %all-to-all-done.1 = bf16[16,32,384]{2,1,0:T(8,128)(2,1)S(1)} async-done(((bf16[16,32,384]{2,1,0:T(8,128)(2,1)}), bf16[16,32,384]{2,1,0:T(8,128)(2,1)S(1)}, u32[]{:S(2)}, u32[]{:S(2)}) %all-to-all-start.1) | async-done | bytes 393248 | tf_op jit(solution)/shard_map/all_to_all | solution.py:38
  74.6 3.4 %shard_map.111 = (bf16[512,4096]{1,0:T(8,128)(2,1)S(1)}, bf16[16,32,128]{2,1,0:T(8,128)(2,1)S(1)}) custom-call(bf16[512,384]{1,0:T(8,128)(2,1)S(1)} %bitcast.54, bf16[4096,384]{1,0:T(8,128)(2,1)S(1)} %fusion.1.protos_ref), custom_call_target="tpu_custom_call" | custom-call | flops 1610612736 | bytes 4194304 | tf_op jit(solution)/shard_map/pallas_call | solution.py:457
  78.0 16.9 %all_to_all.55.got_ref = bf16[16,32,128]{2,1,0:T(8,128)(2,1)S(1)} all-to-all(bf16[16,32,128]{2,1,0:T(8,128)(2,1)S(1)} %get-tuple-element.59), channel_id=1, replica_groups=mesh['dp'=16,'proto'=16] {'dp'}, dimensions={0} | all-to-all | bytes 262144 | tf_op jit(solution)/shard_map/all_to_all | solution.py:38
  94.8 1.4 shard_map.112
  96.2 11.2 %all_to_all.56.got_ref = f32[16,4,128]{2,1,0:T(4,128)S(1)} all-to-all(f32[16,4,128]{2,1,0:T(4,128)S(1)} %shard_map.112), channel_id=1, replica_groups=mesh['dp'=16,'proto'=16] {'proto'}, dimensions={0} | all-to-all | bytes 65536 | tf_op jit(solution)/shard_map/all_to_all | solution.py:38
  107.4 1.6 shard_map.113
  109.0 12.4 %all_to_all.57.got_ref = bf16[16,32,128]{2,1,0:T(8,128)(2,1)S(1)} all-to-all(bf16[16,32,128]{2,1,0:T(8,128)(2,1)S(1)} %shard_map.113), channel_id=1, replica_groups=mesh['dp'=16,'proto'=16] {'dp'}, dimensions={0} | all-to-all | bytes 262144 | tf_op jit(solution)/shard_map/all_to_all | solution.py:38
  121.4 1.4 shard_map.114
  122.8 9.9 %all_to_all.58.got_ref = f32[16,4,128]{2,1,0:T(4,128)S(1)} all-to-all(f32[16,4,128]{2,1,0:T(4,128)S(1)} %shard_map.114), channel_id=1, replica_groups=mesh['dp'=16,'proto'=16] {'proto'}, dimensions={0} | all-to-all | bytes 65536 | tf_op jit(solution)/shard_map/all_to_all | solution.py:38
  132.7 1.6 shard_map.115
  135.0 1.5 convert_reduce_fusion.1
  136.5 1.9 fusion.2
  138.4 3.7 %multiply_reduce_fusion = (f32[512]{0:T(512)S(1)}, f32[512,384]{1,0:T(8,128)}) fusion(f32[384]{0:T(512)S(1)} %convert_reduce_fusion.1, f32[512]{0:T(512)S(1)} %get-tuple-element.134, f32[512]{0:T(512)S(1)} %get-tuple-element.133, bf16[1536,896]{1,0:T(8,128)(2,1)} %all-gather.2.cloned.1.call-done), kind=kOutput, calls=%fused_computation.26 | convolution fusion | flops 604962304 | bytes 3546624 | tf_op jit(solution)/shard_map/dot_general | solution.py:29
  142.1 0.7 multiply_convert_fusion
  142.8 2.3 copy.26
  145.1 1.4 fusion.32
  147.2 1.3 fusion.11.turned_ref
  149.1 5.7 %shard_map.116 = (bf16[512,4096]{1,0:T(8,128)(2,1)S(1)}, f32[512,384]{1,0:T(8,128)S(1)}, f32[4,128]{1,0:T(4,128)S(1)}) custom-call(bf16[512,384]{1,0:T(8,128)(2,1)S(1)} %get-tuple-element.70.student_ref, bf16[4096,384]{1,0:T(8,128)(2,1)S(1)} %fusion.1.protos_ref), custom_call_target="tpu_custom_call" | custom-call | flops 3221225472 | bytes 4194304 | tf_op jit(solution)/shard_map/pallas_call | solution.py:480
  154.8 12.0 %all_to_all.59.got_ref = bf16[16,32,128]{2,1,0:T(8,128)(2,1)S(1)} all-to-all(bf16[16,32,128]{2,1,0:T(8,128)(2,1)S(1)} %copy-done.6), channel_id=1, replica_groups=mesh['dp'=16,'proto'=16] {'dp'}, dimensions={0} | all-to-all | bytes 262144 | tf_op jit(solution)/shard_map/all_to_all | solution.py:38
  166.8 3.6 %shard_map.117 = (f32[16,12,128]{2,1,0:T(8,128)S(1)}, f32[512,384]{1,0:T(8,128)S(1)}, f32[32,128]{1,0:T(8,128)S(1)}) custom-call(bf16[16,32,128]{2,1,0:T(8,128)(2,1)S(1)} %all_to_all.59.got_ref, f32[4,128]{1,0:T(4,128)S(1)} %get-tuple-element.69.partition_ref, bf16[512,4096]{1,0:T(8,128)(2,1)S(1)} %copy-done.1, ...), custom_call_target="tpu_custom_call" | custom-call | flops 1610612736 | bytes 4194304 | tf_op jit(solution)/shard_map/pallas_call | solution.py:486
  170.4 10.0 %all_to_all.60.got_ref = f32[16,12,128]{2,1,0:T(8,128)S(1)} all-to-all(f32[16,12,128]{2,1,0:T(8,128)S(1)} %get-tuple-element.71), channel_id=1, replica_groups=mesh['dp'=16,'proto'=16] {'proto'}, dimensions={0} | all-to-all | bytes 196608 | tf_op jit(solution)/shard_map/all_to_all | solution.py:38
  180.4 5.2 %shard_map.118 = (bf16[512,384]{1,0:T(8,128)(2,1)}, f32[4,128]{1,0:T(4,128)S(1)}, f32[512,128]{1,0:T(8,128)S(1)}, f32[512,128]{1,0:T(8,128)S(1)}, bf16[8,384,256]{2,1,0:T(8,128)(2,1)}) custom-call(s32[1]{0:T(128)} %bitcast.8.core_ref, f32[16,12,128]{2,1,0:T(8,128)S(1)} %all_to_all.60.got_ref, f32[512,384]{1,0:T(8,128)S(1)} %get-tuple-element.72.pulled_ref, ...), custom_call_target="tpu_custom_call" | custom-call | flops 805306368 | bytes 5767168 | tf_op jit(solution)/shard_map/pallas_call | solution.py:487
  186.2 2.1 collective-permute-start.2
  188.3 3.6 %all-to-all-start.8 = ((bf16[16,32,384]{2,1,0:T(8,128)(2,1)}), bf16[16,32,384]{2,1,0:T(8,128)(2,1)S(1)}, u32[]{:S(2)}, u32[]{:S(2)}) async-start(bf16[16,32,384]{2,1,0:T(8,128)(2,1)} %bitcast.15), calls=%async_computation.8 | async-start | bytes 786432 | tf_op jit(solution)/shard_map/all_to_all | solution.py:38
  192.0 2.2 copy-done.2
  194.2 2.2 copy-done.4
  196.3 3.5 %shard_map.120 = bf16[8,384,256]{2,1,0:T(8,128)(2,1)S(1)} custom-call(s32[1]{0:T(128)} %bitcast.9.core_ref, bf16[384,512]{1,0:T(8,128)(2,1)S(1)} %fusion.11.turned_ref, f32[512,128]{1,0:T(8,128)S(1)} %get-tuple-element.87.wanted_ref, f32[512,128]{1,0:T(8,128)S(1)} %get-tuple-element.88.given_ref, f32[32,128]{1,0:T(8,128)S(1)} %get-tuple-element.75.scale_ref, ...), custom_call_target="tpu_custom_call" | custom-call | flops 805306368 | bytes 5767168 | tf_op jit(solution)/shard_map/pallas_call | solution.py:493
  199.9 4.2 %all-to-all-done.8.got_ref = bf16[16,32,384]{2,1,0:T(8,128)(2,1)S(1)} async-done(((bf16[16,32,384]{2,1,0:T(8,128)(2,1)}), bf16[16,32,384]{2,1,0:T(8,128)(2,1)S(1)}, u32[]{:S(2)}, u32[]{:S(2)}) %all-to-all-start.8) | async-done | bytes 393248 | tf_op jit(solution)/shard_map/all_to_all | solution.py:38
  204.0 0.9 shard_map.119
  204.9 2.8 %shard_map.121 = (bf16[2,384,256]{2,1,0:T(8,128)(2,1)S(1)}, bf16[2,384,256]{2,1,0:T(8,128)(2,1)S(1)}, bf16[2,384,256]{2,1,0:T(8,128)(2,1)S(1)}, bf16[2,384,256]{2,1,0:T(8,128)(2,1)S(1)}) custom-call(s32[1]{0:T(128)} %bitcast.10.place_ref, bf16[2,4,384,256]{3,2,1,0:T(8,128)(2,1)S(1)} %bitcast.53, bf16[2,4,384,256]{3,2,1,0:T(8,128)(2,1)} %bitcast.17.got_ref), custom_call_target="tpu_custom_call" | custom-call | flops 1572864 | bytes 4718592 | tf_op jit(solution)/shard_map/pallas_call | solution.py:495
  207.8 5.4 %all-to-all-start.9 = ((bf16[16,32,384]{2,1,0:T(8,128)(2,1)}), bf16[16,32,384]{2,1,0:T(8,128)(2,1)S(1)}, u32[]{:S(2)}, u32[]{:S(2)}) async-start(bf16[16,32,384]{2,1,0:T(8,128)(2,1)} %shard_map.119), calls=%async_computation.9 | async-start | bytes 786432 | tf_op jit(solution)/shard_map/all_to_all | solution.py:38
  213.6 10.8 %all-to-all-done.9 = bf16[16,32,384]{2,1,0:T(8,128)(2,1)S(1)} async-done(((bf16[16,32,384]{2,1,0:T(8,128)(2,1)}), bf16[16,32,384]{2,1,0:T(8,128)(2,1)S(1)}, u32[]{:S(2)}, u32[]{:S(2)}) %all-to-all-start.9) | async-done | bytes 393248 | tf_op jit(solution)/shard_map/all_to_all | solution.py:38
  224.6 0.9 broadcast_in_dim.21
  225.5 5.7 %all-to-all-start.10 = ((bf16[8,96,384]{2,1,0:T(8,128)(2,1)}), bf16[8,96,384]{2,1,0:T(8,128)(2,1)S(1)}, u32[]{:S(2)}, u32[]{:S(2)}) async-start(bf16[8,96,384]{2,1,0:T(8,128)(2,1)} %broadcast_in_dim.21), calls=%async_computation.10 | async-start | bytes 1179648 | tf_op jit(solution)/shard_map/all_to_all | solution.py:505
  231.2 1.4 collective-permute-start.4
  232.6 1.3 collective-permute-start.5
  234.1 4.7 %copy.28 = bf16[4096,384]{0,1:T(8,128)(2,1)} copy(bf16[4096,384]{1,0:T(8,128)(2,1)} %param.14) | data formatting | bytes 6291456 | tf_op jit(solution)/shard_map/optimization_barrier | solution.py:490
  238.8 1.1 fusion.20
  240.0 0.8 select_reduce_fusion
  240.8 8.9 %collective-permute-done.4 = bf16[2,384,256]{2,1,0:T(8,128)(2,1)S(1)} collective-permute-done((bf16[2,384,256]{2,1,0:T(8,128)(2,1)S(1)}, bf16[2,384,256]{2,1,0:T(8,128)(2,1)S(1)}, u32[]{:S(2)}, u32[]{:S(2)}) %collective-permute-start.4) | collective-permute-done | bytes 393248 | tf_op jit(solution)/shard_map/ppermute | solution.py:408
  250.3 2.9 %collective-permute-start.7 = (bf16[384,256]{1,0:T(8,128)(2,1)S(1)}, bf16[384,256]{1,0:T(8,128)(2,1)S(1)}, u32[]{:S(2)}, u32[]{:S(2)}) collective-permute-start(bf16[384,256]{1,0:T(8,128)(2,1)S(1)} %dynamic-slice_bitcast_fusion), channel_id=1, source_target_pairs={{0,128},{16,144},{32,160},{48,176},{64,192},{80,208},{96,224},{112... | collective-permute-start | bytes 589832 | tf_op jit(solution)/shard_map/ppermute | solution.py:56
  253.2 1.4 collective-permute-done.6
  255.3 3.4 %collective-permute-done.7 = bf16[384,256]{1,0:T(8,128)(2,1)S(1)} collective-permute-done((bf16[384,256]{1,0:T(8,128)(2,1)S(1)}, bf16[384,256]{1,0:T(8,128)(2,1)S(1)}, u32[]{:S(2)}, u32[]{:S(2)}) %collective-permute-start.7) | collective-permute-done | bytes 196640 | tf_op jit(solution)/shard_map/ppermute | solution.py:56
  258.7 1.1 fusion.17
  259.9 1.1 fusion.19
  261.0 0.9 copy.29
  (83 shorter events, 7.8 us)
Async XLA Ops:
  7.2 25.1 %copy-start.10 = (bf16[4096,384]{1,0:T(8,128)(2,1)S(1)}, bf16[4096,384]{1,0:T(8,128)(2,1)}, u32[]{:S(2)}) copy-start(bf16[4096,384]{1,0:T(8,128)(2,1)} %param.14) | copy-start | bytes 9437188
  7.2 127.8 %all-gather.2.cloned.1.call-start = ((), (), s32[]{:S(2)}) async-start(), calls=%async_computation.11 | async-start | bytes 2924544 | tf_op jit(solution)/shard_map/all_gather | solution.py:440
  7.2 7.6 %collective-permute-start = (bf16[512,96]{0,1:T(8,128)(2,1)}, bf16[512,96]{0,1:T(8,128)(2,1)S(1)}, u32[]{:S(2)}, u32[]{:S(2)}) collective-permute-start(bf16[512,96]{0,1:T(8,128)(2,1)} %param.8), channel_id=1, source_target_pairs={{0,128},{16,144},{32,160},{48,176},{64,192},{80,208},{96,224},{112... | collective-permute-start | bytes 294920 | tf_op jit(solution)/shard_map/ppermute | solution.py:56
  11.7 0.8 copy-start.17
  12.4 4.2 %copy-start.19 = (f32[96]{0:T(128)}, f32[96]{0:T(128)S(1)}, u32[]{:S(2)}) copy-start(f32[96]{0:T(128)S(1)} %dynamic_slice.21) | copy-start | bytes 1156
  14.1 3.7 %copy-start.14 = (f32[384]{0:T(512)}, f32[384]{0:T(512)S(1)}, u32[]{:S(2)}) copy-start(f32[384]{0:T(512)S(1)} %get-tuple-element.129) | copy-start | bytes 4612
  14.8 1.8 copy-start.15
  15.3 0.6 copy-start.11
  23.9 25.3 %all-to-all-start = ((bf16[16,36,384]{2,1,0:T(8,128)(2,1)}), bf16[16,36,384]{2,1,0:T(8,128)(2,1)}, u32[]{:S(2)}, u32[]{:S(2)}) async-start(bf16[16,36,384]{2,1,0:T(8,128)(2,1)} %fusion.14), calls=%async_computation | async-start | bytes 983040 | tf_op jit(solution)/shard_map/all_to_all | solution.py:38
  51.6 23.0 %all-to-all-start.1 = ((bf16[16,32,384]{2,1,0:T(8,128)(2,1)}), bf16[16,32,384]{2,1,0:T(8,128)(2,1)S(1)}, u32[]{:S(2)}, u32[]{:S(2)}) async-start(bf16[16,32,384]{2,1,0:T(8,128)(2,1)} %broadcast_in_dim.17), calls=%async_computation.1 | async-start | bytes 786432 | tf_op jit(solution)/shard_map/all_to_all | solution.py:38
  78.0 54.8 %copy-start = (bf16[512,4096]{1,0:T(8,128)(2,1)}, bf16[512,4096]{1,0:T(8,128)(2,1)S(1)}, u32[]{:S(2)}) copy-start(bf16[512,4096]{1,0:T(8,128)(2,1)S(1)} %get-tuple-element.60.energy_ref) | copy-start | bytes 12582916
  134.4 0.7 copy-start.5
  138.4 3.7 %copy-start.12 = (bf16[96,512]{1,0:T(8,128)(2,1)S(1)}, bf16[96,512]{1,0:T(8,128)(2,1)}, u32[]{:S(2)}) copy-start(bf16[96,512]{1,0:T(8,128)(2,1)} %copy-done.11) | copy-start | bytes 294916
  138.4 3.7 %copy-start.18 = (f32[96]{0:T(128)S(1)}, f32[96]{0:T(128)}, u32[]{:S(2)}) copy-start(f32[96]{0:T(128)} %copy-done.17) | copy-start | bytes 1156
  149.1 5.7 %copy-start.6 = (bf16[16,32,128]{2,1,0:T(8,128)(2,1)S(1)}, bf16[16,32,128]{2,1,0:T(8,128)(2,1)}, u32[]{:S(2)}) copy-start(bf16[16,32,128]{2,1,0:T(8,128)(2,1)} %copy-done.5) | copy-start | bytes 393220
  149.1 17.7 %copy-start.1 = (bf16[512,4096]{1,0:T(8,128)(2,1)S(1)}, bf16[512,4096]{1,0:T(8,128)(2,1)}, u32[]{:S(2)}) copy-start(bf16[512,4096]{1,0:T(8,128)(2,1)} %copy-done) | copy-start | bytes 12582916
  154.8 25.6 %copy-start.3 = (bf16[512,4096]{1,0:T(8,128)(2,1)}, bf16[512,4096]{1,0:T(8,128)(2,1)S(1)}, u32[]{:S(2)}) copy-start(bf16[512,4096]{1,0:T(8,128)(2,1)S(1)} %get-tuple-element.76.exponent_ref) | copy-start | bytes 12582916
  180.4 11.5 %copy-start.20 = (f32[32,1]{0,1:T(1,128)S(1)}, f32[32,1]{0,1:T(1,128)}, u32[]{:S(2)}) copy-start(f32[32,1]{0,1:T(1,128)} %dynamic-slice_bitcast_fusion.1) | copy-start | bytes 388
  185.6 0.6 copy-start.8
  186.2 18.7 %collective-permute-start.2 = (bf16[8,384,256]{2,1,0:T(8,128)(2,1)}, bf16[8,384,256]{2,1,0:T(8,128)(2,1)}, u32[]{:S(2)}, u32[]{:S(2)}) collective-permute-start(bf16[8,384,256]{2,1,0:T(8,128)(2,1)} %get-tuple-element.89), channel_id=1, source_target_pairs={{0,16},{16,0},{32,48},{48,32},{64,80},{80,64},{96,112},{112,96},{1... | collective-permute-start | bytes 4718600 | tf_op jit(solution)/shard_map/ppermute | solution.py:56
  188.3 15.7 %all-to-all-start.8 = ((bf16[16,32,384]{2,1,0:T(8,128)(2,1)}), bf16[16,32,384]{2,1,0:T(8,128)(2,1)S(1)}, u32[]{:S(2)}, u32[]{:S(2)}) async-start(bf16[16,32,384]{2,1,0:T(8,128)(2,1)} %bitcast.15), calls=%async_computation.8 | async-start | bytes 786432 | tf_op jit(solution)/shard_map/all_to_all | solution.py:38
  192.0 2.2 copy-start.2
  194.2 2.2 copy-start.4
  196.3 7.7 %copy-start.7 = (f32[32,384]{1,0:T(8,128)S(1)}, f32[32,384]{1,0:T(8,128)}, u32[]{:S(2)}) copy-start(f32[32,384]{1,0:T(8,128)} %constant_dynamic-slice_fusion.unit_ref) | copy-start | bytes 147460
  199.8 24.5 %copy-start.13 = (bf16[96,512]{1,0:T(8,128)(2,1)S(1)}, bf16[96,512]{1,0:T(8,128)(2,1)}, u32[]{:S(2)}) copy-start(bf16[96,512]{1,0:T(8,128)(2,1)} %multiply_convert_fusion) | copy-start | bytes 294916
  204.9 29.0 %copy-start.9 = (f32[4,128]{1,0:T(4,128)S(1)}, f32[4,128]{1,0:T(4,128)}, u32[]{:S(2)}) copy-start(f32[4,128]{1,0:T(4,128)} %copy-done.8) | copy-start | bytes 6148
  207.8 16.6 %all-to-all-start.9 = ((bf16[16,32,384]{2,1,0:T(8,128)(2,1)}), bf16[16,32,384]{2,1,0:T(8,128)(2,1)S(1)}, u32[]{:S(2)}, u32[]{:S(2)}) async-start(bf16[16,32,384]{2,1,0:T(8,128)(2,1)} %shard_map.119), calls=%async_computation.9 | async-start | bytes 786432 | tf_op jit(solution)/shard_map/all_to_all | solution.py:38
  213.2 11.4 %collective-permute-start.3 = (bf16[2,384,256]{2,1,0:T(8,128)(2,1)S(1)}, bf16[2,384,256]{2,1,0:T(8,128)(2,1)S(1)}, u32[]{:S(2)}, u32[]{:S(2)}) collective-permute-start(bf16[2,384,256]{2,1,0:T(8,128)(2,1)S(1)} %get-tuple-element.95), channel_id=1, source_target_pairs={{0,64},{16,80},{32,96},{48,112},{64,0},{80,16},{96,32},{112,48},{1... | collective-permute-start | bytes 1179656 | tf_op jit(solution)/shard_map/ppermute | solution.py:408
  225.5 24.3 %all-to-all-start.10 = ((bf16[8,96,384]{2,1,0:T(8,128)(2,1)}), bf16[8,96,384]{2,1,0:T(8,128)(2,1)S(1)}, u32[]{:S(2)}, u32[]{:S(2)}) async-start(bf16[8,96,384]{2,1,0:T(8,128)(2,1)} %broadcast_in_dim.21), calls=%async_computation.10 | async-start | bytes 1179648 | tf_op jit(solution)/shard_map/all_to_all | solution.py:505
  231.2 8.7 %copy-start.16 = (s32[512]{0:T(512)S(1)}, s32[512]{0:T(512)}, u32[]{:S(2)}) copy-start(s32[512]{0:T(512)} %copy-done.15) | copy-start | bytes 6148
  231.2 18.5 %collective-permute-start.4 = (bf16[2,384,256]{2,1,0:T(8,128)(2,1)S(1)}, bf16[2,384,256]{2,1,0:T(8,128)(2,1)S(1)}, u32[]{:S(2)}, u32[]{:S(2)}) collective-permute-start(bf16[2,384,256]{2,1,0:T(8,128)(2,1)S(1)} %get-tuple-element.98), channel_id=1, source_target_pairs={{0,32},{16,48},{32,64},{48,80},{64,96},{80,112},{96,0},{112,16},{1... | collective-permute-start | bytes 1179656 | tf_op jit(solution)/shard_map/ppermute | solution.py:408
  232.6 17.1 %collective-permute-start.5 = (bf16[2,384,256]{2,1,0:T(8,128)(2,1)S(1)}, bf16[2,384,256]{2,1,0:T(8,128)(2,1)S(1)}, u32[]{:S(2)}, u32[]{:S(2)}) collective-permute-start(bf16[2,384,256]{2,1,0:T(8,128)(2,1)S(1)} %get-tuple-element.99), channel_id=1, source_target_pairs={{0,96},{16,112},{32,0},{48,16},{64,32},{80,48},{96,64},{112,80},{1... | collective-permute-start | bytes 1179656 | tf_op jit(solution)/shard_map/ppermute | solution.py:408
  233.9 6.0 %collective-permute-start.1 = (f32[4,128]{1,0:T(4,128)S(1)}, f32[4,128]{1,0:T(4,128)S(1)}, u32[]{:S(2)}, u32[]{:S(2)}) collective-permute-start(f32[4,128]{1,0:T(4,128)S(1)} %copy-done.9), channel_id=1, source_target_pairs={{0,128},{16,144},{32,160},{48,176},{64,192},{80,208},{96,224},{112... | collective-permute-start | bytes 6152 | tf_op jit(solution)/shard_map/ppermute | solution.py:56
  249.8 4.8 %collective-permute-start.6 = (bf16[96,384]{1,0:T(8,128)(2,1)S(1)}, bf16[96,384]{1,0:T(8,128)(2,1)S(1)}, u32[]{:S(2)}, u32[]{:S(2)}) collective-permute-start(bf16[96,384]{1,0:T(8,128)(2,1)S(1)} %reduce_sum.163), channel_id=1, source_target_pairs={{0,128},{16,144},{32,160},{48,176},{64,192},{80,208},{96,224},{112... | collective-permute-start | bytes 221192 | tf_op jit(solution)/shard_map/ppermute | solution.py:56
  250.3 8.4 %collective-permute-start.7 = (bf16[384,256]{1,0:T(8,128)(2,1)S(1)}, bf16[384,256]{1,0:T(8,128)(2,1)S(1)}, u32[]{:S(2)}, u32[]{:S(2)}) collective-permute-start(bf16[384,256]{1,0:T(8,128)(2,1)S(1)} %dynamic-slice_bitcast_fusion), channel_id=1, source_target_pairs={{0,128},{16,144},{32,160},{48,176},{64,192},{80,208},{96,224},{112... | collective-permute-start | bytes 589832 | tf_op jit(solution)/shard_map/ppermute | solution.py:56
Sparse Core Ops, SparseCore 0:
  16.7 78.8 all-gather.1

commit v8 on v7

--- a/solution.py
+++ b/solution.py
@@ -169,6 +169,38 @@
     def _():
         for one in range(sums_ref.shape[0]):
             sums_ref[one] = held[...].astype(BF16)
+
+
+def student_hidden_kernel(gathered_ref, own_ref, unit_ref, wide_ref, factor_ref, turned_ref, normed_ref):
+    depth, crops = gathered_ref.shape[0], own_ref.shape[1]
+    first = jnp.zeros((1, crops), F32)
+    second = jnp.zeros((1, crops), F32)
+    for low in range(0, depth, 64):
+        part = gathered_ref[low : low + 64, :crops].astype(F32)
+        first = first + jnp.sum(part, axis=0, keepdims=True)
+        second = second + jnp.sum(part * part, axis=0, keepdims=True)
+    center, scale = center_and_scale(first, second)
+    normed_ref[...] = ((own_ref[...].astype(F32) - center) * scale).astype(BF16)
+    column = jnp.sum(gathered_ref[:, crops:].astype(F32), axis=0, keepdims=True)
+    wide_ref[...] = contract_first(gathered_ref[:, :crops], gathered_ref[:, crops:])
+
+    def down(row):
+        return jnp.concatenate([column_form(row[:, low : low + LANES]) for low in range(0, crops, LANES)], 0)
+
+    center, scale = down(center), down(scale)
+    cuts = [slice(low, low + LANES) for low in range(0, wide_ref.shape[1], LANES)]
+    total = jnp.zeros((crops, LANES), F32)
+    for cut in cuts:
+        value = scale * (wide_ref[:, cut] - center * column[:, cut])
+        wide_ref[:, cut] = value
+        total = total + value * value
+    factor = lax.rsqrt(jnp.sum(total, axis=1, keepdims=True) + EPSILON)
+    factor_ref[...] = factor
+    for cut in cuts:
+        value = wide_ref[:, cut] * factor
+        wide_ref[:, cut] = value
+        unit_ref[:, cut] = value.astype(BF16)
+        turned_ref[cut, :] = jnp.transpose(value).astype(BF16)
 
 
 def student_kernel(student_ref, protos_ref, exponent_ref, pulled_ref, partition_ref, held):
@@ -333,6 +365,18 @@
             (array((lines, LANES), F32), whole((lines, LANES))),
         ],
         [tall], 2 * product, 2 * matrix, matrix,
+    )
+    depth, width = D, D // parts
+    student_hidden = called(
+        student_hidden_kernel, 1, [whole((depth, crops + size)), whole((width, crops))],
+        [
+            (array((crops, size), BF16), whole((crops, size))),
+            (array((crops, size), F32), whole((crops, size))),
+            (array((crops, 1), F32), whole((crops, 1))),
+            (array((size, crops), BF16), whole((size, crops))),
+            (array((width, crops), BF16), whole((width, crops))),
+        ],
+        [], 2 * crops * depth * size, 2 * depth * (crops + size),
     )
     last = called(
         last_kernel, steps,
@@ -401,7 +445,7 @@
         compiler_params=params,
         cost_estimate=cost,
     )
-    return energy, rows, cols, student, last, unit_grad, hidden_grad, proto_grad, pair_sum
+    return energy, rows, cols, student, last, unit_grad, hidden_grad, proto_grad, pair_sum, student_hidden
 
 
 def along_y(value, step):
@@ -444,7 +488,7 @@
     protos = proto_unit.shape[0]
     calls = make_calls(crops, protos, size, lax.axis_size("dp"), parts)
     energy_call, row_call, col_call, student_call, last_call = calls[:5]
-    unit_grad_call, hidden_grad_call, proto_grad_call, pair_sum_call = calls[5:]
+    unit_grad_call, hidden_grad_call, proto_grad_call, pair_sum_call, student_hidden_call = calls[5:]
     me = lax.axis_index("dp")
     count = protos // lax.axis_size("dp")
     across = me // 8
@@ -461,33 +505,24 @@
         (sums,) = row_call(exchanged(sums, "dp"), energy)
         (sums,) = col_call(exchanged(sums, "proto"), energy)
     sums, gathered, turned = lax.optimization_barrier((sums, gathered, turned))
-    values = gathered[:, :crops].astype(F32)
-    student_center, student_scale = center_and_scale(
-        jnp.sum(values, axis=0)[:, None], jnp.sum(values * values, axis=0)[:, None]
-    )
-    weight = gathered[:, crops:]
-    student_hidden = student_scale * (
-        contract_first(gathered[:, :crops], weight) - student_center * jnp.sum(weight.astype(F32), axis=0)[None]
-    )
-    student_unit32, student_factor = unit_rows(student_hidden)
-    student_unit = student_unit32.astype(BF16)
-    normed = turned.astype(F32) - student_center.reshape(1, crops)
-    normed = (normed * student_scale.reshape(1, crops) * gain_s[:, None]).astype(BF16)
-    student_unit32, student_factor = (
-        lax.dynamic_slice(value, (own_at, jnp.uint32(0)), (own, value.shape[1]))
-        for value in (student_unit32, student_factor)
+    student_unit, student_unit32, student_factor, turned_unit, normed = student_hidden_call(
+        gathered, turned
     )
     fields = student_call(student_unit, proto_unit)
-    student = (student_unit, student_unit32, student_factor, normed, student_unit.T)
-    sums, fields, student = lax.optimization_barrier((sums, fields, student))
-    student_unit, student_unit32, student_factor, normed, turned_unit = student
+    sums, fields, turned_unit = lax.optimization_barrier((sums, fields, turned_unit))
     exponent, pulled, partition = fields
     sums = exchanged(sums, "dp")
     sums, coded, scale = last_call(sums, partition, energy, student_unit, proto_unit)
     unit_grad, crop_loss, wanted, given, give = unit_grad_call(
         other, exchanged(sums, "proto"), pulled, coded, turned_unit, scale, exponent, energy
     )
-    give, unit_grad, crop_loss, prototypes = lax.optimization_barrier((give, unit_grad, crop_loss, prototypes))
+    give, unit_grad, crop_loss, own_at, protos_at = lax.optimization_barrier(
+        (give, unit_grad, crop_loss, own_at, protos_at)
+    )
+    student_unit32, student_factor = (
+        lax.dynamic_slice(value, (own_at, jnp.uint32(0)), (own, value.shape[1]))
+        for value in (student_unit32, student_factor)
+    )
     got = swapped(give, "dp", 1)
     unit_grad = exchanged(unit_grad.reshape(parts, own, size), "proto")
     kept = proto_grad_call(core, turned_unit, wanted, given, scale, exponent, energy)
@@ -495,16 +530,14 @@
     blocks = pair_sum_call(place, kept.reshape(quads), got.reshape(quads))
     crop_loss = swapped(crop_loss, "dp", 8).reshape(1, crops)
     crop_loss = jnp.sum(jnp.where(pick, crop_loss, 0.0), axis=1)
+    unit_grad, blocks = lax.optimization_barrier((unit_grad, blocks))
     (sent,) = hidden_grad_call(unit_grad, student_unit32, student_factor)
-    sent, blocks = lax.optimization_barrier((sent, blocks))
     sent = exchanged(sent, "proto").reshape(crops, size)
-    share = jnp.dot(normed, sent, preferred_element_type=F32).astype(BF16)
-    far = along_y(blocks[2], 2)
-    share, far = lax.optimization_barrier((share, far))
+    share = (gain_s[:, None] * jnp.dot(normed, sent, preferred_element_type=F32)).astype(BF16)
+    terms = (blocks[0], along_y(blocks[1], 1), along_y(blocks[2], 2), along_y(blocks[3], 3))
+    share, terms = lax.optimization_barrier((share, terms))
     near = [[8 * x + other for other in range(8)] for x in range(2)]
     share = lax.all_to_all(jnp.broadcast_to(share[None], (8,) + share.shape), "dp", 0, 0, axis_index_groups=near)
-    terms = (blocks[0], along_y(blocks[1], 1), along_y(blocks[3], 3), far)
-    share, terms = lax.optimization_barrier((share, terms))
     total = sum(term.astype(F32) for term in terms).astype(BF16)
     keep, give = (
         lax.dynamic_slice(total, (at, jnp.uint32(0), jnp.uint32(0)), (1,) + total.shape[1:])[0]

time: 270 us -> 255 us (0.944)
  other arithmetic: 23.7 us -> 13.8 us
  waiting for transfers between devices: 58.8 us -> 53.7 us
  matrix products: 5.65 us -> 1.97 us
  starting transfers between devices: 42.2 us -> 45.7 us
    all_to_all x4, waiting for transfers between devices: 45 us -> 37.4 us  [exchanged(): return lax.all_to_all(blocks, axis, 0, 0)]
    optimization_barrier x2 -> x0, local copies, waits for them, and re-layouts: 4.79 us -> none  [the longest x1 4.71 us: body(): lax.optimization_barrier((give, unit_grad, crop_loss, prototypes))]
    unnamed x43 -> x50, local copies, waits for them, and re-layouts: 7.21 us -> 11.5 us
    dot_general x2 -> x1, matrix products: 3.9 us -> 0.22 us  [body(): jnp.dot(normed, sent, preferred_element_type=F32)]
    convert_element_type x3 -> x0, other arithmetic: 3.43 us -> none  [the longest x2 2.72 us: body(): student_unit = student_unit32.astype(BF16)]
    reduce_sum x2 -> x0, other arithmetic: 3.38 us -> none  [the longest x1 1.88 us: body(): jnp.sum(values * values, axis=0)[:, None]]
  transfers between devices with their start and end apart: 14 -> 14, of which waited for: 7 -> 10; matrix products, arithmetic and copies ran while one was open for 9% -> 9% of each run, Pallas kernels for 5% -> 6%
where the time goes in v8:
time: 255 us; the launch traced here: 252 us
  blocking collectives  72.5 us (28%)
  waiting for transfers between devices  53.7 us (21%)
  starting transfers between devices  45.7 us (18%)
  Pallas kernels  31 us (12%)
  local copies, waits for them, and re-layouts  19.1 us (7%)
  between operations  14.5 us (6%)
  other arithmetic  13.8 us (5%)
    all_to_all x6, blocking collectives, exchanged(): return lax.all_to_all(blocks, axis, 0, 0)  72.5 us
    all_to_all x4, waiting for transfers between devices, exchanged(): return lax.all_to_all(blocks, axis, 0, 0)  37.4 us
    all_to_all x4, starting transfers between devices, exchanged(): return lax.all_to_all(blocks, axis, 0, 0)  25.7 us
    unnamed x50, local copies, waits for them, and re-layouts  11.5 us
    ppermute x5, starting transfers between devices, swapped(): return lax.ppermute(value, axis, [(one, one ^ bit) for one in range(count)])  11.5 us
    ppermute x3, waiting for transfers between devices, along_y(): lax.ppermute(value, 'dp', [(one, one & 9 | one + 2 * step & 6) for one in...  8.89 us
    pallas_call x1, Pallas kernels, body(): fields = student_call(student_unit, proto_unit)  5.68 us
    ppermute x5, waiting for transfers between devices, swapped(): return lax.ppermute(value, axis, [(one, one ^ bit) for one in range(count)])  5.66 us
  transfers between devices with their start and end apart: 14, of which 10 were waited for; matrix products, arithmetic and copies ran while one was open for 9% of the time, Pallas kernels for 6%

profile of v8, /device:TPU:1, one launch (start us, length us, event | category | flops | bytes accessed | tf_op | source)
XLA Modules:
  0.0 252.3 jit_solution(3230813132039260725)
XLA Ops:
  7.2 3.7 %collective-permute-start = (bf16[512,96]{0,1:T(8,128)(2,1)}, bf16[512,96]{0,1:T(8,128)(2,1)S(1)}, u32[]{:S(2)}, u32[]{:S(2)}) collective-permute-start(bf16[512,96]{0,1:T(8,128)(2,1)} %param.8), channel_id=1, source_target_pairs={{0,128},{16,144},{32,160},{48,176},{64,192},{80,208},{96,224},{112... | collective-permute-start | bytes 294920 | tf_op jit(solution)/shard_map/ppermute | solution.py:56
  10.9 0.8 dynamic_slice.22
  11.7 0.8 dynamic_slice.21
  12.4 1.7 fusion.17
  14.1 0.7 add_select_fusion
  15.3 0.7 pad_maximum_fusion
  16.6 0.9 convert_reduce_fusion.1
  18.4 1.3 fusion.2
  19.7 0.9 copy.19
  21.3 0.7 pad_maximum_fusion.3
  22.1 1.9 fusion.7
  23.9 8.3 %all-to-all-start = ((bf16[16,36,384]{2,1,0:T(8,128)(2,1)}), bf16[16,36,384]{2,1,0:T(8,128)(2,1)}, u32[]{:S(2)}, u32[]{:S(2)}) async-start(bf16[16,36,384]{2,1,0:T(8,128)(2,1)} %fusion.7), calls=%async_computation | async-start | bytes 983040 | tf_op jit(solution)/shard_map/all_to_all | solution.py:38
  32.3 0.7 fusion
  33.1 16.2 %all-to-all-done = bf16[16,36,384]{2,1,0:T(8,128)(2,1)} async-done(((bf16[16,36,384]{2,1,0:T(8,128)(2,1)}), bf16[16,36,384]{2,1,0:T(8,128)(2,1)}, u32[]{:S(2)}, u32[]{:S(2)}) %all-to-all-start) | async-done | bytes 442400 | tf_op jit(solution)/shard_map/all_to_all | solution.py:38
  49.2 1.1 convert_reduce_fusion
  50.8 0.8 broadcast_in_dim.17
  51.6 6.8 %all-to-all-start.1 = ((bf16[16,32,384]{2,1,0:T(8,128)(2,1)}), bf16[16,32,384]{2,1,0:T(8,128)(2,1)S(1)}, u32[]{:S(2)}, u32[]{:S(2)}) async-start(bf16[16,32,384]{2,1,0:T(8,128)(2,1)} %broadcast_in_dim.17), calls=%async_computation.1 | async-start | bytes 786432 | tf_op jit(solution)/shard_map/all_to_all | solution.py:38
  58.4 2.3 fusion.1.protos_ref
  60.7 13.8 %all-to-all-done.1 = bf16[16,32,384]{2,1,0:T(8,128)(2,1)S(1)} async-done(((bf16[16,32,384]{2,1,0:T(8,128)(2,1)}), bf16[16,32,384]{2,1,0:T(8,128)(2,1)S(1)}, u32[]{:S(2)}, u32[]{:S(2)}) %all-to-all-start.1) | async-done | bytes 393248 | tf_op jit(solution)/shard_map/all_to_all | solution.py:38
  74.5 3.4 %shard_map.111 = (bf16[512,4096]{1,0:T(8,128)(2,1)S(1)}, bf16[16,32,128]{2,1,0:T(8,128)(2,1)S(1)}) custom-call(bf16[512,384]{1,0:T(8,128)(2,1)S(1)} %bitcast.45, bf16[4096,384]{1,0:T(8,128)(2,1)S(1)} %fusion.1.protos_ref), custom_call_target="tpu_custom_call" | custom-call | flops 1610612736 | bytes 4194304 | tf_op jit(solution)/shard_map/pallas_call | solution.py:501
  77.9 16.9 %all_to_all.55.got_ref = bf16[16,32,128]{2,1,0:T(8,128)(2,1)S(1)} all-to-all(bf16[16,32,128]{2,1,0:T(8,128)(2,1)S(1)} %get-tuple-element.59), channel_id=1, replica_groups=mesh['dp'=16,'proto'=16] {'dp'}, dimensions={0} | all-to-all | bytes 262144 | tf_op jit(solution)/shard_map/all_to_all | solution.py:38
  94.8 1.4 shard_map.112
  96.2 11.6 %all_to_all.56.got_ref = f32[16,4,128]{2,1,0:T(4,128)S(1)} all-to-all(f32[16,4,128]{2,1,0:T(4,128)S(1)} %shard_map.112), channel_id=1, replica_groups=mesh['dp'=16,'proto'=16] {'proto'}, dimensions={0} | all-to-all | bytes 65536 | tf_op jit(solution)/shard_map/all_to_all | solution.py:38
  107.7 1.6 shard_map.113
  109.4 12.2 %all_to_all.57.got_ref = bf16[16,32,128]{2,1,0:T(8,128)(2,1)S(1)} all-to-all(bf16[16,32,128]{2,1,0:T(8,128)(2,1)S(1)} %shard_map.113), channel_id=1, replica_groups=mesh['dp'=16,'proto'=16] {'dp'}, dimensions={0} | all-to-all | bytes 262144 | tf_op jit(solution)/shard_map/all_to_all | solution.py:38
  121.5 1.4 shard_map.114
  122.9 9.9 %all_to_all.58.got_ref = f32[16,4,128]{2,1,0:T(4,128)S(1)} all-to-all(f32[16,4,128]{2,1,0:T(4,128)S(1)} %shard_map.114), channel_id=1, replica_groups=mesh['dp'=16,'proto'=16] {'proto'}, dimensions={0} | all-to-all | bytes 65536 | tf_op jit(solution)/shard_map/all_to_all | solution.py:38
  132.8 1.6 shard_map.115
  135.1 1.8 copy-done.5
  136.9 0.9 copy-done.9
  137.8 1.6 shard_map.116
  139.4 0.7 copy-done.13
  140.1 5.7 %shard_map.117 = (bf16[512,4096]{1,0:T(8,128)(2,1)S(1)}, f32[512,384]{1,0:T(8,128)S(1)}, f32[4,128]{1,0:T(4,128)S(1)}) custom-call(bf16[512,384]{1,0:T(8,128)(2,1)S(1)} %get-tuple-element.64.student_ref, bf16[4096,384]{1,0:T(8,128)(2,1)S(1)} %fusion.1.protos_ref), custom_call_target="tpu_custom_call" | custom-call | flops 3221225472 | bytes 4194304 | tf_op jit(solution)/shard_map/pallas_call | solution.py:511
  145.9 11.9 %all_to_all.59.got_ref = bf16[16,32,128]{2,1,0:T(8,128)(2,1)S(1)} all-to-all(bf16[16,32,128]{2,1,0:T(8,128)(2,1)S(1)} %copy-done.7), channel_id=1, replica_groups=mesh['dp'=16,'proto'=16] {'dp'}, dimensions={0} | all-to-all | bytes 262144 | tf_op jit(solution)/shard_map/all_to_all | solution.py:38
  157.8 3.6 %shard_map.118 = (f32[16,12,128]{2,1,0:T(8,128)S(1)}, f32[512,384]{1,0:T(8,128)S(1)}, f32[32,128]{1,0:T(8,128)S(1)}) custom-call(bf16[16,32,128]{2,1,0:T(8,128)(2,1)S(1)} %all_to_all.59.got_ref, f32[4,128]{1,0:T(4,128)S(1)} %get-tuple-element.70.partition_ref, bf16[512,4096]{1,0:T(8,128)(2,1)S(1)} %copy-done.1, ...), custom_call_target="tpu_custom_call" | custom-call | flops 1610612736 | bytes 4194304 | tf_op jit(solution)/shard_map/pallas_call | solution.py:515
  161.4 10.0 %all_to_all.60.got_ref = f32[16,12,128]{2,1,0:T(8,128)S(1)} all-to-all(f32[16,12,128]{2,1,0:T(8,128)S(1)} %get-tuple-element.71), channel_id=1, replica_groups=mesh['dp'=16,'proto'=16] {'proto'}, dimensions={0} | all-to-all | bytes 196608 | tf_op jit(solution)/shard_map/all_to_all | solution.py:38
  171.4 5.2 %shard_map.119 = (bf16[512,384]{1,0:T(8,128)(2,1)}, f32[4,128]{1,0:T(4,128)S(1)}, f32[512,128]{1,0:T(8,128)S(1)}, f32[512,128]{1,0:T(8,128)S(1)}, bf16[8,384,256]{2,1,0:T(8,128)(2,1)}) custom-call(s32[1]{0:T(128)} %bitcast.8.core_ref, f32[16,12,128]{2,1,0:T(8,128)S(1)} %all_to_all.60.got_ref, f32[512,384]{1,0:T(8,128)S(1)} %get-tuple-element.72.pulled_ref, ...), custom_call_target="tpu_custom_call" | custom-call | flops 805306368 | bytes 5767168 | tf_op jit(solution)/shard_map/pallas_call | solution.py:516
  177.2 2.1 collective-permute-start.2
  179.3 3.6 %all-to-all-start.8 = ((bf16[16,32,384]{2,1,0:T(8,128)(2,1)}), bf16[16,32,384]{2,1,0:T(8,128)(2,1)S(1)}, u32[]{:S(2)}, u32[]{:S(2)}) async-start(bf16[16,32,384]{2,1,0:T(8,128)(2,1)} %bitcast.13), calls=%async_computation.8 | async-start | bytes 786432 | tf_op jit(solution)/shard_map/all_to_all | solution.py:38
  182.9 2.2 copy-done.2
  185.1 2.2 copy-done.4
  187.3 3.5 %shard_map.120 = bf16[8,384,256]{2,1,0:T(8,128)(2,1)S(1)} custom-call(s32[1]{0:T(128)} %bitcast.9.core_ref, bf16[384,512]{1,0:T(8,128)(2,1)S(1)} %get-tuple-element.74.turned_ref, f32[512,128]{1,0:T(8,128)S(1)} %get-tuple-element.87.wanted_ref, f32[512,128]{1,0:T(8,128)S(1)} %get-tuple-element.88.given_ref, f32[32,128]{1,0:T(8,128)S(1)} %get-tuple-element.75.scale_ref, ...), custom_call_target="tpu_custom_call" | custom-call | flops 805306368 | bytes 5767168 | tf_op jit(solution)/shard_map/pallas_call | solution.py:528
  190.8 0.8 constant_dynamic-slice_fusion.1.factor_ref
  191.6 0.8 constant_dynamic-slice_fusion.2.unit_ref
  192.4 1.2 shard_map.121
  193.7 0.7 copy-done.14
  195.1 0.9 shard_map.122
  196.0 7.0 %all-to-all-start.9 = ((bf16[16,32,384]{2,1,0:T(8,128)(2,1)}), bf16[16,32,384]{2,1,0:T(8,128)(2,1)S(1)}, u32[]{:S(2)}, u32[]{:S(2)}) async-start(bf16[16,32,384]{2,1,0:T(8,128)(2,1)} %shard_map.122), calls=%async_computation.9 | async-start | bytes 786432 | tf_op jit(solution)/shard_map/all_to_all | solution.py:38
  203.2 1.9 collective-permute-start.4
  205.1 1.0 collective-permute-start.5
  206.1 1.0 constant_dynamic-slice_fusion
  207.3 6.8 %all-to-all-done.9 = bf16[16,32,384]{2,1,0:T(8,128)(2,1)S(1)} async-done(((bf16[16,32,384]{2,1,0:T(8,128)(2,1)}), bf16[16,32,384]{2,1,0:T(8,128)(2,1)S(1)}, u32[]{:S(2)}, u32[]{:S(2)}) %all-to-all-start.9) | async-done | bytes 393248 | tf_op jit(solution)/shard_map/all_to_all | solution.py:38
  214.3 1.1 collective-permute-done.3
  215.4 6.6 %collective-permute-done.4 = bf16[2,384,256]{2,1,0:T(8,128)(2,1)S(1)} collective-permute-done((bf16[2,384,256]{2,1,0:T(8,128)(2,1)S(1)}, bf16[2,384,256]{2,1,0:T(8,128)(2,1)S(1)}, u32[]{:S(2)}, u32[]{:S(2)}) %collective-permute-start.4) | collective-permute-done | bytes 393248 | tf_op jit(solution)/shard_map/ppermute | solution.py:452
  222.0 1.2 collective-permute-done.5
  223.2 0.9 broadcast_in_dim.25
  224.1 5.6 %all-to-all-start.10 = ((bf16[8,96,384]{2,1,0:T(8,128)(2,1)}), bf16[8,96,384]{2,1,0:T(8,128)(2,1)S(1)}, u32[]{:S(2)}, u32[]{:S(2)}) async-start(bf16[8,96,384]{2,1,0:T(8,128)(2,1)} %broadcast_in_dim.25), calls=%async_computation.10 | async-start | bytes 1179648 | tf_op jit(solution)/shard_map/all_to_all | solution.py:540
  229.9 2.7 %collective-permute-start.7 = (bf16[384,256]{1,0:T(8,128)(2,1)S(1)}, bf16[384,256]{1,0:T(8,128)(2,1)S(1)}, u32[]{:S(2)}, u32[]{:S(2)}) collective-permute-start(bf16[384,256]{1,0:T(8,128)(2,1)S(1)} %dynamic-slice_bitcast_fusion), channel_id=1, source_target_pairs={{0,128},{16,144},{32,160},{48,176},{64,192},{80,208},{96,224},{112... | collective-permute-start | bytes 589832 | tf_op jit(solution)/shard_map/ppermute | solution.py:56
  232.6 0.8 select_reduce_fusion
  233.5 4.6 %collective-permute-done.7 = bf16[384,256]{1,0:T(8,128)(2,1)S(1)} collective-permute-done((bf16[384,256]{1,0:T(8,128)(2,1)S(1)}, bf16[384,256]{1,0:T(8,128)(2,1)S(1)}, u32[]{:S(2)}, u32[]{:S(2)}) %collective-permute-start.7) | collective-permute-done | bytes 196640 | tf_op jit(solution)/shard_map/ppermute | solution.py:56
  238.1 1.7 all-to-all-done.10
  240.0 2.7 %collective-permute-start.6 = (bf16[96,384]{1,0:T(8,128)(2,1)S(1)}, bf16[96,384]{1,0:T(8,128)(2,1)S(1)}, u32[]{:S(2)}, u32[]{:S(2)}) collective-permute-start(bf16[96,384]{1,0:T(8,128)(2,1)S(1)} %reduce_sum.123), channel_id=1, source_target_pairs={{0,128},{16,144},{32,160},{48,176},{64,192},{80,208},{96,224},{112... | collective-permute-start | bytes 221192 | tf_op jit(solution)/shard_map/ppermute | solution.py:56
  242.8 0.9 copy.23
  243.7 1.1 collective-permute-done.6
  (81 shorter events, 6.9 us)
Async XLA Ops:
  7.2 25.2 %copy-start.17 = (bf16[4096,384]{1,0:T(8,128)(2,1)S(1)}, bf16[4096,384]{1,0:T(8,128)(2,1)}, u32[]{:S(2)}) copy-start(bf16[4096,384]{1,0:T(8,128)(2,1)} %param.14) | copy-start | bytes 9437188
  7.2 127.9 %all-gather.2.cloned.1.call-start = ((), (), s32[]{:S(2)}) async-start(), calls=%async_computation.11 | async-start | bytes 2924544 | tf_op jit(solution)/shard_map/all_gather | solution.py:484
  7.2 7.6 %collective-permute-start = (bf16[512,96]{0,1:T(8,128)(2,1)}, bf16[512,96]{0,1:T(8,128)(2,1)S(1)}, u32[]{:S(2)}, u32[]{:S(2)}) collective-permute-start(bf16[512,96]{0,1:T(8,128)(2,1)} %param.8), channel_id=1, source_target_pairs={{0,128},{16,144},{32,160},{48,176},{64,192},{80,208},{96,224},{112... | collective-permute-start | bytes 294920 | tf_op jit(solution)/shard_map/ppermute | solution.py:56
  11.7 0.8 copy-start.21
  12.4 4.2 %copy-start.23 = (f32[96]{0:T(128)}, f32[96]{0:T(128)S(1)}, u32[]{:S(2)}) copy-start(f32[96]{0:T(128)S(1)} %dynamic_slice.21) | copy-start | bytes 1156
  14.1 3.7 %copy-start.18 = (f32[384]{0:T(512)}, f32[384]{0:T(512)S(1)}, u32[]{:S(2)}) copy-start(f32[384]{0:T(512)S(1)} %get-tuple-element.125) | copy-start | bytes 4612
  14.8 1.8 copy-start.19
  16.0 0.6 copy-start.8
  23.9 25.3 %all-to-all-start = ((bf16[16,36,384]{2,1,0:T(8,128)(2,1)}), bf16[16,36,384]{2,1,0:T(8,128)(2,1)}, u32[]{:S(2)}, u32[]{:S(2)}) async-start(bf16[16,36,384]{2,1,0:T(8,128)(2,1)} %fusion.7), calls=%async_computation | async-start | bytes 983040 | tf_op jit(solution)/shard_map/all_to_all | solution.py:38
  51.6 22.9 %all-to-all-start.1 = ((bf16[16,32,384]{2,1,0:T(8,128)(2,1)}), bf16[16,32,384]{2,1,0:T(8,128)(2,1)S(1)}, u32[]{:S(2)}, u32[]{:S(2)}) async-start(bf16[16,32,384]{2,1,0:T(8,128)(2,1)} %broadcast_in_dim.17), calls=%async_computation.1 | async-start | bytes 786432 | tf_op jit(solution)/shard_map/all_to_all | solution.py:38
  77.9 55.0 %copy-start = (bf16[512,4096]{1,0:T(8,128)(2,1)}, bf16[512,4096]{1,0:T(8,128)(2,1)S(1)}, u32[]{:S(2)}) copy-start(bf16[512,4096]{1,0:T(8,128)(2,1)S(1)} %get-tuple-element.60.energy_ref) | copy-start | bytes 12582916
  134.5 0.7 copy-start.6
  135.1 1.8 copy-start.5
  136.9 0.9 copy-start.9
  139.4 0.7 copy-start.13
  140.1 5.7 %copy-start.10 = (bf16[96,512]{1,0:T(8,128)(2,1)}, bf16[96,512]{1,0:T(8,128)(2,1)S(1)}, u32[]{:S(2)}) copy-start(bf16[96,512]{1,0:T(8,128)(2,1)S(1)} %get-tuple-element.83) | copy-start | bytes 294916
  140.1 5.7 %copy-start.12 = (f32[512,384]{1,0:T(8,128)}, f32[512,384]{1,0:T(8,128)S(1)}, u32[]{:S(2)}) copy-start(f32[512,384]{1,0:T(8,128)S(1)} %get-tuple-element.95) | copy-start | bytes 2359300
  140.1 5.7 %copy-start.7 = (bf16[16,32,128]{2,1,0:T(8,128)(2,1)S(1)}, bf16[16,32,128]{2,1,0:T(8,128)(2,1)}, u32[]{:S(2)}) copy-start(bf16[16,32,128]{2,1,0:T(8,128)(2,1)} %copy-done.6) | copy-start | bytes 393220
  140.1 17.7 %copy-start.1 = (bf16[512,4096]{1,0:T(8,128)(2,1)S(1)}, bf16[512,4096]{1,0:T(8,128)(2,1)}, u32[]{:S(2)}) copy-start(bf16[512,4096]{1,0:T(8,128)(2,1)} %copy-done) | copy-start | bytes 12582916
  145.8 25.6 %copy-start.3 = (bf16[512,4096]{1,0:T(8,128)(2,1)}, bf16[512,4096]{1,0:T(8,128)(2,1)S(1)}, u32[]{:S(2)}) copy-start(bf16[512,4096]{1,0:T(8,128)(2,1)S(1)} %get-tuple-element.76.exponent_ref) | copy-start | bytes 12582916
  176.6 0.6 copy-start.15
  177.2 15.2 %collective-permute-start.2 = (bf16[8,384,256]{2,1,0:T(8,128)(2,1)}, bf16[8,384,256]{2,1,0:T(8,128)(2,1)S(1)}, u32[]{:S(2)}, u32[]{:S(2)}) collective-permute-start(bf16[8,384,256]{2,1,0:T(8,128)(2,1)} %get-tuple-element.89), channel_id=1, source_target_pairs={{0,16},{16,0},{32,48},{48,32},{64,80},{80,64},{96,112},{112,96},{1... | collective-permute-start | bytes 4718600 | tf_op jit(solution)/shard_map/ppermute | solution.py:56
  179.3 15.7 %all-to-all-start.8 = ((bf16[16,32,384]{2,1,0:T(8,128)(2,1)}), bf16[16,32,384]{2,1,0:T(8,128)(2,1)S(1)}, u32[]{:S(2)}, u32[]{:S(2)}) async-start(bf16[16,32,384]{2,1,0:T(8,128)(2,1)} %bitcast.13), calls=%async_computation.8 | async-start | bytes 786432 | tf_op jit(solution)/shard_map/all_to_all | solution.py:38
  182.9 2.2 copy-start.2
  185.1 2.2 copy-start.4
  190.8 12.2 %copy-start.16 = (f32[4,128]{1,0:T(4,128)S(1)}, f32[4,128]{1,0:T(4,128)}, u32[]{:S(2)}) copy-start(f32[4,128]{1,0:T(4,128)} %copy-done.15) | copy-start | bytes 6148
  190.8 23.3 %copy-start.11 = (bf16[96,512]{1,0:T(8,128)(2,1)S(1)}, bf16[96,512]{1,0:T(8,128)(2,1)}, u32[]{:S(2)}) copy-start(bf16[96,512]{1,0:T(8,128)(2,1)} %copy-done.10) | copy-start | bytes 294916
  190.8 23.3 %copy-start.22 = (f32[96]{0:T(128)S(1)}, f32[96]{0:T(128)}, u32[]{:S(2)}) copy-start(f32[96]{0:T(128)} %copy-done.21) | copy-start | bytes 1156
  193.7 0.8 copy-start.14
  196.0 36.7 %copy-start.20 = (s32[512]{0:T(512)S(1)}, s32[512]{0:T(512)}, u32[]{:S(2)}) copy-start(s32[512]{0:T(512)} %copy-done.19) | copy-start | bytes 6148
  196.0 18.2 %all-to-all-start.9 = ((bf16[16,32,384]{2,1,0:T(8,128)(2,1)}), bf16[16,32,384]{2,1,0:T(8,128)(2,1)S(1)}, u32[]{:S(2)}, u32[]{:S(2)}) async-start(bf16[16,32,384]{2,1,0:T(8,128)(2,1)} %shard_map.122), calls=%async_computation.9 | async-start | bytes 786432 | tf_op jit(solution)/shard_map/all_to_all | solution.py:38
  203.0 29.6 %collective-permute-start.1 = (f32[4,128]{1,0:T(4,128)S(1)}, f32[4,128]{1,0:T(4,128)S(1)}, u32[]{:S(2)}, u32[]{:S(2)}) collective-permute-start(f32[4,128]{1,0:T(4,128)S(1)} %copy-done.16), channel_id=1, source_target_pairs={{0,128},{16,144},{32,160},{48,176},{64,192},{80,208},{96,224},{112... | collective-permute-start | bytes 6152 | tf_op jit(solution)/shard_map/ppermute | solution.py:56
  203.2 12.2 %collective-permute-start.3 = (bf16[2,384,256]{2,1,0:T(8,128)(2,1)}, bf16[2,384,256]{2,1,0:T(8,128)(2,1)S(1)}, u32[]{:S(2)}, u32[]{:S(2)}) collective-permute-start(bf16[2,384,256]{2,1,0:T(8,128)(2,1)} %copy-done.14), channel_id=1, source_target_pairs={{0,32},{16,48},{32,64},{48,80},{64,96},{80,112},{96,0},{112,16},{1... | collective-permute-start | bytes 1179656 | tf_op jit(solution)/shard_map/ppermute | solution.py:452
  203.2 18.7 %collective-permute-start.4 = (bf16[2,384,256]{2,1,0:T(8,128)(2,1)S(1)}, bf16[2,384,256]{2,1,0:T(8,128)(2,1)S(1)}, u32[]{:S(2)}, u32[]{:S(2)}) collective-permute-start(bf16[2,384,256]{2,1,0:T(8,128)(2,1)S(1)} %get-tuple-element.100), channel_id=1, source_target_pairs={{0,64},{16,80},{32,96},{48,112},{64,0},{80,16},{96,32},{112,48},{1... | collective-permute-start | bytes 1179656 | tf_op jit(solution)/shard_map/ppermute | solution.py:452
  205.1 18.1 %collective-permute-start.5 = (bf16[2,384,256]{2,1,0:T(8,128)(2,1)S(1)}, bf16[2,384,256]{2,1,0:T(8,128)(2,1)S(1)}, u32[]{:S(2)}, u32[]{:S(2)}) collective-permute-start(bf16[2,384,256]{2,1,0:T(8,128)(2,1)S(1)} %get-tuple-element.101), channel_id=1, source_target_pairs={{0,96},{16,112},{32,0},{48,16},{64,32},{80,48},{96,64},{112,80},{1... | collective-permute-start | bytes 1179656 | tf_op jit(solution)/shard_map/ppermute | solution.py:452
  224.1 15.8 %all-to-all-start.10 = ((bf16[8,96,384]{2,1,0:T(8,128)(2,1)}), bf16[8,96,384]{2,1,0:T(8,128)(2,1)S(1)}, u32[]{:S(2)}, u32[]{:S(2)}) async-start(bf16[8,96,384]{2,1,0:T(8,128)(2,1)} %broadcast_in_dim.25), calls=%async_computation.10 | async-start | bytes 1179648 | tf_op jit(solution)/shard_map/all_to_all | solution.py:540
  229.9 8.1 %collective-permute-start.7 = (bf16[384,256]{1,0:T(8,128)(2,1)S(1)}, bf16[384,256]{1,0:T(8,128)(2,1)S(1)}, u32[]{:S(2)}, u32[]{:S(2)}) collective-permute-start(bf16[384,256]{1,0:T(8,128)(2,1)S(1)} %dynamic-slice_bitcast_fusion), channel_id=1, source_target_pairs={{0,128},{16,144},{32,160},{48,176},{64,192},{80,208},{96,224},{112... | collective-permute-start | bytes 589832 | tf_op jit(solution)/shard_map/ppermute | solution.py:56
  240.0 4.8 %collective-permute-start.6 = (bf16[96,384]{1,0:T(8,128)(2,1)S(1)}, bf16[96,384]{1,0:T(8,128)(2,1)S(1)}, u32[]{:S(2)}, u32[]{:S(2)}) collective-permute-start(bf16[96,384]{1,0:T(8,128)(2,1)S(1)} %reduce_sum.123), channel_id=1, source_target_pairs={{0,128},{16,144},{32,160},{48,176},{64,192},{80,208},{96,224},{112... | collective-permute-start | bytes 221192 | tf_op jit(solution)/shard_map/ppermute | solution.py:56
Sparse Core Ops, SparseCore 0:
  16.8 78.9 all-gather.1

commit v9 on v8

--- a/solution.py
+++ b/solution.py
@@ -56,34 +56,17 @@
     return lax.ppermute(value, axis, [(one, one ^ bit) for one in range(count)])
 
 
-def partial_hidden(features, gain, weight):
-    scaled = (gain[:, None] * weight.astype(BF16).astype(F32)).astype(BF16)
-    share = jnp.dot(features, scaled, preferred_element_type=F32)
-    column = jnp.sum(scaled.astype(F32), axis=0)
-    values = features.astype(F32)
-    return share, column, jnp.sum(values, axis=1), jnp.sum(values * values, axis=1)
-
-
 def center_and_scale(first, second):
     center = first / D
     return center, lax.rsqrt(second / D - center * center + EPSILON)
 
 
-def packed_shares(features, gain, weight, parts):
-    crops, size = features.shape[0], weight.shape[1]
-    own = crops // parts
-    share, column, first, second = partial_hidden(features, gain, weight)
-    sums = jnp.stack(three_terms(jnp.stack([first, second])))
-    sums = sums.reshape(6, parts, own).transpose(1, 0, 2).reshape(parts, 1, 6 * own)
-    sums = jnp.pad(sums, ((0, 0), (0, 0), (0, size - 6 * own)))
-    columns = jnp.broadcast_to(jnp.stack(three_terms(column))[None], (parts, 3, size))
-    return jnp.concatenate([share.astype(BF16).reshape(parts, own, size), columns, sums], 1)
-
-
 def summed_hidden(packed):
-    own = packed.shape[1] - 4
+    own = packed.shape[1] - 5
     packed = jnp.sum(packed.astype(F32), axis=0)
-    sums = jnp.sum(packed[own + 3, : 6 * own].reshape(3, 2, own), axis=0)
+    sums = jnp.sum(packed[own + 3 :].reshape(2, 3, LANES), axis=1)
+    at = (lax.axis_index("proto") % (LANES // own) * own).astype(jnp.uint32)
+    sums = lax.dynamic_slice(sums, (jnp.uint32(0), at), (2, own))
     center, scale = center_and_scale(sums[0][:, None], sums[1][:, None])
     column = jnp.sum(packed[own : own + 3], axis=0)[None]
     return scale * (packed[:own] - center * column)
@@ -110,6 +93,23 @@
     for one in range(1, ref.shape[0]):
         total = total + ref[one].astype(F32)
     return total
+
+
+def pack_kernel(features_ref, gain_ref, weight_ref, out_ref):
+    scaled = (gain_ref[...] * weight_ref[...].astype(BF16).astype(F32)).astype(BF16)
+    share = contract_first(features_ref[...], scaled)
+    values = features_ref[...].astype(F32)
+    columns, first, second = (
+        [term.astype(F32) for term in three_terms(jnp.sum(one, axis=0, keepdims=True))]
+        for one in (scaled.astype(F32), values, values * values)
+    )
+    parts = out_ref.shape[0]
+    own = share.shape[0] // parts
+    for part in range(parts):
+        low = part * own // LANES * LANES
+        lines = [jnp.concatenate([term[:, low : low + LANES] for term in terms], 1) for terms in (first, second)]
+        block = jnp.concatenate([share[part * own : (part + 1) * own], *columns, *lines], 0)
+        out_ref[part] = block.astype(BF16)
 
 
 def energy_kernel(teacher_ref, protos_ref, energy_ref, sums_ref, held):
@@ -346,6 +346,12 @@
     row_sent = (array((parts, lines, LANES), F32), whole((parts, lines, LANES)))
     tall = pltpu.VMEM((crops, LANES), F32)
     short = pltpu.VMEM((tiles, LANES), F32)
+    own, width = crops // parts, D // parts
+    pack = called(
+        pack_kernel, 1, [whole((width, crops)), whole((width, 1)), whole((width, size))],
+        [(array((parts, own + 5, size), BF16), whole((parts, own + 5, size)))],
+        [], 2 * crops * width * size, 2 * crops * size,
+    )
     energy = called(
         energy_kernel, steps, [whole((crops, size)), down],
         [(array((crops, protos), BF16), across), col_sent],
@@ -445,7 +451,7 @@
         compiler_params=params,
         cost_estimate=cost,
     )
-    return energy, rows, cols, student, last, unit_grad, hidden_grad, proto_grad, pair_sum, student_hidden
+    return energy, rows, cols, student, last, unit_grad, hidden_grad, proto_grad, pair_sum, student_hidden, pack
 
 
 def along_y(value, step):
@@ -471,7 +477,9 @@
     gain_s = lax.dynamic_slice_in_dim(student_gain, start, width)
     gain_t = lax.dynamic_slice_in_dim(teacher_gain, start, width)
 
-    teacher_blocks = packed_shares(teacher_cls, gain_t, teacher_proj, parts)
+    protos = prototypes.shape[0]
+    calls = make_calls(crops, protos, size, lax.axis_size("dp"), parts)
+    (teacher_blocks,) = calls[-1](teacher_cls.T, gain_t[:, None], teacher_proj)
     teacher_hidden = summed_hidden(exchanged(teacher_blocks, "proto"))
     teacher_unit = unit_rows(teacher_hidden)[0].astype(BF16)
     teacher_all = from_all(teacher_unit, "proto").reshape(crops, size)
@@ -485,10 +493,8 @@
 
     proto_unit32, proto_factor = unit_rows(prototypes.astype(F32))
     proto_unit = proto_unit32.astype(BF16)
-    protos = proto_unit.shape[0]
-    calls = make_calls(crops, protos, size, lax.axis_size("dp"), parts)
     energy_call, row_call, col_call, student_call, last_call = calls[:5]
-    unit_grad_call, hidden_grad_call, proto_grad_call, pair_sum_call, student_hidden_call = calls[5:]
+    unit_grad_call, hidden_grad_call, proto_grad_call, pair_sum_call, student_hidden_call = calls[5:-1]
     me = lax.axis_index("dp")
     count = protos // lax.axis_size("dp")
     across = me // 8

time: 255 us -> 248 us (0.973)
  waiting for transfers between devices: 53.7 us -> 44.8 us
  blocking collectives: 72.5 us -> 75.8 us
  other arithmetic: 13.8 us -> 11 us
    all_to_all x4, waiting for transfers between devices: 37.4 us -> 28.7 us  [exchanged(): return lax.all_to_all(blocks, axis, 0, 0)]
    all_to_all x6, blocking collectives: 72.5 us -> 75.8 us  [exchanged(): return lax.all_to_all(blocks, axis, 0, 0)]
    unnamed x50 -> x46, local copies, waits for them, and re-layouts: 11.5 us -> 13.4 us
  transfers between devices with their start and end apart: 14 -> 14, of which waited for: 10 -> 9; matrix products, arithmetic and copies ran while one was open for 9% -> 7% of each run, Pallas kernels for 6% -> 6%
where the time goes in v9:
time: 248 us; the launch traced here: 245 us
  blocking collectives  75.8 us (31%)
  starting transfers between devices  47.4 us (19%)
  waiting for transfers between devices  44.8 us (18%)
  Pallas kernels  32.4 us (13%)
  local copies, waits for them, and re-layouts  18.7 us (8%)
  between operations  14.4 us (6%)
  other arithmetic  11 us (4%)
    all_to_all x6, blocking collectives, exchanged(): return lax.all_to_all(blocks, axis, 0, 0)  75.8 us
    all_to_all x4, waiting for transfers between devices, exchanged(): return lax.all_to_all(blocks, axis, 0, 0)  28.7 us
    all_to_all x4, starting transfers between devices, exchanged(): return lax.all_to_all(blocks, axis, 0, 0)  27.4 us
    unnamed x46, local copies, waits for them, and re-layouts  13.4 us
    ppermute x5, starting transfers between devices, swapped(): return lax.ppermute(value, axis, [(one, one ^ bit) for one in range(count)])  11.5 us
    ppermute x3, waiting for transfers between devices, along_y(): lax.ppermute(value, 'dp', [(one, one & 9 | one + 2 * step & 6) for one in...  8.8 us
    pallas_call x1, Pallas kernels, body(): fields = student_call(student_unit, proto_unit)  5.75 us
    all_to_all x1, starting transfers between devices, body(): lax.all_to_all(jnp.broadcast_to(share[None], (8,) + share.shape), 'dp', 0...  5.62 us
  transfers between devices with their start and end apart: 14, of which 9 were waited for; matrix products, arithmetic and copies ran while one was open for 7% of the time, Pallas kernels for 6%

profile of v9, /device:TPU:1, one launch (start us, length us, event | category | flops | bytes accessed | tf_op | source)
XLA Modules:
  0.0 245.2 jit_solution(5324644579535064318)
XLA Ops:
  7.2 3.7 %collective-permute-start = (bf16[512,96]{0,1:T(8,128)(2,1)}, bf16[512,96]{0,1:T(8,128)(2,1)S(1)}, u32[]{:S(2)}, u32[]{:S(2)}) collective-permute-start(bf16[512,96]{0,1:T(8,128)(2,1)} %param.8), channel_id=1, source_target_pairs={{0,128},{16,144},{32,160},{48,176},{64,192},{80,208},{96,224},{112... | collective-permute-start | bytes 294920 | tf_op jit(solution)/shard_map/ppermute | solution.py:56
  10.9 0.8 dynamic_slice.26
  11.7 1.6 fusion.13
  13.3 0.7 add_select_fusion
  14.4 0.7 pad_maximum_fusion
  15.1 0.6 copy-done.10
  16.0 0.9 copy-done.7
  16.9 0.9 copy-done.12
  17.8 1.1 shard_map.111
  18.9 8.6 %all-to-all-start = ((bf16[16,37,384]{2,1,0:T(8,128)(2,1)}), bf16[16,37,384]{2,1,0:T(8,128)(2,1)S(1)}, u32[]{:S(2)}, u32[]{:S(2)}) async-start(bf16[16,37,384]{2,1,0:T(8,128)(2,1)} %shard_map.111), calls=%async_computation | async-start | bytes 983040 | tf_op jit(solution)/shard_map/all_to_all | solution.py:38
  27.5 2.6 %fusion = f32[4096]{0:T(1024)S(1)} fusion(bf16[4096,384]{1,0:T(8,128)(2,1)} %param.14), kind=kLoop, calls=%fused_computation.2 | loop fusion | flops 4714496 | bytes 3162112 | tf_op jit(solution)/shard_map/reduce_sum | solution.py:33
  30.7 11.1 %all-to-all-done = bf16[16,37,384]{2,1,0:T(8,128)(2,1)S(1)} async-done(((bf16[16,37,384]{2,1,0:T(8,128)(2,1)}), bf16[16,37,384]{2,1,0:T(8,128)(2,1)S(1)}, u32[]{:S(2)}, u32[]{:S(2)}) %all-to-all-start) | async-done | bytes 454688 | tf_op jit(solution)/shard_map/all_to_all | solution.py:38
  42.3 0.8 broadcast_in_dim.21
  43.1 7.8 %all-to-all-start.1 = ((bf16[16,32,384]{2,1,0:T(8,128)(2,1)}), bf16[16,32,384]{2,1,0:T(8,128)(2,1)S(1)}, u32[]{:S(2)}, u32[]{:S(2)}) async-start(bf16[16,32,384]{2,1,0:T(8,128)(2,1)} %broadcast_in_dim.21), calls=%async_computation.1 | async-start | bytes 786432 | tf_op jit(solution)/shard_map/all_to_all | solution.py:38
  50.9 2.3 fusion.1.protos_ref
  53.2 10.8 %all-to-all-done.1 = bf16[16,32,384]{2,1,0:T(8,128)(2,1)S(1)} async-done(((bf16[16,32,384]{2,1,0:T(8,128)(2,1)}), bf16[16,32,384]{2,1,0:T(8,128)(2,1)S(1)}, u32[]{:S(2)}, u32[]{:S(2)}) %all-to-all-start.1) | async-done | bytes 393248 | tf_op jit(solution)/shard_map/all_to_all | solution.py:38
  64.0 3.4 %shard_map.112 = (bf16[512,4096]{1,0:T(8,128)(2,1)S(1)}, bf16[16,32,128]{2,1,0:T(8,128)(2,1)S(1)}) custom-call(bf16[512,384]{1,0:T(8,128)(2,1)S(1)} %bitcast.41, bf16[4096,384]{1,0:T(8,128)(2,1)S(1)} %fusion.1.protos_ref), custom_call_target="tpu_custom_call" | custom-call | flops 1610612736 | bytes 4194304 | tf_op jit(solution)/shard_map/pallas_call | solution.py:507
  67.4 20.5 %all_to_all.55.got_ref = bf16[16,32,128]{2,1,0:T(8,128)(2,1)S(1)} all-to-all(bf16[16,32,128]{2,1,0:T(8,128)(2,1)S(1)} %get-tuple-element.59), channel_id=1, replica_groups=mesh['dp'=16,'proto'=16] {'dp'}, dimensions={0} | all-to-all | bytes 262144 | tf_op jit(solution)/shard_map/all_to_all | solution.py:38
  87.8 1.4 shard_map.113
  89.2 11.0 %all_to_all.56.got_ref = f32[16,4,128]{2,1,0:T(4,128)S(1)} all-to-all(f32[16,4,128]{2,1,0:T(4,128)S(1)} %shard_map.113), channel_id=1, replica_groups=mesh['dp'=16,'proto'=16] {'proto'}, dimensions={0} | all-to-all | bytes 65536 | tf_op jit(solution)/shard_map/all_to_all | solution.py:38
  100.2 1.6 shard_map.114
  101.9 12.4 %all_to_all.57.got_ref = bf16[16,32,128]{2,1,0:T(8,128)(2,1)S(1)} all-to-all(bf16[16,32,128]{2,1,0:T(8,128)(2,1)S(1)} %shard_map.114), channel_id=1, replica_groups=mesh['dp'=16,'proto'=16] {'dp'}, dimensions={0} | all-to-all | bytes 262144 | tf_op jit(solution)/shard_map/all_to_all | solution.py:38
  114.3 1.4 shard_map.115
  115.6 9.9 %all_to_all.58.got_ref = f32[16,4,128]{2,1,0:T(4,128)S(1)} all-to-all(f32[16,4,128]{2,1,0:T(4,128)S(1)} %shard_map.115), channel_id=1, replica_groups=mesh['dp'=16,'proto'=16] {'proto'}, dimensions={0} | all-to-all | bytes 65536 | tf_op jit(solution)/shard_map/all_to_all | solution.py:38
  125.6 1.6 shard_map.116
  127.2 0.6 copy-done.8
  127.9 1.8 copy-done.6
  129.6 0.9 copy-done.11
  130.5 1.6 shard_map.117
  132.1 0.7 copy-done.18
  132.9 5.8 %shard_map.118 = (bf16[512,4096]{1,0:T(8,128)(2,1)S(1)}, f32[512,384]{1,0:T(8,128)S(1)}, f32[4,128]{1,0:T(4,128)S(1)}) custom-call(bf16[512,384]{1,0:T(8,128)(2,1)S(1)} %get-tuple-element.64.student_ref, bf16[4096,384]{1,0:T(8,128)(2,1)S(1)} %fusion.1.protos_ref), custom_call_target="tpu_custom_call" | custom-call | flops 3221225472 | bytes 4194304 | tf_op jit(solution)/shard_map/pallas_call | solution.py:517
  138.7 12.0 %all_to_all.59.got_ref = bf16[16,32,128]{2,1,0:T(8,128)(2,1)S(1)} all-to-all(bf16[16,32,128]{2,1,0:T(8,128)(2,1)S(1)} %copy-done.9), channel_id=1, replica_groups=mesh['dp'=16,'proto'=16] {'dp'}, dimensions={0} | all-to-all | bytes 262144 | tf_op jit(solution)/shard_map/all_to_all | solution.py:38
  150.6 3.7 %shard_map.119 = (f32[16,12,128]{2,1,0:T(8,128)S(1)}, f32[512,384]{1,0:T(8,128)S(1)}, f32[32,128]{1,0:T(8,128)S(1)}) custom-call(bf16[16,32,128]{2,1,0:T(8,128)(2,1)S(1)} %all_to_all.59.got_ref, f32[4,128]{1,0:T(4,128)S(1)} %get-tuple-element.70.partition_ref, bf16[512,4096]{1,0:T(8,128)(2,1)S(1)} %copy-done.2, ...), custom_call_target="tpu_custom_call" | custom-call | flops 1610612736 | bytes 4194304 | tf_op jit(solution)/shard_map/pallas_call | solution.py:521
  154.3 10.0 %all_to_all.60.got_ref = f32[16,12,128]{2,1,0:T(8,128)S(1)} all-to-all(f32[16,12,128]{2,1,0:T(8,128)S(1)} %get-tuple-element.71), channel_id=1, replica_groups=mesh['dp'=16,'proto'=16] {'proto'}, dimensions={0} | all-to-all | bytes 196608 | tf_op jit(solution)/shard_map/all_to_all | solution.py:38
  164.3 5.3 %shard_map.120 = (bf16[512,384]{1,0:T(8,128)(2,1)}, f32[4,128]{1,0:T(4,128)S(1)}, f32[512,128]{1,0:T(8,128)S(1)}, f32[512,128]{1,0:T(8,128)S(1)}, bf16[8,384,256]{2,1,0:T(8,128)(2,1)}) custom-call(s32[1]{0:T(128)} %bitcast.5.core_ref, f32[16,12,128]{2,1,0:T(8,128)S(1)} %all_to_all.60.got_ref, f32[512,384]{1,0:T(8,128)S(1)} %get-tuple-element.72.pulled_ref, ...), custom_call_target="tpu_custom_call" | custom-call | flops 805306368 | bytes 5767168 | tf_op jit(solution)/shard_map/pallas_call | solution.py:522
  169.6 2.1 collective-permute-start.2
  171.7 3.6 %all-to-all-start.8 = ((bf16[16,32,384]{2,1,0:T(8,128)(2,1)}), bf16[16,32,384]{2,1,0:T(8,128)(2,1)S(1)}, u32[]{:S(2)}, u32[]{:S(2)}) async-start(bf16[16,32,384]{2,1,0:T(8,128)(2,1)} %bitcast.10), calls=%async_computation.8 | async-start | bytes 786432 | tf_op jit(solution)/shard_map/all_to_all | solution.py:38
  175.3 2.2 copy-done.3
  177.5 2.2 copy-done.5
  179.7 0.7 copy-done.16
  180.4 3.5 %shard_map.121 = bf16[8,384,256]{2,1,0:T(8,128)(2,1)S(1)} custom-call(s32[1]{0:T(128)} %bitcast.6.core_ref, bf16[384,512]{1,0:T(8,128)(2,1)S(1)} %get-tuple-element.74.turned_ref, f32[512,128]{1,0:T(8,128)S(1)} %get-tuple-element.87.wanted_ref, f32[512,128]{1,0:T(8,128)S(1)} %get-tuple-element.88.given_ref, f32[32,128]{1,0:T(8,128)S(1)} %copy-done.16, ...), custom_call_target="tpu_custom_call" | custom-call | flops 805306368 | bytes 5767168 | tf_op jit(solution)/shard_map/pallas_call | solution.py:534
  183.9 0.8 constant_dynamic-slice_fusion.1.factor_ref
  184.7 0.8 constant_dynamic-slice_fusion.2.unit_ref
  185.5 1.2 shard_map.122
  186.8 0.7 copy-done.19
  187.5 0.9 shard_map.123
  188.4 7.5 %all-to-all-start.9 = ((bf16[16,32,384]{2,1,0:T(8,128)(2,1)}), bf16[16,32,384]{2,1,0:T(8,128)(2,1)S(1)}, u32[]{:S(2)}, u32[]{:S(2)}) async-start(bf16[16,32,384]{2,1,0:T(8,128)(2,1)} %shard_map.123), calls=%async_computation.9 | async-start | bytes 786432 | tf_op jit(solution)/shard_map/all_to_all | solution.py:38
  196.2 1.9 collective-permute-start.4
  198.1 0.9 collective-permute-start.5
  199.0 1.0 constant_dynamic-slice_fusion
  200.2 6.9 %all-to-all-done.9 = bf16[16,32,384]{2,1,0:T(8,128)(2,1)S(1)} async-done(((bf16[16,32,384]{2,1,0:T(8,128)(2,1)}), bf16[16,32,384]{2,1,0:T(8,128)(2,1)S(1)}, u32[]{:S(2)}, u32[]{:S(2)}) %all-to-all-start.9) | async-done | bytes 393248 | tf_op jit(solution)/shard_map/all_to_all | solution.py:38
  207.3 0.9 collective-permute-done.3
  208.2 6.8 %collective-permute-done.4 = bf16[2,384,256]{2,1,0:T(8,128)(2,1)S(1)} collective-permute-done((bf16[2,384,256]{2,1,0:T(8,128)(2,1)S(1)}, bf16[2,384,256]{2,1,0:T(8,128)(2,1)S(1)}, u32[]{:S(2)}, u32[]{:S(2)}) %collective-permute-start.4) | collective-permute-done | bytes 393248 | tf_op jit(solution)/shard_map/ppermute | solution.py:458
  215.1 1.1 collective-permute-done.5
  216.1 0.9 broadcast_in_dim.25
  217.0 5.6 %all-to-all-start.10 = ((bf16[8,96,384]{2,1,0:T(8,128)(2,1)}), bf16[8,96,384]{2,1,0:T(8,128)(2,1)S(1)}, u32[]{:S(2)}, u32[]{:S(2)}) async-start(bf16[8,96,384]{2,1,0:T(8,128)(2,1)} %broadcast_in_dim.25), calls=%async_computation.10 | async-start | bytes 1179648 | tf_op jit(solution)/shard_map/all_to_all | solution.py:546
  222.9 2.8 %collective-permute-start.7 = (bf16[384,256]{1,0:T(8,128)(2,1)S(1)}, bf16[384,256]{1,0:T(8,128)(2,1)S(1)}, u32[]{:S(2)}, u32[]{:S(2)}) collective-permute-start(bf16[384,256]{1,0:T(8,128)(2,1)S(1)} %dynamic-slice_bitcast_fusion), channel_id=1, source_target_pairs={{0,128},{16,144},{32,160},{48,176},{64,192},{80,208},{96,224},{112... | collective-permute-start | bytes 589832 | tf_op jit(solution)/shard_map/ppermute | solution.py:56
  225.6 0.8 select_reduce_fusion
  226.4 4.5 %collective-permute-done.7 = bf16[384,256]{1,0:T(8,128)(2,1)S(1)} collective-permute-done((bf16[384,256]{1,0:T(8,128)(2,1)S(1)}, bf16[384,256]{1,0:T(8,128)(2,1)S(1)}, u32[]{:S(2)}, u32[]{:S(2)}) %collective-permute-start.7) | collective-permute-done | bytes 196640 | tf_op jit(solution)/shard_map/ppermute | solution.py:56
  231.1 1.7 all-to-all-done.10
  232.9 2.8 %collective-permute-start.6 = (bf16[96,384]{1,0:T(8,128)(2,1)S(1)}, bf16[96,384]{1,0:T(8,128)(2,1)S(1)}, u32[]{:S(2)}, u32[]{:S(2)}) collective-permute-start(bf16[96,384]{1,0:T(8,128)(2,1)S(1)} %reduce_sum.90), channel_id=1, source_target_pairs={{0,128},{16,144},{32,160},{48,176},{64,192},{80,208},{96,224},{112... | collective-permute-start | bytes 221192 | tf_op jit(solution)/shard_map/ppermute | solution.py:56
  235.7 0.9 copy.20
  236.7 1.0 collective-permute-done.6
  237.7 0.7 convert_add_fusion.1
  (66 shorter events, 3.1 us)
Async XLA Ops:
  7.2 8.6 %copy-start = (f32[1536]{0:T(1024)S(1)}, f32[1536]{0:T(1024)}, u32[]{:S(2)}) copy-start(f32[1536]{0:T(1024)} %param.11) | copy-start | bytes 18436
  7.2 120.7 %all-gather.2.cloned.1.call-start = ((), (), s32[]{:S(2)}) async-start(), calls=%async_computation.11 | async-start | bytes 2924544 | tf_op jit(solution)/shard_map/all_gather | solution.py:492
  7.2 6.8 %collective-permute-start = (bf16[512,96]{0,1:T(8,128)(2,1)}, bf16[512,96]{0,1:T(8,128)(2,1)S(1)}, u32[]{:S(2)}, u32[]{:S(2)}) collective-permute-start(bf16[512,96]{0,1:T(8,128)(2,1)} %param.8), channel_id=1, source_target_pairs={{0,128},{16,144},{32,160},{48,176},{64,192},{80,208},{96,224},{112... | collective-permute-start | bytes 294920 | tf_op jit(solution)/shard_map/ppermute | solution.py:56
  11.7 2.3 copy-start.20
  15.1 0.6 copy-start.10
  16.0 0.9 copy-start.7
  16.9 0.9 copy-start.12
  18.9 22.9 %all-to-all-start = ((bf16[16,37,384]{2,1,0:T(8,128)(2,1)}), bf16[16,37,384]{2,1,0:T(8,128)(2,1)S(1)}, u32[]{:S(2)}, u32[]{:S(2)}) async-start(bf16[16,37,384]{2,1,0:T(8,128)(2,1)} %shard_map.111), calls=%async_computation | async-start | bytes 983040 | tf_op jit(solution)/shard_map/all_to_all | solution.py:38
  43.1 20.9 %all-to-all-start.1 = ((bf16[16,32,384]{2,1,0:T(8,128)(2,1)}), bf16[16,32,384]{2,1,0:T(8,128)(2,1)S(1)}, u32[]{:S(2)}, u32[]{:S(2)}) async-start(bf16[16,32,384]{2,1,0:T(8,128)(2,1)} %broadcast_in_dim.21), calls=%async_computation.1 | async-start | bytes 786432 | tf_op jit(solution)/shard_map/all_to_all | solution.py:38
  67.4 58.2 %copy-start.1 = (bf16[512,4096]{1,0:T(8,128)(2,1)}, bf16[512,4096]{1,0:T(8,128)(2,1)S(1)}, u32[]{:S(2)}) copy-start(bf16[512,4096]{1,0:T(8,128)(2,1)S(1)} %get-tuple-element.60.energy_ref) | copy-start | bytes 12582916
  127.2 0.7 copy-start.8
  127.8 1.8 copy-start.6
  129.6 0.9 copy-start.11
  132.1 0.7 copy-start.18
  132.8 5.8 %copy-start.13 = (bf16[96,512]{1,0:T(8,128)(2,1)}, bf16[96,512]{1,0:T(8,128)(2,1)S(1)}, u32[]{:S(2)}) copy-start(bf16[96,512]{1,0:T(8,128)(2,1)S(1)} %get-tuple-element.83) | copy-start | bytes 294916
  132.8 5.8 %copy-start.17 = (f32[512,384]{1,0:T(8,128)}, f32[512,384]{1,0:T(8,128)S(1)}, u32[]{:S(2)}) copy-start(f32[512,384]{1,0:T(8,128)S(1)} %get-tuple-element.95) | copy-start | bytes 2359300
  132.9 5.8 %copy-start.9 = (bf16[16,32,128]{2,1,0:T(8,128)(2,1)S(1)}, bf16[16,32,128]{2,1,0:T(8,128)(2,1)}, u32[]{:S(2)}) copy-start(bf16[16,32,128]{2,1,0:T(8,128)(2,1)} %copy-done.8) | copy-start | bytes 393220
  132.9 17.8 %copy-start.2 = (bf16[512,4096]{1,0:T(8,128)(2,1)S(1)}, bf16[512,4096]{1,0:T(8,128)(2,1)}, u32[]{:S(2)}) copy-start(bf16[512,4096]{1,0:T(8,128)(2,1)} %copy-done.1) | copy-start | bytes 12582916
  138.6 25.7 %copy-start.4 = (bf16[512,4096]{1,0:T(8,128)(2,1)}, bf16[512,4096]{1,0:T(8,128)(2,1)S(1)}, u32[]{:S(2)}) copy-start(bf16[512,4096]{1,0:T(8,128)(2,1)S(1)} %get-tuple-element.76.exponent_ref) | copy-start | bytes 12582916
  154.3 15.3 %copy-start.15 = (f32[32,128]{1,0:T(8,128)}, f32[32,128]{1,0:T(8,128)S(1)}, u32[]{:S(2)}) copy-start(f32[32,128]{1,0:T(8,128)S(1)} %get-tuple-element.75.scale_ref) | copy-start | bytes 49156
  169.6 15.9 %collective-permute-start.2 = (bf16[8,384,256]{2,1,0:T(8,128)(2,1)}, bf16[8,384,256]{2,1,0:T(8,128)(2,1)S(1)}, u32[]{:S(2)}, u32[]{:S(2)}) collective-permute-start(bf16[8,384,256]{2,1,0:T(8,128)(2,1)} %get-tuple-element.89), channel_id=1, source_target_pairs={{0,16},{16,0},{32,48},{48,32},{64,80},{80,64},{96,112},{112,96},{1... | collective-permute-start | bytes 4718600 | tf_op jit(solution)/shard_map/ppermute | solution.py:56
  171.7 15.8 %all-to-all-start.8 = ((bf16[16,32,384]{2,1,0:T(8,128)(2,1)}), bf16[16,32,384]{2,1,0:T(8,128)(2,1)S(1)}, u32[]{:S(2)}, u32[]{:S(2)}) async-start(bf16[16,32,384]{2,1,0:T(8,128)(2,1)} %bitcast.10), calls=%async_computation.8 | async-start | bytes 786432 | tf_op jit(solution)/shard_map/all_to_all | solution.py:38
  175.3 2.2 copy-start.3
  177.5 2.2 copy-start.5
  179.6 0.7 copy-start.16
  183.9 23.2 %copy-start.14 = (bf16[96,512]{1,0:T(8,128)(2,1)S(1)}, bf16[96,512]{1,0:T(8,128)(2,1)}, u32[]{:S(2)}) copy-start(bf16[96,512]{1,0:T(8,128)(2,1)} %copy-done.13) | copy-start | bytes 294916
  183.9 23.2 %copy-start.21 = (f32[96]{0:T(128)S(1)}, f32[96]{0:T(128)}, u32[]{:S(2)}) copy-start(f32[96]{0:T(128)} %copy-done.20) | copy-start | bytes 1156
  186.8 0.7 copy-start.19
  188.4 18.7 %all-to-all-start.9 = ((bf16[16,32,384]{2,1,0:T(8,128)(2,1)}), bf16[16,32,384]{2,1,0:T(8,128)(2,1)S(1)}, u32[]{:S(2)}, u32[]{:S(2)}) async-start(bf16[16,32,384]{2,1,0:T(8,128)(2,1)} %shard_map.123), calls=%async_computation.9 | async-start | bytes 786432 | tf_op jit(solution)/shard_map/all_to_all | solution.py:38
  195.9 29.7 %collective-permute-start.1 = (f32[4,128]{1,0:T(4,128)S(1)}, f32[4,128]{1,0:T(4,128)S(1)}, u32[]{:S(2)}, u32[]{:S(2)}) collective-permute-start(f32[4,128]{1,0:T(4,128)S(1)} %get-tuple-element.82), channel_id=1, source_target_pairs={{0,128},{16,144},{32,160},{48,176},{64,192},{80,208},{96,224},{112... | collective-permute-start | bytes 6152 | tf_op jit(solution)/shard_map/ppermute | solution.py:56
  196.2 12.0 %collective-permute-start.3 = (bf16[2,384,256]{2,1,0:T(8,128)(2,1)}, bf16[2,384,256]{2,1,0:T(8,128)(2,1)S(1)}, u32[]{:S(2)}, u32[]{:S(2)}) collective-permute-start(bf16[2,384,256]{2,1,0:T(8,128)(2,1)} %copy-done.19), channel_id=1, source_target_pairs={{0,32},{16,48},{32,64},{48,80},{64,96},{80,112},{96,0},{112,16},{1... | collective-permute-start | bytes 1179656 | tf_op jit(solution)/shard_map/ppermute | solution.py:458
  196.2 18.9 %collective-permute-start.4 = (bf16[2,384,256]{2,1,0:T(8,128)(2,1)S(1)}, bf16[2,384,256]{2,1,0:T(8,128)(2,1)S(1)}, u32[]{:S(2)}, u32[]{:S(2)}) collective-permute-start(bf16[2,384,256]{2,1,0:T(8,128)(2,1)S(1)} %get-tuple-element.100), channel_id=1, source_target_pairs={{0,64},{16,80},{32,96},{48,112},{64,0},{80,16},{96,32},{112,48},{1... | collective-permute-start | bytes 1179656 | tf_op jit(solution)/shard_map/ppermute | solution.py:458
  198.1 18.0 %collective-permute-start.5 = (bf16[2,384,256]{2,1,0:T(8,128)(2,1)S(1)}, bf16[2,384,256]{2,1,0:T(8,128)(2,1)S(1)}, u32[]{:S(2)}, u32[]{:S(2)}) collective-permute-start(bf16[2,384,256]{2,1,0:T(8,128)(2,1)S(1)} %get-tuple-element.101), channel_id=1, source_target_pairs={{0,96},{16,112},{32,0},{48,16},{64,32},{80,48},{96,64},{112,80},{1... | collective-permute-start | bytes 1179656 | tf_op jit(solution)/shard_map/ppermute | solution.py:458
  217.0 15.8 %all-to-all-start.10 = ((bf16[8,96,384]{2,1,0:T(8,128)(2,1)}), bf16[8,96,384]{2,1,0:T(8,128)(2,1)S(1)}, u32[]{:S(2)}, u32[]{:S(2)}) async-start(bf16[8,96,384]{2,1,0:T(8,128)(2,1)} %broadcast_in_dim.25), calls=%async_computation.10 | async-start | bytes 1179648 | tf_op jit(solution)/shard_map/all_to_all | solution.py:546
  222.9 8.1 %collective-permute-start.7 = (bf16[384,256]{1,0:T(8,128)(2,1)S(1)}, bf16[384,256]{1,0:T(8,128)(2,1)S(1)}, u32[]{:S(2)}, u32[]{:S(2)}) collective-permute-start(bf16[384,256]{1,0:T(8,128)(2,1)S(1)} %dynamic-slice_bitcast_fusion), channel_id=1, source_target_pairs={{0,128},{16,144},{32,160},{48,176},{64,192},{80,208},{96,224},{112... | collective-permute-start | bytes 589832 | tf_op jit(solution)/shard_map/ppermute | solution.py:56
  232.9 4.8 %collective-permute-start.6 = (bf16[96,384]{1,0:T(8,128)(2,1)S(1)}, bf16[96,384]{1,0:T(8,128)(2,1)S(1)}, u32[]{:S(2)}, u32[]{:S(2)}) collective-permute-start(bf16[96,384]{1,0:T(8,128)(2,1)S(1)} %reduce_sum.90), channel_id=1, source_target_pairs={{0,128},{16,144},{32,160},{48,176},{64,192},{80,208},{96,224},{112... | collective-permute-start | bytes 221192 | tf_op jit(solution)/shard_map/ppermute | solution.py:56
Sparse Core Ops, SparseCore 0:
  15.9 77.1 all-gather.1
